TPU v7x, 32 devices: a whole 2x2x4 slice. The times are simulated.
32 devices in a mesh: layer: 8 (over y, x, core), feat: 4 (over z).
Axes of the slice: x: 2, y: 2, z: 4, core: 2. Of those that a mesh axis runs over, the one named last changes fastest.
Arguments:
- tokens_in: bfloat16 [512, 4096], P('feat', 'layer'), may hold values from -6 to 6
- targets: bfloat16 [512, 4096], P('feat', 'layer'), may hold values from -6 to 6
- enc_weight: bfloat16 [2048, 32768], P(None, ('layer', 'feat')), may hold values from -0.125 to 0.125
- enc_bias: float32 [32768], P(('layer', 'feat')), may hold values from -1 to 0.5
- dec_weight: bfloat16 [2, 32768, 2048], P(None, ('layer', 'feat')), may hold values from -0.046875 to 0.046875
Outputs:
- recon_error: float32 [512, 4096], P('feat', 'layer')
- mean_square: float32 [], replicated
- enc_grad: bfloat16 [2048, 32768], P(None, ('layer', 'feat'))
- bias_grad: float32 [32768], P(('layer', 'feat'))
- dec_grad: bfloat16 [2, 32768, 2048], P(None, ('layer', 'feat'))
All inputs are finite; a program needn't handle non-finite values.
Results may differ from a plain program's by a relative error of at most 0.02.
Values may be sent and summed in bfloat16 or wider, within the bound.
No kernel may reach another device: no remote copies, remote signals or barrier semaphores. Data moves between devices by JAX's collectives and lax.ppermute only.
A program may use at most 128 MiB of HBM per device.

v0:
```python
import jax
import jax.numpy as jnp
from jax import lax
from jax.experimental import pallas as pl
from jax.experimental.pallas import tpu as pltpu
from jax.sharding import PartitionSpec as P

loss_scale = 64.0
tile = 256
in_vmem = pl.BlockSpec(memory_space=pltpu.VMEM)
in_smem = pl.BlockSpec(memory_space=pltpu.SMEM)
in_hbm = pl.BlockSpec(memory_space=pltpu.HBM)


def over_feat(value, mask):
    pairs = [(source, source ^ mask) for source in range(lax.axis_size("feat"))]
    return lax.ppermute(value, "feat", pairs)


def over_members(value, bit_level):
    mask = 2**bit_level
    pairs = [(source, source ^ mask) for source in range(lax.axis_size("layer"))]
    return lax.ppermute(value, "layer", pairs)


def to_layer(value, offset, sub_count):
    count = lax.axis_size("layer")
    shift = offset * sub_count
    pairs = [(p, p + shift) for p in range(count - shift)]
    return lax.ppermute(value, "layer", pairs)


def from_layer(value, offset, sub_count):
    count = lax.axis_size("layer")
    pairs = [(p, (p - offset * sub_count) % count) for p in range(count)]
    return lax.ppermute(value, "layer", pairs)


def after(value, *others):
    return lax.optimization_barrier((value, *others))[0]


def all_over_feat(value):
    blocks = [value, over_feat(value, 1)]
    for s in range(2, lax.axis_size("feat")):
        blocks.append(over_feat(after(value, blocks[1]) if s > 2 else value, s))
    return blocks


def params(flops, bytes_accessed, scratch_mib):
    return dict(
        compiler_params=pltpu.CompilerParams(vmem_limit_bytes=scratch_mib * 1024 * 1024),
        cost_estimate=pl.CostEstimate(
            flops=flops, bytes_accessed=bytes_accessed, transcendentals=0
        ),
    )


def dot(left, right, contract):
    return lax.dot_general(
        left, right, ((contract[:1], contract[1:]), ((), ())), preferred_element_type=jnp.float32
    )


def span(index, size):
    return pl.ds(pl.multiple_of(index * size, size), size)


def encode_first(indices, pieces, enc_weight, dec_weight, offset, late, ahead):
    feat_count, rows, cols = pieces[0].shape
    tok = feat_count * rows
    width = enc_weight.shape[1]
    now = len(pieces)

    def kernel(index_ref, *refs):
        piece_refs = refs[:now]
        weight_ref, next_ref, out_ref, late_ref, ahead_ref, held, sems = refs[now:]
        copies = []
        for i in range(now + late):
            copies.append(
                pltpu.make_async_copy(
                    weight_ref.at[span(index_ref[i], cols)],
                    held.at[i] if i < now else late_ref.at[i - now],
                    sems.at[i],
                )
            )
        for i in range(ahead):
            copies.append(
                pltpu.make_async_copy(
                    next_ref.at[offset, :, span(index_ref[now + late + i], cols)],
                    ahead_ref.at[i],
                    sems.at[now + late + i],
                )
            )
        for copy in copies:
            copy.start()
        for copy in copies[:now]:
            copy.wait()
        left = jnp.concatenate([ref[...].reshape(tok, cols) for ref in piece_refs], 1)
        for start in range(0, width, tile):
            here = slice(start, start + tile)
            right = jnp.concatenate([held[i, :, here] for i in range(now)], 0)
            out_ref[:, here] = dot(left, right, (1, 0))
        for copy in copies[now:]:
            copy.wait()

    return pl.pallas_call(
        kernel,
        in_specs=[in_smem] + [in_vmem] * now + [in_hbm] * 2,
        out_specs=[in_vmem] * 3,
        out_shape=[
            jax.ShapeDtypeStruct((tok, width), jnp.float32),
            jax.ShapeDtypeStruct((late, cols, width), jnp.bfloat16),
            jax.ShapeDtypeStruct((ahead, width, cols), jnp.bfloat16),
        ],
        scratch_shapes=[
            pltpu.VMEM((now, cols, width), jnp.bfloat16),
            pltpu.SemaphoreType.DMA((now + late + ahead,)),
        ],
        name="encode_first",
        **params(2 * now * tok * cols * width, 2 * (now + late + 2 * ahead) * cols * width, 12),
    )(indices, *pieces, enc_weight, dec_weight)


def encode_next(piece, weights, place, partial, bias):
    feat_count, rows, cols = piece.shape
    tok = feat_count * rows
    width = weights.shape[2]
    extra = [partial] if bias is None else [partial, bias]

    def kernel(piece_ref, weight_ref, partial_ref, *refs):
        left = piece_ref[...].reshape(tok, cols)
        for start in range(0, width, tile):
            here = slice(start, start + tile)
            total = partial_ref[:, here] + dot(left, weight_ref[place, :, here], (1, 0))
            if bias is None:
                refs[0][:, here] = total
            else:
                pre_act = total + refs[0][:, here]
                refs[1][:, here] = jnp.maximum(pre_act, 0.0).astype(jnp.bfloat16)
                refs[2][:, here] = jnp.where(pre_act > 0.0, 1.0, 0.0).astype(jnp.bfloat16)

    if bias is None:
        out_shape = [jax.ShapeDtypeStruct((tok, width), jnp.float32)]
    else:
        out_shape = [jax.ShapeDtypeStruct((tok, width), jnp.bfloat16)] * 2
    return pl.pallas_call(
        kernel,
        in_specs=[in_vmem] * (2 + len(extra)),
        out_specs=[in_vmem] * len(out_shape),
        out_shape=out_shape,
        name="encode_next",
        **params(2 * tok * cols * width, 2 * cols * width, 8),
    )(piece, weights, *extra)


def decode(features, weights, groups, rows, indices=None, dec_weight=None, offset=None):
    tok, width = features.shape
    count, _, cols = weights.shape
    ahead = indices is not None

    def kernel(feat_ref, weight_ref, *refs):
        if ahead:
            index_ref, next_ref = refs[:2]
            out_refs, next_out, sems = refs[2:-2], refs[-2], refs[-1]
            copies = [
                pltpu.make_async_copy(
                    next_ref.at[offset, :, span(index_ref[i], cols)], next_out.at[i], sems.at[i]
                )
                for i in range(count)
            ]
            for copy in copies:
                copy.start()
        else:
            out_refs = refs
        left = feat_ref[...]
        for piece in range(count):
            for start in range(0, cols, tile):
                here = slice(start, start + tile)
                product = dot(left, weight_ref[piece, :, here], (1, 0)).astype(jnp.bfloat16)
                for group, out_ref in zip(groups, out_refs):
                    for place, block in enumerate(group):
                        out_ref[piece, place, :, here] = product[block * rows : (block + 1) * rows]
        if ahead:
            for copy in copies:
                copy.wait()

    out_shape = [
        jax.ShapeDtypeStruct((count, len(group), rows, cols), jnp.bfloat16) for group in groups
    ]
    if ahead:
        out_shape.append(jax.ShapeDtypeStruct((count, width, cols), jnp.bfloat16))
    result = pl.pallas_call(
        kernel,
        in_specs=[in_vmem] * 2 + ([in_smem, in_hbm] if ahead else []),
        out_specs=[in_vmem] * len(out_shape),
        out_shape=out_shape,
        scratch_shapes=[pltpu.SemaphoreType.DMA((count,))] if ahead else [],
        name="decode",
        **params(2 * count * tok * cols * width, 2 * count * cols * width, 8),
    )(features, weights, *([indices, dec_weight] if ahead else []))
    return result[: len(groups)], (result[-1] if ahead else None)


def turned(value):
    count, tok, width = value.shape

    def kernel(in_ref, out_ref):
        for piece in range(count):
            for start in range(0, width, tile):
                out_ref[piece, start : start + tile, :] = in_ref[
                    piece, :, start : start + tile
                ].T

    return pl.pallas_call(
        kernel,
        in_specs=[in_vmem],
        out_specs=in_vmem,
        out_shape=jax.ShapeDtypeStruct((count, width, tok), value.dtype),
        name="turned",
        **params(0, 4 * count * tok * width, 12),
    )(value)


def tree_sum(values):
    while len(values) > 1:
        values = [values[i] + values[i + 1] for i in range(0, len(values), 2)]
    return values[0]


def backward_piece(info, offset, grads, turned_features, dec_weight, feature_grad, dec_grad):
    layers, width, depth = dec_weight.shape
    tok = turned_features.shape[1]
    cols = grads[0].shape[2]
    first = feature_grad is None
    extra = [] if first else [feature_grad, dec_grad]

    def kernel(info_ref, *refs):
        grad_refs = refs[: len(grads)]
        feat_ref, weight_ref = refs[len(grads) : len(grads) + 2]
        out_ref, dec_ref, square_ref, held, weights, sems = refs[-6:]
        columns = span(info_ref[0], cols)
        fetch = pltpu.make_async_copy(
            weight_ref.at[offset, :, columns], weights, sems.at[width // tile]
        )
        fetch.start()
        blocks = [ref[i] for ref in grad_refs for i in range(ref.shape[0])]
        sums = []
        for block in blocks:
            total = jnp.zeros((8, 128), jnp.float32)
            for row in range(0, block.shape[0], 8):
                for col in range(0, cols, 128):
                    part = block[row : row + 8, col : col + 128].astype(jnp.float32)
                    total += part * part
            sums.append(total)
        square_ref[...] = tree_sum(sums)
        grad = jnp.concatenate(blocks, 0)
        if offset > 0:
            grad = jnp.where(info_ref[1] > 0, grad, jnp.zeros_like(grad))
        copies = []
        for place, start in enumerate(range(0, width, tile)):
            here = slice(start, start + tile)
            held[here] = dot(feat_ref[here], grad, (1, 0)).astype(jnp.bfloat16)
            copy = pltpu.make_async_copy(
                held.at[here], dec_ref.at[offset, here, columns], sems.at[place]
            )
            copy.start()
            copies.append(copy)
        fetch.wait()
        for start in range(0, width, tile):
            here = slice(start, start + tile)
            product = dot(grad, weights[here], (1, 1))
            if not first:
                product += refs[len(grads) + 2][:, here]
            out_ref[:, here] = product
        for copy in copies:
            copy.wait()

    return pl.pallas_call(
        kernel,
        in_specs=[in_smem]
        + [in_vmem] * (len(grads) + 1)
        + [in_hbm]
        + ([] if first else [in_vmem, in_hbm]),
        out_specs=[in_vmem, in_hbm, in_vmem],
        out_shape=[
            jax.ShapeDtypeStruct((tok, width), jnp.float32),
            jax.ShapeDtypeStruct((layers, width, depth), jnp.bfloat16),
            jax.ShapeDtypeStruct((8, 128), jnp.float32),
        ],
        scratch_shapes=[
            pltpu.VMEM((width, cols), jnp.bfloat16),
            pltpu.VMEM((width, cols), jnp.bfloat16),
            pltpu.SemaphoreType.DMA((width // tile + 1,)),
        ],
        input_output_aliases={} if first else {len(grads) + 3: 0, len(grads) + 4: 1},
        name="backward_piece",
        **params(tok * cols, tok * cols, 12),
    )(info, *grads, turned_features, dec_weight, *extra)


def encoder_grad(indices, turned_tokens, mask, feature_grad, squares, scale):
    count, cols, tok = turned_tokens[0].shape
    width = mask.shape[1]
    pieces = len(turned_tokens) * count

    def kernel(index_ref, *refs):
        token_refs = refs[: len(turned_tokens)]
        mask_ref, grad_ref = refs[len(turned_tokens) : len(turned_tokens) + 2]
        square_refs = refs[len(turned_tokens) + 2 : -6]
        enc_ref, bias_ref, mean_ref, preact, held, sems = refs[-6:]
        mean_ref[...] = scale * jnp.sum(
            tree_sum([ref[...] for ref in square_refs]), (0, 1), keepdims=True
        )
        for start in range(0, width, tile):
            here = slice(start, start + tile)
            kept = jnp.where(mask_ref[:, here] > 0.0, grad_ref[:, here], 0.0).astype(jnp.bfloat16)
            preact[:, here] = kept
            bias_ref[:, here] = jnp.sum(kept.astype(jnp.float32), 0, keepdims=True)
        copies = []
        for piece in range(pieces):
            held[piece] = dot(
                token_refs[piece // count][piece % count], preact[...], (1, 0)
            ).astype(jnp.bfloat16)
            copy = pltpu.make_async_copy(
                held.at[piece], enc_ref.at[span(index_ref[piece], cols)], sems.at[piece]
            )
            copy.start()
            copies.append(copy)
        for copy in copies:
            copy.wait()

    return pl.pallas_call(
        kernel,
        in_specs=[in_smem] + [in_vmem] * (len(turned_tokens) + 2 + len(squares)),
        out_specs=[in_hbm, in_vmem, in_vmem],
        out_shape=[
            jax.ShapeDtypeStruct((pieces * cols, width), jnp.bfloat16),
            jax.ShapeDtypeStruct((1, width), jnp.float32),
            jax.ShapeDtypeStruct((1, 1), jnp.float32),
        ],
        scratch_shapes=[
            pltpu.VMEM((tok, width), jnp.bfloat16),
            pltpu.VMEM((pieces, cols, width), jnp.bfloat16),
            pltpu.SemaphoreType.DMA((pieces,)),
        ],
        name="encoder_grad",
        **params(
            2 * pieces * tok * cols * width, 2 * pieces * cols * (tok + width) + 6 * tok * width, 16
        ),
    )(indices, *turned_tokens, mask, feature_grad, *squares)


def add_pair(left, right):
    return (left.astype(jnp.float32) + right.astype(jnp.float32)).astype(jnp.bfloat16)


def on_device(tokens_in, targets, enc_weight, enc_bias, dec_weight):
    layers, width, depth = dec_weight.shape
    feat_count = lax.axis_size("feat")
    sub_count = lax.axis_size("layer") // layers
    member = lax.axis_index("layer") % sub_count
    rows, cols = tokens_in.shape
    tok = feat_count * rows
    bit_count = sub_count.bit_length() - 1
    near = member ^ (2 * jnp.arange(sub_count // 2, dtype=jnp.int32))
    far = near ^ 1
    groups = [list(range(feat_count // 2)), list(range(feat_count // 2, feat_count))]

    enc_weight = pltpu.with_memory_space_constraint(enc_weight, pltpu.HBM)
    dec_weight = pltpu.with_memory_space_constraint(dec_weight, pltpu.HBM)

    held = {0: all_over_feat(tokens_in)}
    for bit_level in range(bit_count - 1, 0, -1):
        for rel in list(held):
            held[rel ^ 2**bit_level] = [None] * feat_count
    for s in range(feat_count):
        known = [0]
        for bit_level in range(bit_count - 1, 0, -1):
            for rel in known:
                held[rel ^ 2**bit_level][s] = over_members(held[rel][s], bit_level)
            known += [rel ^ 2**bit_level for rel in known]
    order = [rel for pair in sorted(held) for rel in (pair, pair ^ 1)]
    early = [held[rel][s] for rel in order[2::2] for s in range(feat_count - 1)]
    tokens = {0: after(jnp.stack(held[0], 0), *early)}
    tokens[1] = over_members(tokens[0], 0)
    partial, late_weights, weights = encode_first(
        jnp.concatenate([jnp.stack([member ^ rel for rel in order]), far]),
        [tokens[0], tokens[1]],
        enc_weight,
        dec_weight,
        layers - 1,
        len(order) - 2,
        len(order) // 2,
    )
    for rel in order[2::2]:
        tokens[rel] = jnp.stack([after(block, partial) for block in held[rel]], 0)
        tokens[rel ^ 1] = over_members(tokens[rel], 0)
    for place, rel in enumerate(order[2:-1]):
        partial = encode_next(tokens[rel], late_weights, place, partial, None)[0]
    features, mask = encode_next(
        tokens[order[-1]], late_weights, len(order) - 3, partial, enc_bias[None]
    )

    current, source = {}, features
    for k in reversed(range(layers)):
        sent, weights = decode(source, weights, groups, rows, near, dec_weight, k)
        if k > 0:
            kept, weights = decode(source, weights, groups, rows, far, dec_weight, k - 1)
        else:
            kept, weights = decode(source, weights, groups, rows)
        for place in reversed(range(len(groups))):
            current[place, k] = add_pair(kept[place], over_members(sent[place], 0))
        source = after(features, current[len(groups) - 1, k])
    turns = sorted(current, reverse=True)
    joined = {}
    for bit_level in range(1, bit_count):
        halves = {}
        for turn, value in current.items():
            split = value.reshape((value.shape[0] // 2, 2) + value.shape[1:])
            halves[turn] = (split[:, 0], split[:, 1])
        if bit_level == bit_count - 1:
            for k in range(1, layers):
                kept, sent = halves.pop((0, k))
                sent = to_layer(sent, k, sub_count)
                halves[0, 0] = (halves[0, 0][0], add_pair(halves[0, 0][1], sent))
                joined[0, k] = kept
            turns = [turn for turn in turns if turn in halves]
        received, operands = [], []
        for turn in turns:
            operand = halves[turn][1]
            if len(received) > 1:
                operand = after(operand, received[-2], operands[-1])
            operands.append(operand)
            received.append(over_members(operand, bit_level))
        for place, turn in enumerate(turns):
            arrived = after(received[place], *operands[place + 1 :][:1])
            if bit_level < bit_count - 1:
                current[turn] = add_pair(halves[turn][0], arrived)
            else:
                current[turn] = (halves[turn][0], arrived)
    blocks = [None] * feat_count
    for place in reversed(range(len(groups))):
        total = sum(part.astype(jnp.float32) for part in current[place, 0])
        for k in range(1, layers):
            if (place, k) in joined:
                moved = to_layer(after(joined[place, k], moved), k, sub_count)
            else:
                moved = to_layer(add_pair(*current[place, k]), k, sub_count)
            total = total + moved.astype(jnp.float32)
        for index, block in enumerate(groups[place]):
            blocks[block] = total[0, index]
    rebuilt = blocks[0]
    for s in reversed(range(1, feat_count)):
        rebuilt = rebuilt + over_feat(blocks[s].astype(jnp.bfloat16), s).astype(jnp.float32)
    turned_features = turned(source[None])[0]
    turned_tokens = [
        turned(after(tokens[rel], turned_features).reshape(1, tok, cols)) for rel in order
    ]
    recon_error = rebuilt - after(targets, turned_features, *turned_tokens).astype(jnp.float32)
    scaled = (loss_scale / tok * recon_error).astype(jnp.bfloat16)

    layer = lax.axis_index("layer") // sub_count
    there = [(layer + k < layers).astype(jnp.int32) for k in range(layers)]
    blocks = all_over_feat(scaled)
    stages = [[0]]
    for level in range(bit_count - 1, 0, -1):
        known = [rel for stage in stages for rel in stage]
        stages.append([rel ^ 2**level for rel in known])
    spans = [[s] for s in range(min(2, feat_count))]
    spans += [list(range(2, feat_count))] if feat_count > 2 else []
    groups_of = {(0, k): [None] * len(spans) for k in range(layers)}
    early, last = [], len(spans) - 1
    for place, group in enumerate(spans):
        stacked = jnp.stack([after(blocks[s], *early) for s in group], 0)
        groups_of[0, 0][place] = stacked
        for k in range(1, layers):
            groups_of[0, k][place] = from_layer(stacked, k, sub_count)
        known = [0]
        for level in range(bit_count - 1, 0, -1):
            for rel in known:
                other = rel ^ 2**level
                for k in range(layers):
                    if k == 0 or place < last:
                        part = over_members(groups_of[rel, k][place], level)
                    else:
                        part = from_layer(groups_of[other, 0][place], k, sub_count)
                    groups_of.setdefault((other, k), [None] * len(spans))[place] = part
            known += [rel ^ 2**level for rel in known]
        if place == last - 1:
            early = [part for parts in groups_of.values() for part in parts if part is not None]
            later = early.pop()

    feature_grad, dec_grad, squares = None, None, {}
    for number, stage in enumerate(stages):
        for k in range(layers):
            if k > 0 and number + 1 < len(stages):
                guard = [part for rel in stages[number + 1] for part in groups_of[rel, k - 1]]
                feature_grad = after(feature_grad, *guard)
            for rel in stage:
                parts = groups_of[rel, k]
                if feature_grad is not None:
                    parts = [after(part, feature_grad) for part in parts]
                groups_of[rel ^ 1, k] = [over_members(part, 0) for part in parts]
                for half in (rel, rel ^ 1):
                    if k == 0 and number > 0:
                        coming = groups_of[rel, layers - 1][-(half % 2)]
                        feature_grad = after(feature_grad, coming)
                    elif (half, k) == (1, 0):
                        feature_grad = after(feature_grad, later)
                    feature_grad, dec_grad, squares[k, half] = backward_piece(
                        jnp.stack([member ^ half, there[k]]),
                        k,
                        groups_of[half, k],
                        turned_features,
                        dec_weight,
                        feature_grad,
                        dec_grad,
                    )
    scale = (tok / loss_scale) ** 2 / (layers * tok * depth)
    enc_grad, bias_grad, mean_square = encoder_grad(
        jnp.stack([member ^ rel for rel in order]),
        turned_tokens,
        mask,
        feature_grad,
        [squares[key] for key in sorted(squares)],
        scale,
    )
    return (recon_error, mean_square[0, 0], enc_grad, bias_grad[0], dec_grad)


def solution(mesh):
    placed = (
        P("feat", "layer"),
        P("feat", "layer"),
        P(None, ("layer", "feat")),
        P(("layer", "feat")),
        P(None, ("layer", "feat"), None),
    )
    return jax.shard_map(
        on_device,
        mesh=mesh,
        in_specs=placed,
        out_specs=(
            P("feat", "layer"),
            P(),
            P(None, ("layer", "feat")),
            P(("layer", "feat")),
            P(None, ("layer", "feat"), None),
        ),
        check_vma=False,
    )
```

profile of v0, /device:TPU:0, one launch (start us, length us, event | category | flops | bytes accessed | tf_op | source)
XLA Modules:
  0.0 134.1 jit_solution(8325803120711438989)
XLA Ops:
  0.6 3.1 %collective-permute-start.1 = (bf16[128,512]{1,0:T(8,128)(2,1)}, bf16[128,512]{1,0:T(8,128)(2,1)S(1)}, u32[]{:S(2)}, u32[]{:S(2)}) collective-permute-start(bf16[128,512]{1,0:T(8,128)(2,1)} %param.5), channel_id=1, source_target_pairs={{0,1},{1,0},{2,3},{3,2},{4,5},{5,4},{6,7},{7,6},{8,9},{9,8},{10,11... | collective-permute-start | bytes 393224 | tf_op jit(solution)/shard_map/ppermute | solution.py:17
  3.7 2.6 %collective-permute-start.2 = (bf16[128,512]{1,0:T(8,128)(2,1)}, bf16[128,512]{1,0:T(8,128)(2,1)S(1)}, u32[]{:S(2)}, u32[]{:S(2)}) collective-permute-start(bf16[128,512]{1,0:T(8,128)(2,1)} %param.5), channel_id=1, source_target_pairs={{0,2},{1,3},{2,0},{3,1},{4,6},{5,7},{6,4},{7,5},{8,10},{9,11},{10,... | collective-permute-start | bytes 393224 | tf_op jit(solution)/shard_map/ppermute | solution.py:17
  6.3 2.9 %collective-permute-done.1 = bf16[128,512]{1,0:T(8,128)(2,1)S(1)} collective-permute-done((bf16[128,512]{1,0:T(8,128)(2,1)}, bf16[128,512]{1,0:T(8,128)(2,1)S(1)}, u32[]{:S(2)}, u32[]{:S(2)}) %collective-permute-start.1) | collective-permute-done | bytes 131104 | tf_op jit(solution)/shard_map/ppermute | solution.py:17
  9.2 3.5 %collective-permute-start.3 = (bf16[128,512]{1,0:T(8,128)(2,1)}, bf16[128,512]{1,0:T(8,128)(2,1)S(1)}, u32[]{:S(2)}, u32[]{:S(2)}) collective-permute-start(bf16[128,512]{1,0:T(8,128)(2,1)} %param.5), channel_id=1, source_target_pairs={{0,3},{1,2},{2,1},{3,0},{4,7},{5,6},{6,5},{7,4},{8,11},{9,10},{10,... | collective-permute-start | bytes 393224 | tf_op jit(solution)/shard_map/ppermute | solution.py:17
  12.8 1.5 %collective-permute-start = (bf16[128,512]{1,0:T(8,128)(2,1)}, bf16[128,512]{1,0:T(8,128)(2,1)S(1)}, u32[]{:S(2)}, u32[]{:S(2)}) collective-permute-start(bf16[128,512]{1,0:T(8,128)(2,1)} %param.5), channel_id=1, source_target_pairs={{0,8},{4,12},{8,0},{12,4},{16,24},{20,28},{24,16},{28,20},{1,9},{5... | collective-permute-start | bytes 393224 | tf_op jit(solution)/shard_map/ppermute | solution.py:23
  14.3 0.5 collective-permute-start.4
  14.8 1.5 %collective-permute-start.5 = (bf16[128,512]{1,0:T(8,128)(2,1)S(1)}, bf16[128,512]{1,0:T(8,128)(2,1)S(1)}, u32[]{:S(2)}, u32[]{:S(2)}) collective-permute-start(bf16[128,512]{1,0:T(8,128)(2,1)S(1)} %collective-permute-done.2), channel_id=1, source_target_pairs={{0,8},{4,12},{8,0},{12,4},{16,24},{20,28},{24,16},{28,20},{1,9},{5... | collective-permute-start | bytes 393224 | tf_op jit(solution)/shard_map/ppermute | solution.py:23
  16.3 1.0 pad_maximum_fusion.refs_0_
  17.3 2.1 %collective-permute-done = bf16[128,512]{1,0:T(8,128)(2,1)S(1)} collective-permute-done((bf16[128,512]{1,0:T(8,128)(2,1)}, bf16[128,512]{1,0:T(8,128)(2,1)S(1)}, u32[]{:S(2)}, u32[]{:S(2)}) %collective-permute-start) | collective-permute-done | bytes 131104 | tf_op jit(solution)/shard_map/ppermute | solution.py:23
  19.4 1.9 %collective-permute-done.4 = bf16[128,512]{1,0:T(8,128)(2,1)S(1)} collective-permute-done((bf16[128,512]{1,0:T(8,128)(2,1)S(1)}, bf16[128,512]{1,0:T(8,128)(2,1)S(1)}, u32[]{:S(2)}, u32[]{:S(2)}) %collective-permute-start.4) | collective-permute-done | bytes 131104 | tf_op jit(solution)/shard_map/ppermute | solution.py:23
  21.3 1.4 %collective-permute-done.5 = bf16[128,512]{1,0:T(8,128)(2,1)S(1)} collective-permute-done((bf16[128,512]{1,0:T(8,128)(2,1)S(1)}, bf16[128,512]{1,0:T(8,128)(2,1)S(1)}, u32[]{:S(2)}, u32[]{:S(2)}) %collective-permute-start.5) | collective-permute-done | bytes 131104 | tf_op jit(solution)/shard_map/ppermute | solution.py:23
  22.7 1.5 %collective-permute-start.7 = (bf16[128,512]{1,0:T(8,128)(2,1)S(1)}, bf16[128,512]{1,0:T(8,128)(2,1)S(1)}, u32[]{:S(2)}, u32[]{:S(2)}) collective-permute-start(bf16[128,512]{1,0:T(8,128)(2,1)S(1)} %collective-permute-done.3), channel_id=1, source_target_pairs={{0,8},{4,12},{8,0},{12,4},{16,24},{20,28},{24,16},{28,20},{1,9},{5... | collective-permute-start | bytes 393224 | tf_op jit(solution)/shard_map/ppermute | solution.py:23
  24.6 3.4 %encode_first.1 = (f32[512,1024]{1,0:T(8,128)S(1)}, bf16[2,512,1024]{2,1,0:T(8,128)(2,1)S(1)}, bf16[2,1024,512]{2,1,0:T(8,128)(2,1)S(1)}) custom-call(s32[6]{0:T(128)S(1)} %concatenate.3.index_ref, bf16[4,128,512]{2,1,0:T(8,128)(2,1)S(1)} %pad_maximum_fusion.refs_0_, bf16[4,128,512]{2,1,0:T(8,128)(2,1)S(1)} %collective-permute-done.6.refs_1_, ...), custom_call_target="tpu_custom_call" | custom-call | flops 1073741824 | bytes 8388608 | tf_op jit(solution)/shard_map/encode_first/pallas_call | solution.py:107
  28.0 0.6 collective-permute-done.7
  28.8 0.7 encode_next.2.partial_ref
  29.5 1.2 collective-permute-done.8.piece_ref
  30.7 0.9 encode_next.3
  31.6 1.0 copy-done.21
  32.5 3.0 %decode.4 = (bf16[2,2,128,512]{3,2,1,0:T(8,128)(2,1)S(1)}, bf16[2,2,128,512]{3,2,1,0:T(8,128)(2,1)S(1)}, bf16[2,1024,512]{2,1,0:T(8,128)(2,1)S(1)}) custom-call(bf16[512,1024]{1,0:T(8,128)(2,1)S(1)} %get-tuple-element.107.feat_ref, bf16[2,1024,512]{2,1,0:T(8,128)(2,1)S(1)} %get-tuple-element.90.weight_ref, s32[2]{0:T(128)S(1)} %multiply_xor_fusion.refs_0_, ...), custom_call_target="tpu_custom_call" | custom-call | flops 1073741824 | bytes 2097152 | tf_op jit(solution)/shard_map/decode/pallas_call | solution.py:193
  35.7 0.4 collective-permute-start.11
  36.1 3.0 %decode.5 = (bf16[2,2,128,512]{3,2,1,0:T(8,128)(2,1)S(1)}, bf16[2,2,128,512]{3,2,1,0:T(8,128)(2,1)S(1)}, bf16[2,1024,512]{2,1,0:T(8,128)(2,1)S(1)}) custom-call(bf16[512,1024]{1,0:T(8,128)(2,1)S(1)} %get-tuple-element.107.feat_ref, bf16[2,1024,512]{2,1,0:T(8,128)(2,1)S(1)} %get-tuple-element.91.weight_ref, s32[2]{0:T(128)S(1)} %broadcast_xor_fusion.refs_0_, ...), custom_call_target="tpu_custom_call" | custom-call | flops 1073741824 | bytes 2097152 | tf_op jit(solution)/shard_map/decode/pallas_call | solution.py:193
  39.2 3.0 %decode.6 = (bf16[2,2,128,512]{3,2,1,0:T(8,128)(2,1)S(1)}, bf16[2,2,128,512]{3,2,1,0:T(8,128)(2,1)S(1)}, bf16[2,1024,512]{2,1,0:T(8,128)(2,1)S(1)}) custom-call(bf16[512,1024]{1,0:T(8,128)(2,1)S(1)} %get-tuple-element.107.feat_ref, bf16[2,1024,512]{2,1,0:T(8,128)(2,1)S(1)} %get-tuple-element.95.weight_ref, s32[2]{0:T(128)S(1)} %multiply_xor_fusion.refs_0_, ...), custom_call_target="tpu_custom_call" | custom-call | flops 1073741824 | bytes 2097152 | tf_op jit(solution)/shard_map/decode/pallas_call | solution.py:193
  42.4 0.4 collective-permute-start.14
  43.0 3.4 %collective-permute-start.12 = (bf16[1,2,128,512]{3,2,1,0:T(8,128)(2,1)S(1)}, bf16[1,2,128,512]{3,2,1,0:T(8,128)(2,1)S(1)}, u32[]{:S(2)}, u32[]{:S(2)}) collective-permute-start(bf16[1,2,128,512]{3,2,1,0:T(8,128)(2,1)S(1)} %get-tuple-element.159), channel_id=1, source_target_pairs={{0,16},{4,20},{8,24},{12,28},{1,17},{5,21},{9,25},{13,29},{2,18},{... | collective-permute-start | bytes 786440 | tf_op jit(solution)/shard_map/ppermute | solution.py:30
  46.5 1.6 %collective-permute-start.13 = (bf16[1,2,128,512]{3,2,1,0:T(8,128)(2,1)S(1)}, bf16[1,2,128,512]{3,2,1,0:T(8,128)(2,1)S(1)}, u32[]{:S(2)}, u32[]{:S(2)}) collective-permute-start(bf16[1,2,128,512]{3,2,1,0:T(8,128)(2,1)S(1)} %slice_bitcast_fusion.5), channel_id=1, source_target_pairs={{0,8},{4,12},{8,0},{12,4},{16,24},{20,28},{24,16},{28,20},{1,9},{5... | collective-permute-start | bytes 786440 | tf_op jit(solution)/shard_map/ppermute | solution.py:23
  48.0 1.2 decode.7
  49.5 0.6 collective-permute-start.18
  50.1 5.7 %collective-permute-done.13 = bf16[1,2,128,512]{3,2,1,0:T(8,128)(2,1)S(1)} collective-permute-done((bf16[1,2,128,512]{3,2,1,0:T(8,128)(2,1)S(1)}, bf16[1,2,128,512]{3,2,1,0:T(8,128)(2,1)S(1)}, u32[]{:S(2)}, u32[]{:S(2)}) %collective-permute-start.13) | collective-permute-done | bytes 262176 | tf_op jit(solution)/shard_map/ppermute | solution.py:23
  55.8 1.3 collective-permute-start.16
  57.4 1.5 %collective-permute-start.15 = (bf16[1,2,128,512]{3,2,1,0:T(8,128)(2,1)S(1)}, bf16[1,2,128,512]{3,2,1,0:T(8,128)(2,1)S(1)}, u32[]{:S(2)}, u32[]{:S(2)}) collective-permute-start(bf16[1,2,128,512]{3,2,1,0:T(8,128)(2,1)S(1)} %fusion.5), channel_id=1, source_target_pairs={{0,8},{4,12},{8,0},{12,4},{16,24},{20,28},{24,16},{28,20},{1,9},{5... | collective-permute-start | bytes 786440 | tf_op jit(solution)/shard_map/ppermute | solution.py:23
  58.9 2.4 %collective-permute-done.18 = bf16[1,2,128,512]{3,2,1,0:T(8,128)(2,1)S(1)} collective-permute-done((bf16[1,2,128,512]{3,2,1,0:T(8,128)(2,1)S(1)}, bf16[1,2,128,512]{3,2,1,0:T(8,128)(2,1)S(1)}, u32[]{:S(2)}, u32[]{:S(2)}) %collective-permute-start.18) | collective-permute-done | bytes 262176 | tf_op jit(solution)/shard_map/ppermute | solution.py:23
  61.4 4.5 %collective-permute-start.17 = (bf16[1,2,128,512]{3,2,1,0:T(8,128)(2,1)S(1)}, bf16[1,2,128,512]{3,2,1,0:T(8,128)(2,1)S(1)}, u32[]{:S(2)}, u32[]{:S(2)}) collective-permute-start(bf16[1,2,128,512]{3,2,1,0:T(8,128)(2,1)S(1)} %get-tuple-element.105), channel_id=1, source_target_pairs={{0,16},{4,20},{8,24},{12,28},{1,17},{5,21},{9,25},{13,29},{2,18},{... | collective-permute-start | bytes 786440 | tf_op jit(solution)/shard_map/ppermute | solution.py:30
  66.3 3.2 %collective-permute-done.17 = bf16[1,2,128,512]{3,2,1,0:T(8,128)(2,1)S(1)} collective-permute-done((bf16[1,2,128,512]{3,2,1,0:T(8,128)(2,1)S(1)}, bf16[1,2,128,512]{3,2,1,0:T(8,128)(2,1)S(1)}, u32[]{:S(2)}, u32[]{:S(2)}) %collective-permute-start.17) | collective-permute-done | bytes 262176 | tf_op jit(solution)/shard_map/ppermute | solution.py:30
  69.6 1.0 collective-permute-start.21
  71.8 1.6 %collective-permute-done.19 = bf16[128,512]{1,0:T(8,128)(2,1)S(1)} collective-permute-done((bf16[128,512]{1,0:T(8,128)(2,1)S(1)}, bf16[128,512]{1,0:T(8,128)(2,1)S(1)}, u32[]{:S(2)}, u32[]{:S(2)}) %collective-permute-start.19) | collective-permute-done | bytes 131104 | tf_op jit(solution)/shard_map/ppermute | solution.py:17
  73.4 3.2 %collective-permute-done.20 = bf16[128,512]{1,0:T(8,128)(2,1)S(1)} collective-permute-done((bf16[128,512]{1,0:T(8,128)(2,1)S(1)}, bf16[128,512]{1,0:T(8,128)(2,1)S(1)}, u32[]{:S(2)}, u32[]{:S(2)}) %collective-permute-start.20) | collective-permute-done | bytes 131104 | tf_op jit(solution)/shard_map/ppermute | solution.py:17
  76.7 0.8 multiply_convert_fusion
  77.5 1.0 collective-permute-start.22
  78.5 1.5 %collective-permute-start.24 = (bf16[1,128,512]{2,1,0:T(8,128)(2,1)S(1)}, bf16[1,128,512]{2,1,0:T(8,128)(2,1)S(1)}, u32[]{:S(2)}, u32[]{:S(2)}) collective-permute-start(bf16[1,128,512]{2,1,0:T(8,128)(2,1)S(1)} %bitcast.92), channel_id=1, source_target_pairs={{0,8},{4,12},{8,0},{12,4},{16,24},{20,28},{24,16},{28,20},{1,9},{5... | collective-permute-start | bytes 393224 | tf_op jit(solution)/shard_map/ppermute | solution.py:23
  80.1 1.7 %collective-permute-start.28 = (bf16[128,512]{1,0:T(8,128)(2,1)S(1)}, bf16[128,512]{1,0:T(8,128)(2,1)S(1)}, u32[]{:S(2)}, u32[]{:S(2)}) collective-permute-start(bf16[128,512]{1,0:T(8,128)(2,1)S(1)} %get-tuple-element.115), channel_id=1, source_target_pairs={{0,2},{1,3},{2,0},{3,1},{4,6},{5,7},{6,4},{7,5},{8,10},{9,11},{10,... | collective-permute-start | bytes 393224 | tf_op jit(solution)/shard_map/ppermute | solution.py:17
  81.7 1.6 %collective-permute-done.26 = bf16[128,512]{1,0:T(8,128)(2,1)} collective-permute-done((bf16[128,512]{1,0:T(8,128)(2,1)S(1)}, bf16[128,512]{1,0:T(8,128)(2,1)}, u32[]{:S(2)}, u32[]{:S(2)}) %collective-permute-start.26) | collective-permute-done | bytes 131104 | tf_op jit(solution)/shard_map/ppermute | solution.py:17
  83.3 1.5 %collective-permute-start.29 = (bf16[1,128,512]{2,1,0:T(8,128)(2,1)}, bf16[1,128,512]{2,1,0:T(8,128)(2,1)S(1)}, u32[]{:S(2)}, u32[]{:S(2)}) collective-permute-start(bf16[1,128,512]{2,1,0:T(8,128)(2,1)} %bitcast.38.refs_1_), channel_id=1, source_target_pairs={{0,16},{4,20},{8,24},{12,28},{16,0},{20,4},{24,8},{28,12},{1,17},{... | collective-permute-start | bytes 393224 | tf_op jit(solution)/shard_map/ppermute | solution.py:36
  84.8 0.6 collective-permute-start.30
  85.4 1.5 %collective-permute-start.23 = (bf16[1,128,512]{2,1,0:T(8,128)(2,1)S(1)}, bf16[1,128,512]{2,1,0:T(8,128)(2,1)S(1)}, u32[]{:S(2)}, u32[]{:S(2)}) collective-permute-start(bf16[1,128,512]{2,1,0:T(8,128)(2,1)S(1)} %collective-permute-done.22.refs_0_), channel_id=1, source_target_pairs={{0,8},{4,12},{8,0},{12,4},{16,24},{20,28},{24,16},{28,20},{1,9},{5... | collective-permute-start | bytes 393224 | tf_op jit(solution)/shard_map/ppermute | solution.py:23
  86.9 1.3 collective-permute-start.31
  88.2 1.6 %collective-permute-done.28 = bf16[128,512]{1,0:T(8,128)(2,1)S(1)} collective-permute-done((bf16[128,512]{1,0:T(8,128)(2,1)S(1)}, bf16[128,512]{1,0:T(8,128)(2,1)S(1)}, u32[]{:S(2)}, u32[]{:S(2)}) %collective-permute-start.28) | collective-permute-done | bytes 131104 | tf_op jit(solution)/shard_map/ppermute | solution.py:17
  89.8 1.6 %collective-permute-done.23.refs_0_ = bf16[1,128,512]{2,1,0:T(8,128)(2,1)S(1)} collective-permute-done((bf16[1,128,512]{2,1,0:T(8,128)(2,1)S(1)}, bf16[1,128,512]{2,1,0:T(8,128)(2,1)S(1)}, u32[]{:S(2)}, u32[]{:S(2)}) %collective-permute-start.23) | collective-permute-done | bytes 131104 | tf_op jit(solution)/shard_map/ppermute | solution.py:23
  91.5 2.2 %collective-permute-done.31 = bf16[128,512]{1,0:T(8,128)(2,1)S(1)} collective-permute-done((bf16[128,512]{1,0:T(8,128)(2,1)S(1)}, bf16[128,512]{1,0:T(8,128)(2,1)S(1)}, u32[]{:S(2)}, u32[]{:S(2)}) %collective-permute-start.31) | collective-permute-done | bytes 131104 | tf_op jit(solution)/shard_map/ppermute | solution.py:17
  93.6 0.6 collective-permute-start.33
  94.4 1.5 %collective-permute-start.34 = (bf16[2,128,512]{2,1,0:T(8,128)(2,1)S(1)}, bf16[2,128,512]{2,1,0:T(8,128)(2,1)}, u32[]{:S(2)}, u32[]{:S(2)}) collective-permute-start(bf16[2,128,512]{2,1,0:T(8,128)(2,1)S(1)} %pad_maximum_fusion.2.refs_2_), channel_id=1, source_target_pairs={{0,8},{4,12},{8,0},{12,4},{16,24},{20,28},{24,16},{28,20},{1,9},{5... | collective-permute-start | bytes 786440 | tf_op jit(solution)/shard_map/ppermute | solution.py:23
  95.8 0.5 collective-permute-start.37
  96.4 3.4 %collective-permute-done.33.refs_1_ = bf16[1,128,512]{2,1,0:T(8,128)(2,1)S(1)} collective-permute-done((bf16[1,128,512]{2,1,0:T(8,128)(2,1)S(1)}, bf16[1,128,512]{2,1,0:T(8,128)(2,1)S(1)}, u32[]{:S(2)}, u32[]{:S(2)}) %collective-permute-start.33) | collective-permute-done | bytes 131104 | tf_op jit(solution)/shard_map/ppermute | solution.py:23
  99.8 0.5 copy-done.12
  100.4 2.9 %backward_piece.8 = (f32[512,1024]{1,0:T(8,128)S(1)}, bf16[2,1024,2048]{2,1,0:T(8,128)(2,1)}, f32[8,128]{1,0:T(8,128)S(1)}) custom-call(s32[2]{0:T(128)S(1)} %pad_add_fusion.6.info_ref, bf16[1,128,512]{2,1,0:T(8,128)(2,1)S(1)} %bitcast.94, bf16[1,128,512]{2,1,0:T(8,128)(2,1)} %bitcast.38.refs_1_, bf16[2,128,512]{2,1,0:T(8,128)(2,1)S(1)} %pad_maximum_fusion.2.refs_2_, ...), custom_call_target="tpu_custom_call" | custom-call | flops 262144 | bytes 262144 | tf_op jit(solution)/shard_map/backward_piece/pallas_call | solution.py:279
  103.4 3.1 %backward_piece.9 = (f32[512,1024]{1,0:T(8,128)S(1)}, bf16[2,1024,2048]{2,1,0:T(8,128)(2,1)}, f32[8,128]{1,0:T(8,128)S(1)}) custom-call(s32[2]{0:T(128)S(1)} %pad_add_fusion.3.info_ref, bf16[1,128,512]{2,1,0:T(8,128)(2,1)S(1)} %collective-permute-done.25.refs_0_, ...), custom_call_target="tpu_custom_call", output_to_operand_aliasing={{0}: (6, {}), {1}: (7, {})} | custom-call | flops 262144 | bytes 262144 | tf_op jit(solution)/shard_map/backward_piece/pallas_call | solution.py:279
  106.6 0.5 collective-permute-start.36
  107.6 0.9 copy-done.19
  108.5 3.1 %backward_piece.10 = (f32[512,1024]{1,0:T(8,128)S(1)}, bf16[2,1024,2048]{2,1,0:T(8,128)(2,1)}, f32[8,128]{1,0:T(8,128)S(1)}) custom-call(s32[2]{0:T(128)S(1)} %pad_add_fusion.5.info_ref, bf16[1,128,512]{2,1,0:T(8,128)(2,1)S(1)} %copy-done.17, bf16[1,128,512]{2,1,0:T(8,128)(2,1)S(1)} %copy-done.19, ...), custom_call_target="tpu_custom_call", output_to_operand_aliasing={{0}: (6, {}), {1}: (7, {})} | custom-call | flops 262144 | bytes 262144 | tf_op jit(solution)/shard_map/backward_piece/pallas_call | solution.py:279
  111.6 3.2 %backward_piece.11 = (f32[512,1024]{1,0:T(8,128)S(1)}, bf16[2,1024,2048]{2,1,0:T(8,128)(2,1)}, f32[8,128]{1,0:T(8,128)S(1)}) custom-call(s32[2]{0:T(128)S(1)} %pad_add_fusion.4.info_ref, bf16[1,128,512]{2,1,0:T(8,128)(2,1)S(1)} %collective-permute-done.35.refs_0_, ...), custom_call_target="tpu_custom_call", output_to_operand_aliasing={{0}: (6, {}), {1}: (7, {})} | custom-call | flops 262144 | bytes 262144 | tf_op jit(solution)/shard_map/backward_piece/pallas_call | solution.py:279
  115.8 3.1 %backward_piece.12 = (f32[512,1024]{1,0:T(8,128)S(1)}, bf16[2,1024,2048]{2,1,0:T(8,128)(2,1)}, f32[8,128]{1,0:T(8,128)S(1)}) custom-call(s32[2]{0:T(128)S(1)} %pad_add_fusion.8.info_ref, bf16[1,128,512]{2,1,0:T(8,128)(2,1)S(1)} %copy-done.11, bf16[1,128,512]{2,1,0:T(8,128)(2,1)S(1)} %copy-done.15, ...), custom_call_target="tpu_custom_call", output_to_operand_aliasing={{0}: (6, {}), {1}: (7, {})} | custom-call | flops 262144 | bytes 262144 | tf_op jit(solution)/shard_map/backward_piece/pallas_call | solution.py:279
  118.9 2.7 %backward_piece.13 = (f32[512,1024]{1,0:T(8,128)S(1)}, bf16[2,1024,2048]{2,1,0:T(8,128)(2,1)}, f32[8,128]{1,0:T(8,128)S(1)}) custom-call(s32[2]{0:T(128)S(1)} %pad_add_fusion.1.info_ref, bf16[1,128,512]{2,1,0:T(8,128)(2,1)S(1)} %collective-permute-done.39.refs_0_, ...), custom_call_target="tpu_custom_call", output_to_operand_aliasing={{0}: (6, {}), {1}: (7, {})} | custom-call | flops 262144 | bytes 262144 | tf_op jit(solution)/shard_map/backward_piece/pallas_call | solution.py:279
  122.7 3.2 %backward_piece.14 = (f32[512,1024]{1,0:T(8,128)S(1)}, bf16[2,1024,2048]{2,1,0:T(8,128)(2,1)}, f32[8,128]{1,0:T(8,128)S(1)}) custom-call(s32[2]{0:T(128)S(1)} %pad_add_fusion.7.info_ref, bf16[1,128,512]{2,1,0:T(8,128)(2,1)S(1)} %copy-done.9, bf16[1,128,512]{2,1,0:T(8,128)(2,1)S(1)} %copy-done.13, ...), custom_call_target="tpu_custom_call", output_to_operand_aliasing={{0}: (6, {}), {1}: (7, {})} | custom-call | flops 262144 | bytes 262144 | tf_op jit(solution)/shard_map/backward_piece/pallas_call | solution.py:279
  126.0 3.2 %backward_piece.15 = (f32[512,1024]{1,0:T(8,128)S(1)}, bf16[2,1024,2048]{2,1,0:T(8,128)(2,1)}, f32[8,128]{1,0:T(8,128)S(1)}) custom-call(s32[2]{0:T(128)S(1)} %pad_add_fusion.2.info_ref, bf16[1,128,512]{2,1,0:T(8,128)(2,1)S(1)} %collective-permute-done.43.refs_0_, ...), custom_call_target="tpu_custom_call", output_to_operand_aliasing={{0}: (6, {}), {1}: (7, {})} | custom-call | flops 262144 | bytes 262144 | tf_op jit(solution)/shard_map/backward_piece/pallas_call | solution.py:279
  129.2 4.7 %encoder_grad.1 = (bf16[2048,1024]{1,0:T(8,128)(2,1)}, f32[1,1024]{1,0:T(1,128)}, f32[1,1]{1,0:T(1,128)}) custom-call(s32[4]{0:T(128)S(1)} %pad_add_fusion.index_ref, bf16[1,512,512]{2,1,0:T(8,128)(2,1)S(1)} %copy-done.7, bf16[1,512,512]{2,1,0:T(8,128)(2,1)S(1)} %copy-done.5, bf16[1,512,512]{2,1,0:T(8,128)(2,1)S(1)} %copy-done.3, ...), custom_call_target="tpu_custom_call" | custom-call | flops 2147483648 | bytes 9437184 | tf_op jit(solution)/shard_map/encoder_grad/pallas_call | solution.py:333
  (126 shorter events, 6.4 us)
Async XLA Ops:
  0.6 8.6 %collective-permute-start.1 = (bf16[128,512]{1,0:T(8,128)(2,1)}, bf16[128,512]{1,0:T(8,128)(2,1)S(1)}, u32[]{:S(2)}, u32[]{:S(2)}) collective-permute-start(bf16[128,512]{1,0:T(8,128)(2,1)} %param.5), channel_id=1, source_target_pairs={{0,1},{1,0},{2,3},{3,2},{4,5},{5,4},{6,7},{7,6},{8,9},{9,8},{10,11... | collective-permute-start | bytes 393224 | tf_op jit(solution)/shard_map/ppermute | solution.py:17
  3.7 11.1 %collective-permute-start.2 = (bf16[128,512]{1,0:T(8,128)(2,1)}, bf16[128,512]{1,0:T(8,128)(2,1)S(1)}, u32[]{:S(2)}, u32[]{:S(2)}) collective-permute-start(bf16[128,512]{1,0:T(8,128)(2,1)} %param.5), channel_id=1, source_target_pairs={{0,2},{1,3},{2,0},{3,1},{4,6},{5,7},{6,4},{7,5},{8,10},{9,11},{10,... | collective-permute-start | bytes 393224 | tf_op jit(solution)/shard_map/ppermute | solution.py:17
  9.2 7.1 %collective-permute-start.3 = (bf16[128,512]{1,0:T(8,128)(2,1)}, bf16[128,512]{1,0:T(8,128)(2,1)S(1)}, u32[]{:S(2)}, u32[]{:S(2)}) collective-permute-start(bf16[128,512]{1,0:T(8,128)(2,1)} %param.5), channel_id=1, source_target_pairs={{0,3},{1,2},{2,1},{3,0},{4,7},{5,6},{6,5},{7,4},{8,11},{9,10},{10,... | collective-permute-start | bytes 393224 | tf_op jit(solution)/shard_map/ppermute | solution.py:17
  12.8 6.6 %collective-permute-start = (bf16[128,512]{1,0:T(8,128)(2,1)}, bf16[128,512]{1,0:T(8,128)(2,1)S(1)}, u32[]{:S(2)}, u32[]{:S(2)}) collective-permute-start(bf16[128,512]{1,0:T(8,128)(2,1)} %param.5), channel_id=1, source_target_pairs={{0,8},{4,12},{8,0},{12,4},{16,24},{20,28},{24,16},{28,20},{1,9},{5... | collective-permute-start | bytes 393224 | tf_op jit(solution)/shard_map/ppermute | solution.py:23
  14.3 7.0 %collective-permute-start.4 = (bf16[128,512]{1,0:T(8,128)(2,1)S(1)}, bf16[128,512]{1,0:T(8,128)(2,1)S(1)}, u32[]{:S(2)}, u32[]{:S(2)}) collective-permute-start(bf16[128,512]{1,0:T(8,128)(2,1)S(1)} %collective-permute-done.1), channel_id=1, source_target_pairs={{0,8},{4,12},{8,0},{12,4},{16,24},{20,28},{24,16},{28,20},{1,9},{5... | collective-permute-start | bytes 393224 | tf_op jit(solution)/shard_map/ppermute | solution.py:23
  14.8 7.9 %collective-permute-start.5 = (bf16[128,512]{1,0:T(8,128)(2,1)S(1)}, bf16[128,512]{1,0:T(8,128)(2,1)S(1)}, u32[]{:S(2)}, u32[]{:S(2)}) collective-permute-start(bf16[128,512]{1,0:T(8,128)(2,1)S(1)} %collective-permute-done.2), channel_id=1, source_target_pairs={{0,8},{4,12},{8,0},{12,4},{16,24},{20,28},{24,16},{28,20},{1,9},{5... | collective-permute-start | bytes 393224 | tf_op jit(solution)/shard_map/ppermute | solution.py:23
  22.7 1.9 %collective-permute-start.6 = (bf16[4,128,512]{2,1,0:T(8,128)(2,1)S(1)}, bf16[4,128,512]{2,1,0:T(8,128)(2,1)S(1)}, u32[]{:S(2)}, u32[]{:S(2)}) collective-permute-start(bf16[4,128,512]{2,1,0:T(8,128)(2,1)S(1)} %pad_maximum_fusion.refs_0_), channel_id=1, source_target_pairs={{0,4},{4,0},{8,12},{12,8},{16,20},{20,16},{24,28},{28,24},{1,5},{5... | collective-permute-start | bytes 1572872 | tf_op jit(solution)/shard_map/ppermute | solution.py:23
  22.7 5.9 %collective-permute-start.7 = (bf16[128,512]{1,0:T(8,128)(2,1)S(1)}, bf16[128,512]{1,0:T(8,128)(2,1)S(1)}, u32[]{:S(2)}, u32[]{:S(2)}) collective-permute-start(bf16[128,512]{1,0:T(8,128)(2,1)S(1)} %collective-permute-done.3), channel_id=1, source_target_pairs={{0,8},{4,12},{8,0},{12,4},{16,24},{20,28},{24,16},{28,20},{1,9},{5... | collective-permute-start | bytes 393224 | tf_op jit(solution)/shard_map/ppermute | solution.py:23
  28.7 2.0 %collective-permute-start.8 = (bf16[4,128,512]{2,1,0:T(8,128)(2,1)S(1)}, bf16[4,128,512]{2,1,0:T(8,128)(2,1)S(1)}, u32[]{:S(2)}, u32[]{:S(2)}) collective-permute-start(bf16[4,128,512]{2,1,0:T(8,128)(2,1)S(1)} %pad_maximum_fusion.1.piece_ref), channel_id=1, source_target_pairs={{0,4},{4,0},{8,12},{12,8},{16,20},{20,16},{24,28},{28,24},{1,5},{5... | collective-permute-start | bytes 1572872 | tf_op jit(solution)/shard_map/ppermute | solution.py:23
  35.5 3.6 %collective-permute-start.9 = (bf16[2,2,128,512]{3,2,1,0:T(8,128)(2,1)S(1)}, bf16[2,2,128,512]{3,2,1,0:T(8,128)(2,1)S(1)}, u32[]{:S(2)}, u32[]{:S(2)}) collective-permute-start(bf16[2,2,128,512]{3,2,1,0:T(8,128)(2,1)S(1)} %get-tuple-element.93), channel_id=1, source_target_pairs={{0,4},{4,0},{8,12},{12,8},{16,20},{20,16},{24,28},{28,24},{1,5},{5... | collective-permute-start | bytes 1572872 | tf_op jit(solution)/shard_map/ppermute | solution.py:23
  35.7 7.1 %collective-permute-start.11 = (bf16[2,2,128,512]{3,2,1,0:T(8,128)(2,1)S(1)}, bf16[2,2,128,512]{3,2,1,0:T(8,128)(2,1)S(1)}, u32[]{:S(2)}, u32[]{:S(2)}) collective-permute-start(bf16[2,2,128,512]{3,2,1,0:T(8,128)(2,1)S(1)} %get-tuple-element.100), channel_id=1, source_target_pairs={{0,4},{4,0},{8,12},{12,8},{16,20},{20,16},{24,28},{28,24},{1,5},{5... | collective-permute-start | bytes 1572872 | tf_op jit(solution)/shard_map/ppermute | solution.py:23
  42.2 14.9 %collective-permute-start.10 = (bf16[2,2,128,512]{3,2,1,0:T(8,128)(2,1)S(1)}, bf16[2,2,128,512]{3,2,1,0:T(8,128)(2,1)S(1)}, u32[]{:S(2)}, u32[]{:S(2)}) collective-permute-start(bf16[2,2,128,512]{3,2,1,0:T(8,128)(2,1)S(1)} %get-tuple-element.98), channel_id=1, source_target_pairs={{0,4},{4,0},{8,12},{12,8},{16,20},{20,16},{24,28},{28,24},{1,5},{5... | collective-permute-start | bytes 1572872 | tf_op jit(solution)/shard_map/ppermute | solution.py:23
  42.4 6.9 %collective-permute-start.14 = (bf16[2,2,128,512]{3,2,1,0:T(8,128)(2,1)S(1)}, bf16[2,2,128,512]{3,2,1,0:T(8,128)(2,1)S(1)}, u32[]{:S(2)}, u32[]{:S(2)}) collective-permute-start(bf16[2,2,128,512]{3,2,1,0:T(8,128)(2,1)S(1)} %get-tuple-element.102), channel_id=1, source_target_pairs={{0,4},{4,0},{8,12},{12,8},{16,20},{20,16},{24,28},{28,24},{1,5},{5... | collective-permute-start | bytes 1572872 | tf_op jit(solution)/shard_map/ppermute | solution.py:23
  43.0 14.3 %collective-permute-start.12 = (bf16[1,2,128,512]{3,2,1,0:T(8,128)(2,1)S(1)}, bf16[1,2,128,512]{3,2,1,0:T(8,128)(2,1)S(1)}, u32[]{:S(2)}, u32[]{:S(2)}) collective-permute-start(bf16[1,2,128,512]{3,2,1,0:T(8,128)(2,1)S(1)} %get-tuple-element.159), channel_id=1, source_target_pairs={{0,16},{4,20},{8,24},{12,28},{1,17},{5,21},{9,25},{13,29},{2,18},{... | collective-permute-start | bytes 786440 | tf_op jit(solution)/shard_map/ppermute | solution.py:30
  46.5 9.3 %collective-permute-start.13 = (bf16[1,2,128,512]{3,2,1,0:T(8,128)(2,1)S(1)}, bf16[1,2,128,512]{3,2,1,0:T(8,128)(2,1)S(1)}, u32[]{:S(2)}, u32[]{:S(2)}) collective-permute-start(bf16[1,2,128,512]{3,2,1,0:T(8,128)(2,1)S(1)} %slice_bitcast_fusion.5), channel_id=1, source_target_pairs={{0,8},{4,12},{8,0},{12,4},{16,24},{20,28},{24,16},{28,20},{1,9},{5... | collective-permute-start | bytes 786440 | tf_op jit(solution)/shard_map/ppermute | solution.py:23
  49.5 11.9 %collective-permute-start.18 = (bf16[1,2,128,512]{3,2,1,0:T(8,128)(2,1)S(1)}, bf16[1,2,128,512]{3,2,1,0:T(8,128)(2,1)S(1)}, u32[]{:S(2)}, u32[]{:S(2)}) collective-permute-start(bf16[1,2,128,512]{3,2,1,0:T(8,128)(2,1)S(1)} %slice_bitcast_fusion.4), channel_id=1, source_target_pairs={{0,8},{4,12},{8,0},{12,4},{16,24},{20,28},{24,16},{28,20},{1,9},{5... | collective-permute-start | bytes 786440 | tf_op jit(solution)/shard_map/ppermute | solution.py:23
  55.8 5.5 %collective-permute-start.16 = (bf16[1,2,128,512]{3,2,1,0:T(8,128)(2,1)S(1)}, bf16[1,2,128,512]{3,2,1,0:T(8,128)(2,1)S(1)}, u32[]{:S(2)}, u32[]{:S(2)}) collective-permute-start(bf16[1,2,128,512]{3,2,1,0:T(8,128)(2,1)S(1)} %fusion.4), channel_id=1, source_target_pairs={{0,16},{4,20},{8,24},{12,28},{1,17},{5,21},{9,25},{13,29},{2,18},{... | collective-permute-start | bytes 786440 | tf_op jit(solution)/shard_map/ppermute | solution.py:30
  57.4 9.0 %collective-permute-start.15 = (bf16[1,2,128,512]{3,2,1,0:T(8,128)(2,1)S(1)}, bf16[1,2,128,512]{3,2,1,0:T(8,128)(2,1)S(1)}, u32[]{:S(2)}, u32[]{:S(2)}) collective-permute-start(bf16[1,2,128,512]{3,2,1,0:T(8,128)(2,1)S(1)} %fusion.5), channel_id=1, source_target_pairs={{0,8},{4,12},{8,0},{12,4},{16,24},{20,28},{24,16},{28,20},{1,9},{5... | collective-permute-start | bytes 786440 | tf_op jit(solution)/shard_map/ppermute | solution.py:23
  61.4 8.1 %collective-permute-start.17 = (bf16[1,2,128,512]{3,2,1,0:T(8,128)(2,1)S(1)}, bf16[1,2,128,512]{3,2,1,0:T(8,128)(2,1)S(1)}, u32[]{:S(2)}, u32[]{:S(2)}) collective-permute-start(bf16[1,2,128,512]{3,2,1,0:T(8,128)(2,1)S(1)} %get-tuple-element.105), channel_id=1, source_target_pairs={{0,16},{4,20},{8,24},{12,28},{1,17},{5,21},{9,25},{13,29},{2,18},{... | collective-permute-start | bytes 786440 | tf_op jit(solution)/shard_map/ppermute | solution.py:30
  66.0 7.4 %collective-permute-start.19 = (bf16[128,512]{1,0:T(8,128)(2,1)S(1)}, bf16[128,512]{1,0:T(8,128)(2,1)S(1)}, u32[]{:S(2)}, u32[]{:S(2)}) collective-permute-start(bf16[128,512]{1,0:T(8,128)(2,1)S(1)} %get-tuple-element.161), channel_id=1, source_target_pairs={{0,3},{1,2},{2,1},{3,0},{4,7},{5,6},{6,5},{7,4},{8,11},{9,10},{10,... | collective-permute-start | bytes 393224 | tf_op jit(solution)/shard_map/ppermute | solution.py:17
  66.3 10.3 %collective-permute-start.20 = (bf16[128,512]{1,0:T(8,128)(2,1)S(1)}, bf16[128,512]{1,0:T(8,128)(2,1)S(1)}, u32[]{:S(2)}, u32[]{:S(2)}) collective-permute-start(bf16[128,512]{1,0:T(8,128)(2,1)S(1)} %get-tuple-element.162), channel_id=1, source_target_pairs={{0,2},{1,3},{2,0},{3,1},{4,6},{5,7},{6,4},{7,5},{8,10},{9,11},{10,... | collective-permute-start | bytes 393224 | tf_op jit(solution)/shard_map/ppermute | solution.py:17
  69.6 7.0 %collective-permute-start.21 = (bf16[128,512]{1,0:T(8,128)(2,1)S(1)}, bf16[128,512]{1,0:T(8,128)(2,1)S(1)}, u32[]{:S(2)}, u32[]{:S(2)}) collective-permute-start(bf16[128,512]{1,0:T(8,128)(2,1)S(1)} %fusion.11), channel_id=1, source_target_pairs={{0,1},{1,0},{2,3},{3,2},{4,5},{5,4},{6,7},{7,6},{8,9},{9,8},{10,11... | collective-permute-start | bytes 393224 | tf_op jit(solution)/shard_map/ppermute | solution.py:17
  70.9 5.7 %copy-start.23 = (bf16[128,512]{1,0:T(8,128)(2,1)S(1)}, bf16[128,512]{1,0:T(8,128)(2,1)}, u32[]{:S(2)}) copy-start(bf16[128,512]{1,0:T(8,128)(2,1)} %param.6) | copy-start | bytes 393220
  71.2 6.3 %copy-start = (bf16[1,512,512]{2,1,0:T(8,128)(2,1)}, bf16[1,512,512]{2,1,0:T(8,128)(2,1)S(1)}, u32[]{:S(2)}) copy-start(bf16[1,512,512]{2,1,0:T(8,128)(2,1)S(1)} %turned.9.refs_3_) | copy-start | bytes 1572868
  71.4 28.4 %copy-start.2 = (bf16[1,512,512]{2,1,0:T(8,128)(2,1)}, bf16[1,512,512]{2,1,0:T(8,128)(2,1)S(1)}, u32[]{:S(2)}) copy-start(bf16[1,512,512]{2,1,0:T(8,128)(2,1)S(1)} %turned.8.refs_2_) | copy-start | bytes 1572868
  71.6 5.1 %copy-start.4 = (bf16[1,512,512]{2,1,0:T(8,128)(2,1)}, bf16[1,512,512]{2,1,0:T(8,128)(2,1)S(1)}, u32[]{:S(2)}) copy-start(bf16[1,512,512]{2,1,0:T(8,128)(2,1)S(1)} %turned.7.refs_1_) | copy-start | bytes 1572868
  71.8 28.0 %copy-start.6 = (bf16[1,512,512]{2,1,0:T(8,128)(2,1)}, bf16[1,512,512]{2,1,0:T(8,128)(2,1)S(1)}, u32[]{:S(2)}) copy-start(bf16[1,512,512]{2,1,0:T(8,128)(2,1)S(1)} %turned.6.refs_0_) | copy-start | bytes 1572868
  77.5 5.8 %collective-permute-start.26 = (bf16[128,512]{1,0:T(8,128)(2,1)S(1)}, bf16[128,512]{1,0:T(8,128)(2,1)}, u32[]{:S(2)}, u32[]{:S(2)}) collective-permute-start(bf16[128,512]{1,0:T(8,128)(2,1)S(1)} %get-tuple-element.115), channel_id=1, source_target_pairs={{0,1},{1,0},{2,3},{3,2},{4,5},{5,4},{6,7},{7,6},{8,9},{9,8},{10,11... | collective-permute-start | bytes 393224 | tf_op jit(solution)/shard_map/ppermute | solution.py:17
  77.5 7.9 %collective-permute-start.22 = (bf16[1,128,512]{2,1,0:T(8,128)(2,1)S(1)}, bf16[1,128,512]{2,1,0:T(8,128)(2,1)S(1)}, u32[]{:S(2)}, u32[]{:S(2)}) collective-permute-start(bf16[1,128,512]{2,1,0:T(8,128)(2,1)S(1)} %bitcast.91), channel_id=1, source_target_pairs={{0,16},{4,20},{8,24},{12,28},{16,0},{20,4},{24,8},{28,12},{1,17},{... | collective-permute-start | bytes 393224 | tf_op jit(solution)/shard_map/ppermute | solution.py:36
  78.5 8.3 %collective-permute-start.24 = (bf16[1,128,512]{2,1,0:T(8,128)(2,1)S(1)}, bf16[1,128,512]{2,1,0:T(8,128)(2,1)S(1)}, u32[]{:S(2)}, u32[]{:S(2)}) collective-permute-start(bf16[1,128,512]{2,1,0:T(8,128)(2,1)S(1)} %bitcast.92), channel_id=1, source_target_pairs={{0,8},{4,12},{8,0},{12,4},{16,24},{20,28},{24,16},{28,20},{1,9},{5... | collective-permute-start | bytes 393224 | tf_op jit(solution)/shard_map/ppermute | solution.py:23
  80.1 9.8 %collective-permute-start.28 = (bf16[128,512]{1,0:T(8,128)(2,1)S(1)}, bf16[128,512]{1,0:T(8,128)(2,1)S(1)}, u32[]{:S(2)}, u32[]{:S(2)}) collective-permute-start(bf16[128,512]{1,0:T(8,128)(2,1)S(1)} %get-tuple-element.115), channel_id=1, source_target_pairs={{0,2},{1,3},{2,0},{3,1},{4,6},{5,7},{6,4},{7,5},{8,10},{9,11},{10,... | collective-permute-start | bytes 393224 | tf_op jit(solution)/shard_map/ppermute | solution.py:17
  83.3 8.1 %collective-permute-start.29 = (bf16[1,128,512]{2,1,0:T(8,128)(2,1)}, bf16[1,128,512]{2,1,0:T(8,128)(2,1)S(1)}, u32[]{:S(2)}, u32[]{:S(2)}) collective-permute-start(bf16[1,128,512]{2,1,0:T(8,128)(2,1)} %bitcast.38.refs_1_), channel_id=1, source_target_pairs={{0,16},{4,20},{8,24},{12,28},{16,0},{20,4},{24,8},{28,12},{1,17},{... | collective-permute-start | bytes 393224 | tf_op jit(solution)/shard_map/ppermute | solution.py:36
  84.8 6.6 %collective-permute-start.30 = (bf16[1,128,512]{2,1,0:T(8,128)(2,1)}, bf16[1,128,512]{2,1,0:T(8,128)(2,1)S(1)}, u32[]{:S(2)}, u32[]{:S(2)}) collective-permute-start(bf16[1,128,512]{2,1,0:T(8,128)(2,1)} %bitcast.38.refs_1_), channel_id=1, source_target_pairs={{0,8},{4,12},{8,0},{12,4},{16,24},{20,28},{24,16},{28,20},{1,9},{5... | collective-permute-start | bytes 393224 | tf_op jit(solution)/shard_map/ppermute | solution.py:23
  85.4 14.4 %copy-start.16 = (bf16[1,128,512]{2,1,0:T(8,128)(2,1)}, bf16[1,128,512]{2,1,0:T(8,128)(2,1)S(1)}, u32[]{:S(2)}) copy-start(bf16[1,128,512]{2,1,0:T(8,128)(2,1)S(1)} %collective-permute-done.22.refs_0_) | copy-start | bytes 393220
  85.4 6.0 %collective-permute-start.23 = (bf16[1,128,512]{2,1,0:T(8,128)(2,1)S(1)}, bf16[1,128,512]{2,1,0:T(8,128)(2,1)S(1)}, u32[]{:S(2)}, u32[]{:S(2)}) collective-permute-start(bf16[1,128,512]{2,1,0:T(8,128)(2,1)S(1)} %collective-permute-done.22.refs_0_), channel_id=1, source_target_pairs={{0,8},{4,12},{8,0},{12,4},{16,24},{20,28},{24,16},{28,20},{1,9},{5... | collective-permute-start | bytes 393224 | tf_op jit(solution)/shard_map/ppermute | solution.py:23
  86.9 7.4 %copy-start.10 = (bf16[1,128,512]{2,1,0:T(8,128)(2,1)}, bf16[1,128,512]{2,1,0:T(8,128)(2,1)S(1)}, u32[]{:S(2)}) copy-start(bf16[1,128,512]{2,1,0:T(8,128)(2,1)S(1)} %collective-permute-done.24.refs_0_) | copy-start | bytes 393220
  86.9 6.8 %collective-permute-start.31 = (bf16[128,512]{1,0:T(8,128)(2,1)S(1)}, bf16[128,512]{1,0:T(8,128)(2,1)S(1)}, u32[]{:S(2)}, u32[]{:S(2)}) collective-permute-start(bf16[128,512]{1,0:T(8,128)(2,1)S(1)} %get-tuple-element.115), channel_id=1, source_target_pairs={{0,3},{1,2},{2,1},{3,0},{4,7},{5,6},{6,5},{7,4},{8,11},{9,10},{10,... | collective-permute-start | bytes 393224 | tf_op jit(solution)/shard_map/ppermute | solution.py:17
  91.4 8.4 %copy-start.18 = (bf16[1,128,512]{2,1,0:T(8,128)(2,1)}, bf16[1,128,512]{2,1,0:T(8,128)(2,1)S(1)}, u32[]{:S(2)}) copy-start(bf16[1,128,512]{2,1,0:T(8,128)(2,1)S(1)} %collective-permute-done.29.refs_1_) | copy-start | bytes 393220
  91.4 8.4 %copy-start.14 = (bf16[1,128,512]{2,1,0:T(8,128)(2,1)}, bf16[1,128,512]{2,1,0:T(8,128)(2,1)S(1)}, u32[]{:S(2)}) copy-start(bf16[1,128,512]{2,1,0:T(8,128)(2,1)S(1)} %collective-permute-done.30.refs_1_) | copy-start | bytes 393220
  93.6 6.1 %collective-permute-start.33 = (bf16[1,128,512]{2,1,0:T(8,128)(2,1)S(1)}, bf16[1,128,512]{2,1,0:T(8,128)(2,1)S(1)}, u32[]{:S(2)}, u32[]{:S(2)}) collective-permute-start(bf16[1,128,512]{2,1,0:T(8,128)(2,1)S(1)} %collective-permute-done.29.refs_1_), channel_id=1, source_target_pairs={{0,8},{4,12},{8,0},{12,4},{16,24},{20,28},{24,16},{28,20},{1,9},{5... | collective-permute-start | bytes 393224 | tf_op jit(solution)/shard_map/ppermute | solution.py:23
  94.3 9.1 %collective-permute-start.32 = (bf16[2,128,512]{2,1,0:T(8,128)(2,1)S(1)}, bf16[2,128,512]{2,1,0:T(8,128)(2,1)}, u32[]{:S(2)}, u32[]{:S(2)}) collective-permute-start(bf16[2,128,512]{2,1,0:T(8,128)(2,1)S(1)} %pad_maximum_fusion.2.refs_2_), channel_id=1, source_target_pairs={{0,4},{4,0},{8,12},{12,8},{16,20},{20,16},{24,28},{28,24},{1,5},{5... | collective-permute-start | bytes 786440 | tf_op jit(solution)/shard_map/ppermute | solution.py:23
  94.4 12.2 %collective-permute-start.34 = (bf16[2,128,512]{2,1,0:T(8,128)(2,1)S(1)}, bf16[2,128,512]{2,1,0:T(8,128)(2,1)}, u32[]{:S(2)}, u32[]{:S(2)}) collective-permute-start(bf16[2,128,512]{2,1,0:T(8,128)(2,1)S(1)} %pad_maximum_fusion.2.refs_2_), channel_id=1, source_target_pairs={{0,8},{4,12},{8,0},{12,4},{16,24},{20,28},{24,16},{28,20},{1,9},{5... | collective-permute-start | bytes 786440 | tf_op jit(solution)/shard_map/ppermute | solution.py:23
  95.8 10.7 %collective-permute-start.37 = (bf16[2,128,512]{2,1,0:T(8,128)(2,1)S(1)}, bf16[2,128,512]{2,1,0:T(8,128)(2,1)}, u32[]{:S(2)}, u32[]{:S(2)}) collective-permute-start(bf16[2,128,512]{2,1,0:T(8,128)(2,1)S(1)} %pad_maximum_fusion.2.refs_2_), channel_id=1, source_target_pairs={{0,16},{4,20},{8,24},{12,28},{16,0},{20,4},{24,8},{28,12},{1,17},{... | collective-permute-start | bytes 786440 | tf_op jit(solution)/shard_map/ppermute | solution.py:36
  96.3 7.0 %collective-permute-start.25 = (bf16[1,128,512]{2,1,0:T(8,128)(2,1)S(1)}, bf16[1,128,512]{2,1,0:T(8,128)(2,1)S(1)}, u32[]{:S(2)}, u32[]{:S(2)}) collective-permute-start(bf16[1,128,512]{2,1,0:T(8,128)(2,1)S(1)} %bitcast.93), channel_id=1, source_target_pairs={{0,4},{4,0},{8,12},{12,8},{16,20},{20,16},{24,28},{28,24},{1,5},{5... | collective-permute-start | bytes 393224 | tf_op jit(solution)/shard_map/ppermute | solution.py:23
  99.7 3.7 %collective-permute-start.27 = (bf16[1,128,512]{2,1,0:T(8,128)(2,1)}, bf16[1,128,512]{2,1,0:T(8,128)(2,1)S(1)}, u32[]{:S(2)}, u32[]{:S(2)}) collective-permute-start(bf16[1,128,512]{2,1,0:T(8,128)(2,1)} %bitcast.38.refs_1_), channel_id=1, source_target_pairs={{0,4},{4,0},{8,12},{12,8},{16,20},{20,16},{24,28},{28,24},{1,5},{5... | collective-permute-start | bytes 393224 | tf_op jit(solution)/shard_map/ppermute | solution.py:23
  103.4 3.7 %copy-start.17 = (bf16[1,128,512]{2,1,0:T(8,128)(2,1)S(1)}, bf16[1,128,512]{2,1,0:T(8,128)(2,1)}, u32[]{:S(2)}) copy-start(bf16[1,128,512]{2,1,0:T(8,128)(2,1)} %copy-done.16) | copy-start | bytes 393220
  106.6 5.0 %collective-permute-start.38 = (bf16[2,128,512]{2,1,0:T(8,128)(2,1)}, bf16[2,128,512]{2,1,0:T(8,128)(2,1)S(1)}, u32[]{:S(2)}, u32[]{:S(2)}) collective-permute-start(bf16[2,128,512]{2,1,0:T(8,128)(2,1)} %collective-permute-done.37.refs_2_), channel_id=1, source_target_pairs={{0,4},{4,0},{8,12},{12,8},{16,20},{20,16},{24,28},{28,24},{1,5},{5... | collective-permute-start | bytes 786440 | tf_op jit(solution)/shard_map/ppermute | solution.py:23
  106.6 4.9 %collective-permute-start.36 = (bf16[1,128,512]{2,1,0:T(8,128)(2,1)}, bf16[1,128,512]{2,1,0:T(8,128)(2,1)S(1)}, u32[]{:S(2)}, u32[]{:S(2)}) collective-permute-start(bf16[1,128,512]{2,1,0:T(8,128)(2,1)} %copy-done.18), channel_id=1, source_target_pairs={{0,4},{4,0},{8,12},{12,8},{16,20},{20,16},{24,28},{28,24},{1,5},{5... | collective-permute-start | bytes 393224 | tf_op jit(solution)/shard_map/ppermute | solution.py:23
  107.1 4.4 %collective-permute-start.35 = (bf16[1,128,512]{2,1,0:T(8,128)(2,1)S(1)}, bf16[1,128,512]{2,1,0:T(8,128)(2,1)S(1)}, u32[]{:S(2)}, u32[]{:S(2)}) collective-permute-start(bf16[1,128,512]{2,1,0:T(8,128)(2,1)S(1)} %copy-done.17), channel_id=1, source_target_pairs={{0,4},{4,0},{8,12},{12,8},{16,20},{20,16},{24,28},{28,24},{1,5},{5... | collective-permute-start | bytes 393224 | tf_op jit(solution)/shard_map/ppermute | solution.py:23
  107.4 11.5 %collective-permute-start.42 = (bf16[2,128,512]{2,1,0:T(8,128)(2,1)}, bf16[2,128,512]{2,1,0:T(8,128)(2,1)S(1)}, u32[]{:S(2)}, u32[]{:S(2)}) collective-permute-start(bf16[2,128,512]{2,1,0:T(8,128)(2,1)} %collective-permute-done.34.refs_2_), channel_id=1, source_target_pairs={{0,16},{4,20},{8,24},{12,28},{16,0},{20,4},{24,8},{28,12},{1,17},{... | collective-permute-start | bytes 786440 | tf_op jit(solution)/shard_map/ppermute | solution.py:36
  111.6 3.5 %copy-start.15 = (bf16[1,128,512]{2,1,0:T(8,128)(2,1)S(1)}, bf16[1,128,512]{2,1,0:T(8,128)(2,1)}, u32[]{:S(2)}) copy-start(bf16[1,128,512]{2,1,0:T(8,128)(2,1)} %copy-done.14) | copy-start | bytes 393220
  111.6 3.8 %copy-start.11 = (bf16[1,128,512]{2,1,0:T(8,128)(2,1)S(1)}, bf16[1,128,512]{2,1,0:T(8,128)(2,1)}, u32[]{:S(2)}) copy-start(bf16[1,128,512]{2,1,0:T(8,128)(2,1)} %copy-done.10) | copy-start | bytes 393220
  114.8 4.0 %collective-permute-start.41 = (bf16[2,128,512]{2,1,0:T(8,128)(2,1)}, bf16[2,128,512]{2,1,0:T(8,128)(2,1)S(1)}, u32[]{:S(2)}, u32[]{:S(2)}) collective-permute-start(bf16[2,128,512]{2,1,0:T(8,128)(2,1)} %collective-permute-done.34.refs_2_), channel_id=1, source_target_pairs={{0,4},{4,0},{8,12},{12,8},{16,20},{20,16},{24,28},{28,24},{1,5},{5... | collective-permute-start | bytes 786440 | tf_op jit(solution)/shard_map/ppermute | solution.py:23
  115.1 3.7 %collective-permute-start.40 = (bf16[1,128,512]{2,1,0:T(8,128)(2,1)S(1)}, bf16[1,128,512]{2,1,0:T(8,128)(2,1)S(1)}, u32[]{:S(2)}, u32[]{:S(2)}) collective-permute-start(bf16[1,128,512]{2,1,0:T(8,128)(2,1)S(1)} %copy-done.15), channel_id=1, source_target_pairs={{0,4},{4,0},{8,12},{12,8},{16,20},{20,16},{24,28},{28,24},{1,5},{5... | collective-permute-start | bytes 393224 | tf_op jit(solution)/shard_map/ppermute | solution.py:23
  115.4 3.4 %collective-permute-start.39 = (bf16[1,128,512]{2,1,0:T(8,128)(2,1)S(1)}, bf16[1,128,512]{2,1,0:T(8,128)(2,1)S(1)}, u32[]{:S(2)}, u32[]{:S(2)}) collective-permute-start(bf16[1,128,512]{2,1,0:T(8,128)(2,1)S(1)} %copy-done.11), channel_id=1, source_target_pairs={{0,4},{4,0},{8,12},{12,8},{16,20},{20,16},{24,28},{28,24},{1,5},{5... | collective-permute-start | bytes 393224 | tf_op jit(solution)/shard_map/ppermute | solution.py:23
  118.9 3.4 %copy-start.9 = (bf16[1,128,512]{2,1,0:T(8,128)(2,1)S(1)}, bf16[1,128,512]{2,1,0:T(8,128)(2,1)}, u32[]{:S(2)}) copy-start(bf16[1,128,512]{2,1,0:T(8,128)(2,1)} %copy-done.8) | copy-start | bytes 393220
  121.6 4.3 %collective-permute-start.45 = (bf16[2,128,512]{2,1,0:T(8,128)(2,1)S(1)}, bf16[2,128,512]{2,1,0:T(8,128)(2,1)S(1)}, u32[]{:S(2)}, u32[]{:S(2)}) collective-permute-start(bf16[2,128,512]{2,1,0:T(8,128)(2,1)S(1)} %collective-permute-done.42.refs_2_), channel_id=1, source_target_pairs={{0,4},{4,0},{8,12},{12,8},{16,20},{20,16},{24,28},{28,24},{1,5},{5... | collective-permute-start | bytes 786440 | tf_op jit(solution)/shard_map/ppermute | solution.py:23
  122.1 3.9 %collective-permute-start.44 = (bf16[1,128,512]{2,1,0:T(8,128)(2,1)S(1)}, bf16[1,128,512]{2,1,0:T(8,128)(2,1)S(1)}, u32[]{:S(2)}, u32[]{:S(2)}) collective-permute-start(bf16[1,128,512]{2,1,0:T(8,128)(2,1)S(1)} %copy-done.13), channel_id=1, source_target_pairs={{0,4},{4,0},{8,12},{12,8},{16,20},{20,16},{24,28},{28,24},{1,5},{5... | collective-permute-start | bytes 393224 | tf_op jit(solution)/shard_map/ppermute | solution.py:23
  122.3 3.7 %collective-permute-start.43 = (bf16[1,128,512]{2,1,0:T(8,128)(2,1)S(1)}, bf16[1,128,512]{2,1,0:T(8,128)(2,1)S(1)}, u32[]{:S(2)}, u32[]{:S(2)}) collective-permute-start(bf16[1,128,512]{2,1,0:T(8,128)(2,1)S(1)} %copy-done.9), channel_id=1, source_target_pairs={{0,4},{4,0},{8,12},{12,8},{16,20},{20,16},{24,28},{28,24},{1,5},{5... | collective-permute-start | bytes 393224 | tf_op jit(solution)/shard_map/ppermute | solution.py:23
  126.0 3.2 %copy-start.1 = (bf16[1,512,512]{2,1,0:T(8,128)(2,1)S(1)}, bf16[1,512,512]{2,1,0:T(8,128)(2,1)}, u32[]{:S(2)}) copy-start(bf16[1,512,512]{2,1,0:T(8,128)(2,1)} %copy-done) | copy-start | bytes 1572868
  126.0 3.2 %copy-start.3 = (bf16[1,512,512]{2,1,0:T(8,128)(2,1)S(1)}, bf16[1,512,512]{2,1,0:T(8,128)(2,1)}, u32[]{:S(2)}) copy-start(bf16[1,512,512]{2,1,0:T(8,128)(2,1)} %copy-done.2) | copy-start | bytes 1572868
  126.0 3.2 %copy-start.5 = (bf16[1,512,512]{2,1,0:T(8,128)(2,1)S(1)}, bf16[1,512,512]{2,1,0:T(8,128)(2,1)}, u32[]{:S(2)}) copy-start(bf16[1,512,512]{2,1,0:T(8,128)(2,1)} %copy-done.4) | copy-start | bytes 1572868
  126.0 3.2 %copy-start.7 = (bf16[1,512,512]{2,1,0:T(8,128)(2,1)S(1)}, bf16[1,512,512]{2,1,0:T(8,128)(2,1)}, u32[]{:S(2)}) copy-start(bf16[1,512,512]{2,1,0:T(8,128)(2,1)} %copy-done.6) | copy-start | bytes 1572868
  126.0 3.2 %copy-start.22 = (bf16[512,1024]{1,0:T(8,128)(2,1)S(1)}, bf16[512,1024]{1,0:T(8,128)(2,1)}, u32[]{:S(2)}) copy-start(bf16[512,1024]{1,0:T(8,128)(2,1)} %copy-done.21) | copy-start | bytes 3145732
  (6 other events, 10.4 us)
where the time goes:
time: 135 us; the launch traced here: 134 us
  Pallas kernels  45.4 us (34%)
  starting transfers between devices  44 us (33%)
  waiting for transfers between devices  37 us (27%)
  other arithmetic  3.44 us (3%)
  local copies, waits for them, and re-layouts  2.71 us (2%)
  between operations  1.52 us (1%)
    pallas_call x8, Pallas kernels, backward_piece(): pl.pallas_call(kernel, in_specs=[in_smem] + [in_vmem] * (len(grads) + 1)...  24.4 us
    ppermute x30, waiting for transfers between devices, over_members(): return lax.ppermute(value, 'layer', pairs)  20.6 us
    ppermute x30, starting transfers between devices, over_members(): return lax.ppermute(value, 'layer', pairs)  18 us
    ppermute x9, starting transfers between devices, over_feat(): return lax.ppermute(value, 'feat', pairs)  13.6 us
    ppermute x9, waiting for transfers between devices, over_feat(): return lax.ppermute(value, 'feat', pairs)  13.2 us
    pallas_call x4, Pallas kernels, decode(): pl.pallas_call(kernel, in_specs=[in_vmem] * 2 + ([in_smem, in_hbm] if ahe...  10.2 us
    ppermute x3, starting transfers between devices, to_layer(): return lax.ppermute(value, 'layer', pairs)  9.2 us
    pallas_call x1, Pallas kernels, encoder_grad(): pl.pallas_call(kernel, in_specs=[in_smem] + [in_vmem] * (len(turned_token...  4.67 us
  transfers between devices with their start and end apart: 46, of which 17 were waited for; matrix products, arithmetic and copies ran while one was open for 2% of the time, Pallas kernels for 23%

commit v1 on v0

--- a/solution.py
+++ b/solution.py
@@ -43,7 +43,7 @@
 def all_over_feat(value):
     blocks = [value, over_feat(value, 1)]
     for s in range(2, lax.axis_size("feat")):
-        blocks.append(over_feat(after(value, blocks[1]) if s > 2 else value, s))
+        blocks.append(over_feat(value, s))
     return blocks
 
 
@@ -66,6 +66,18 @@
     return pl.ds(pl.multiple_of(index * size, size), size)
 
 
+def in_parts(source, target, sems, first, count=8):
+    size = target.shape[0] // count
+    return [
+        pltpu.make_async_copy(
+            source.at[pl.ds(part * size, size)],
+            target.at[pl.ds(part * size, size)],
+            sems.at[first + part],
+        )
+        for part in range(count)
+    ]
+
+
 def encode_first(indices, pieces, enc_weight, dec_weight, offset, late, ahead):
     feat_count, rows, cols = pieces[0].shape
     tok = feat_count * rows
@@ -77,31 +89,22 @@
         weight_ref, next_ref, out_ref, late_ref, ahead_ref, held, sems = refs[now:]
         copies = []
         for i in range(now + late):
-            copies.append(
-                pltpu.make_async_copy(
-                    weight_ref.at[span(index_ref[i], cols)],
-                    held.at[i] if i < now else late_ref.at[i - now],
-                    sems.at[i],
-                )
-            )
+            target = held.at[i] if i < now else late_ref.at[i - now]
+            source = weight_ref.at[span(index_ref[i], cols)]
+            copies += in_parts(source, target, sems, 8 * i)
         for i in range(ahead):
-            copies.append(
-                pltpu.make_async_copy(
-                    next_ref.at[offset, :, span(index_ref[now + late + i], cols)],
-                    ahead_ref.at[i],
-                    sems.at[now + late + i],
-                )
-            )
+            source = next_ref.at[offset, :, span(index_ref[now + late + i], cols)]
+            copies += in_parts(source, ahead_ref.at[i], sems, 8 * (now + late + i))
         for copy in copies:
             copy.start()
-        for copy in copies[:now]:
+        for copy in copies[: 8 * now]:
             copy.wait()
         left = jnp.concatenate([ref[...].reshape(tok, cols) for ref in piece_refs], 1)
         for start in range(0, width, tile):
             here = slice(start, start + tile)
             right = jnp.concatenate([held[i, :, here] for i in range(now)], 0)
             out_ref[:, here] = dot(left, right, (1, 0))
-        for copy in copies[now:]:
+        for copy in copies[8 * now :]:
             copy.wait()
 
     return pl.pallas_call(
@@ -115,7 +118,7 @@
         ],
         scratch_shapes=[
             pltpu.VMEM((now, cols, width), jnp.bfloat16),
-            pltpu.SemaphoreType.DMA((now + late + ahead,)),
+            pltpu.SemaphoreType.DMA((8 * (now + late + ahead),)),
         ],
         name="encode_first",
         **params(2 * now * tok * cols * width, 2 * (now + late + 2 * ahead) * cols * width, 12),
@@ -137,17 +140,17 @@
                 refs[0][:, here] = total
             else:
                 pre_act = total + refs[0][:, here]
-                refs[1][:, here] = jnp.maximum(pre_act, 0.0).astype(jnp.bfloat16)
-                refs[2][:, here] = jnp.where(pre_act > 0.0, 1.0, 0.0).astype(jnp.bfloat16)
+                refs[1][0, :, here] = jnp.maximum(pre_act, 0.0).astype(jnp.bfloat16)
+                refs[1][1, :, here] = jnp.where(pre_act > 0.0, 1.0, 0.0).astype(jnp.bfloat16)
 
     if bias is None:
-        out_shape = [jax.ShapeDtypeStruct((tok, width), jnp.float32)]
+        out_shape = jax.ShapeDtypeStruct((tok, width), jnp.float32)
     else:
-        out_shape = [jax.ShapeDtypeStruct((tok, width), jnp.bfloat16)] * 2
+        out_shape = jax.ShapeDtypeStruct((2, tok, width), jnp.bfloat16)
     return pl.pallas_call(
         kernel,
         in_specs=[in_vmem] * (2 + len(extra)),
-        out_specs=[in_vmem] * len(out_shape),
+        out_specs=in_vmem,
         out_shape=out_shape,
         name="encode_next",
         **params(2 * tok * cols * width, 2 * cols * width, 8),
@@ -155,7 +158,7 @@
 
 
 def decode(features, weights, groups, rows, indices=None, dec_weight=None, offset=None):
-    tok, width = features.shape
+    _, tok, width = features.shape
     count, _, cols = weights.shape
     ahead = indices is not None
 
@@ -163,17 +166,15 @@
         if ahead:
             index_ref, next_ref = refs[:2]
             out_refs, next_out, sems = refs[2:-2], refs[-2], refs[-1]
-            copies = [
-                pltpu.make_async_copy(
-                    next_ref.at[offset, :, span(index_ref[i], cols)], next_out.at[i], sems.at[i]
-                )
-                for i in range(count)
-            ]
+            copies = []
+            for i in range(count):
+                source = next_ref.at[offset, :, span(index_ref[i], cols)]
+                copies += in_parts(source, next_out.at[i], sems, 8 * i)
             for copy in copies:
                 copy.start()
         else:
             out_refs = refs
-        left = feat_ref[...]
+        left = feat_ref[0]
         for piece in range(count):
             for start in range(0, cols, tile):
                 here = slice(start, start + tile)
@@ -195,7 +196,7 @@
         in_specs=[in_vmem] * 2 + ([in_smem, in_hbm] if ahead else []),
         out_specs=[in_vmem] * len(out_shape),
         out_shape=out_shape,
-        scratch_shapes=[pltpu.SemaphoreType.DMA((count,))] if ahead else [],
+        scratch_shapes=[pltpu.SemaphoreType.DMA((8 * count,))] if ahead else [],
         name="decode",
         **params(2 * count * tok * cols * width, 2 * count * cols * width, 8),
     )(features, weights, *([indices, dec_weight] if ahead else []))
@@ -218,7 +219,7 @@
         out_specs=in_vmem,
         out_shape=jax.ShapeDtypeStruct((count, width, tok), value.dtype),
         name="turned",
-        **params(0, 4 * count * tok * width, 12),
+        **params(0, 4 * count * tok * width, 4),
     )(value)
 
 
@@ -240,10 +241,18 @@
         feat_ref, weight_ref = refs[len(grads) : len(grads) + 2]
         out_ref, dec_ref, square_ref, held, weights, sems = refs[-6:]
         columns = span(info_ref[0], cols)
-        fetch = pltpu.make_async_copy(
-            weight_ref.at[offset, :, columns], weights, sems.at[width // tile]
-        )
-        fetch.start()
+        starts = range(0, width, tile)
+        fetches = in_parts(weight_ref.at[offset, :, columns], weights, sems, len(starts))
+        for fetch in fetches:
+            fetch.start()
+        copies = [
+            pltpu.make_async_copy(
+                held.at[slice(start, start + tile)],
+                dec_ref.at[offset, slice(start, start + tile), columns],
+                sems.at[place],
+            )
+            for place, start in enumerate(starts)
+        ]
         blocks = [ref[i] for ref in grad_refs for i in range(ref.shape[0])]
         sums = []
         for block in blocks:
@@ -254,25 +263,35 @@
                     total += part * part
             sums.append(total)
         square_ref[...] = tree_sum(sums)
-        grad = jnp.concatenate(blocks, 0)
-        if offset > 0:
-            grad = jnp.where(info_ref[1] > 0, grad, jnp.zeros_like(grad))
-        copies = []
-        for place, start in enumerate(range(0, width, tile)):
-            here = slice(start, start + tile)
-            held[here] = dot(feat_ref[here], grad, (1, 0)).astype(jnp.bfloat16)
-            copy = pltpu.make_async_copy(
-                held.at[here], dec_ref.at[offset, here, columns], sems.at[place]
-            )
-            copy.start()
-            copies.append(copy)
-        fetch.wait()
-        for start in range(0, width, tile):
-            here = slice(start, start + tile)
-            product = dot(grad, weights[here], (1, 1))
-            if not first:
-                product += refs[len(grads) + 2][:, here]
-            out_ref[:, here] = product
+
+        def products():
+            grad = jnp.concatenate(blocks, 0)
+            for copy, start in zip(copies, starts):
+                here = slice(start, start + tile)
+                held[here] = dot(feat_ref[here], grad, (1, 0)).astype(jnp.bfloat16)
+                copy.start()
+            for fetch in fetches:
+                fetch.wait()
+            for start in starts:
+                here = slice(start, start + tile)
+                product = dot(grad, weights[here], (1, 1))
+                if not first:
+                    product += refs[len(grads) + 2][:, here]
+                out_ref[:, here] = product
+
+        def nothing():
+            held[...] = jnp.zeros_like(held)
+            for copy in copies:
+                copy.start()
+            out_ref[...] = refs[len(grads) + 2][...]
+            for fetch in fetches:
+                fetch.wait()
+
+        if offset == 0:
+            products()
+        else:
+            pl.when(info_ref[1] > 0)(products)
+            pl.when(info_ref[1] == 0)(nothing)
         for copy in copies:
             copy.wait()
 
@@ -291,17 +310,17 @@
         scratch_shapes=[
             pltpu.VMEM((width, cols), jnp.bfloat16),
             pltpu.VMEM((width, cols), jnp.bfloat16),
-            pltpu.SemaphoreType.DMA((width // tile + 1,)),
+            pltpu.SemaphoreType.DMA((width // tile + 8,)),
         ],
         input_output_aliases={} if first else {len(grads) + 3: 0, len(grads) + 4: 1},
         name="backward_piece",
-        **params(tok * cols, tok * cols, 12),
+        **params(tok * cols, tok * cols, 6),
     )(info, *grads, turned_features, dec_weight, *extra)
 
 
-def encoder_grad(indices, turned_tokens, mask, feature_grad, squares, scale):
+def encoder_grad(indices, turned_tokens, features, feature_grad, squares, scale):
     count, cols, tok = turned_tokens[0].shape
-    width = mask.shape[1]
+    width = features.shape[2]
     pieces = len(turned_tokens) * count
 
     def kernel(index_ref, *refs):
@@ -314,7 +333,7 @@
         )
         for start in range(0, width, tile):
             here = slice(start, start + tile)
-            kept = jnp.where(mask_ref[:, here] > 0.0, grad_ref[:, here], 0.0).astype(jnp.bfloat16)
+            kept = jnp.where(mask_ref[1, :, here] > 0.0, grad_ref[:, here], 0.0).astype(jnp.bfloat16)
             preact[:, here] = kept
             bias_ref[:, here] = jnp.sum(kept.astype(jnp.float32), 0, keepdims=True)
         copies = []
@@ -346,9 +365,9 @@
         ],
         name="encoder_grad",
         **params(
-            2 * pieces * tok * cols * width, 2 * pieces * cols * (tok + width) + 6 * tok * width, 16
+            2 * pieces * tok * cols * width, 2 * pieces * cols * (tok + width) + 6 * tok * width, 10
         ),
-    )(indices, *turned_tokens, mask, feature_grad, *squares)
+    )(indices, *turned_tokens, features, feature_grad, *squares)
 
 
 def add_pair(left, right):
@@ -365,7 +384,8 @@
     bit_count = sub_count.bit_length() - 1
     near = member ^ (2 * jnp.arange(sub_count // 2, dtype=jnp.int32))
     far = near ^ 1
-    groups = [list(range(feat_count // 2)), list(range(feat_count // 2, feat_count))]
+    groups = [list(range(feat_count // 2))]
+    groups += [[s] for s in range(feat_count // 2, feat_count)]
 
     enc_weight = pltpu.with_memory_space_constraint(enc_weight, pltpu.HBM)
     dec_weight = pltpu.with_memory_space_constraint(dec_weight, pltpu.HBM)
@@ -381,7 +401,7 @@
                 held[rel ^ 2**bit_level][s] = over_members(held[rel][s], bit_level)
             known += [rel ^ 2**bit_level for rel in known]
     order = [rel for pair in sorted(held) for rel in (pair, pair ^ 1)]
-    early = [held[rel][s] for rel in order[2::2] for s in range(feat_count - 1)]
+    early = [held[rel][s] for rel in order[2::2] for s in range(2)]
     tokens = {0: after(jnp.stack(held[0], 0), *early)}
     tokens[1] = over_members(tokens[0], 0)
     partial, late_weights, weights = encode_first(
@@ -397,8 +417,8 @@
         tokens[rel] = jnp.stack([after(block, partial) for block in held[rel]], 0)
         tokens[rel ^ 1] = over_members(tokens[rel], 0)
     for place, rel in enumerate(order[2:-1]):
-        partial = encode_next(tokens[rel], late_weights, place, partial, None)[0]
-    features, mask = encode_next(
+        partial = encode_next(tokens[rel], late_weights, place, partial, None)
+    features = encode_next(
         tokens[order[-1]], late_weights, len(order) - 3, partial, enc_bias[None]
     )
 
@@ -421,11 +441,10 @@
             halves[turn] = (split[:, 0], split[:, 1])
         if bit_level == bit_count - 1:
             for k in range(1, layers):
-                kept, sent = halves.pop((0, k))
-                sent = to_layer(sent, k, sub_count)
+                joined[k], sent = halves.pop((0, k))
+                sent = to_layer(after(sent, halves[len(groups) - 1, 0][1]), k, sub_count)
                 halves[0, 0] = (halves[0, 0][0], add_pair(halves[0, 0][1], sent))
-                joined[0, k] = kept
-            turns = [turn for turn in turns if turn in halves]
+        turns = [turn for turn in turns if turn in halves]
         received, operands = [], []
         for turn in turns:
             operand = halves[turn][1]
@@ -439,21 +458,24 @@
                 current[turn] = add_pair(halves[turn][0], arrived)
             else:
                 current[turn] = (halves[turn][0], arrived)
-    blocks = [None] * feat_count
+    blocks, operands = [None] * feat_count, []
     for place in reversed(range(len(groups))):
         total = sum(part.astype(jnp.float32) for part in current[place, 0])
         for k in range(1, layers):
-            if (place, k) in joined:
-                moved = to_layer(after(joined[place, k], moved), k, sub_count)
+            if place > 0:
+                moved = to_layer(add_pair(*current[place, k]), k, sub_count)
             else:
-                moved = to_layer(add_pair(*current[place, k]), k, sub_count)
+                moved = to_layer(after(joined[k], *operands), k, sub_count)
             total = total + moved.astype(jnp.float32)
-        for index, block in enumerate(groups[place]):
-            blocks[block] = total[0, index]
-    rebuilt = blocks[0]
-    for s in reversed(range(1, feat_count)):
-        rebuilt = rebuilt + over_feat(blocks[s].astype(jnp.bfloat16), s).astype(jnp.float32)
-    turned_features = turned(source[None])[0]
+        for spot, block in enumerate(groups[place]):
+            if block == 0:
+                rebuilt = total[0, spot]
+            else:
+                operands.append(total[0, spot].astype(jnp.bfloat16))
+                blocks[block] = over_feat(operands[-1], block)
+    for block in reversed(blocks[1:]):
+        rebuilt = rebuilt + block.astype(jnp.float32)
+    turned_features = turned(source[:1])[0]
     turned_tokens = [
         turned(after(tokens[rel], turned_features).reshape(1, tok, cols)) for rel in order
     ]
@@ -472,7 +494,7 @@
     groups_of = {(0, k): [None] * len(spans) for k in range(layers)}
     early, last = [], len(spans) - 1
     for place, group in enumerate(spans):
-        stacked = jnp.stack([after(blocks[s], *early) for s in group], 0)
+        stacked = jnp.stack([blocks[s] for s in group], 0)
         groups_of[0, 0][place] = stacked
         for k in range(1, layers):
             groups_of[0, k][place] = from_layer(stacked, k, sub_count)
@@ -489,7 +511,7 @@
             known += [rel ^ 2**level for rel in known]
         if place == last - 1:
             early = [part for parts in groups_of.values() for part in parts if part is not None]
-            later = early.pop()
+            early.pop()
 
     feature_grad, dec_grad, squares = None, None, {}
     for number, stage in enumerate(stages):
@@ -502,12 +524,12 @@
                 if feature_grad is not None:
                     parts = [after(part, feature_grad) for part in parts]
                 groups_of[rel ^ 1, k] = [over_members(part, 0) for part in parts]
+                if feature_grad is None:
+                    groups_of[rel, k][0] = after(parts[0], *early)
                 for half in (rel, rel ^ 1):
                     if k == 0 and number > 0:
                         coming = groups_of[rel, layers - 1][-(half % 2)]
                         feature_grad = after(feature_grad, coming)
-                    elif (half, k) == (1, 0):
-                        feature_grad = after(feature_grad, later)
                     feature_grad, dec_grad, squares[k, half] = backward_piece(
                         jnp.stack([member ^ half, there[k]]),
                         k,
@@ -521,7 +543,7 @@
     enc_grad, bias_grad, mean_square = encoder_grad(
         jnp.stack([member ^ rel for rel in order]),
         turned_tokens,
-        mask,
+        features,
         feature_grad,
         [squares[key] for key in sorted(squares)],
         scale,

time: 135 us -> 136 us (level)
  waiting for transfers between devices: 37 us -> 21.6 us
  starting transfers between devices: 44 us -> 57.4 us
  Pallas kernels: 45.4 us -> 48.1 us
    ppermute x30 -> x34, waiting for transfers between devices: 20.6 us -> 6.04 us  [over_members(): return lax.ppermute(value, 'layer', pairs)]
    ppermute x3 -> x4, starting transfers between devices: 9.2 us -> 15.2 us  [to_layer(): return lax.ppermute(value, 'layer', pairs)]
    ppermute x30 -> x34, starting transfers between devices: 18 us -> 21.7 us  [over_members(): return lax.ppermute(value, 'layer', pairs)]
    ppermute x3 -> x4, waiting for transfers between devices: 3.17 us -> 0.91 us  [to_layer(): return lax.ppermute(value, 'layer', pairs)]
    pallas_call x8, Pallas kernels: 24.4 us -> 26.4 us  [backward_piece(): pl.pallas_call(kernel, in_specs=[in_smem] + [in_vmem] * (len(grads) + 1)...]
    ppermute x9, starting transfers between devices: 13.6 us -> 15.4 us  [over_feat(): return lax.ppermute(value, 'feat', pairs)]
    ppermute x4, starting transfers between devices: 3.29 us -> 4.98 us  [from_layer(): return lax.ppermute(value, 'layer', pairs)]
    ppermute x9, waiting for transfers between devices: 13.2 us -> 14.6 us  [over_feat(): return lax.ppermute(value, 'feat', pairs)]
  transfers between devices with their start and end apart: 46 -> 51, of which waited for: 17 -> 12; matrix products, arithmetic and copies ran while one was open for 2% -> 2% of each run, Pallas kernels for 23% -> 27%
where the time goes in v1:
time: 136 us; the launch traced here: 135 us
  starting transfers between devices  57.4 us (42%)
  Pallas kernels  48.1 us (35%)
  waiting for transfers between devices  21.6 us (16%)
  other arithmetic  3.42 us (3%)
  local copies, waits for them, and re-layouts  2.87 us (2%)
  between operations  1.64 us (1%)
    pallas_call x8, Pallas kernels, backward_piece(): pl.pallas_call(kernel, in_specs=[in_smem] + [in_vmem] * (len(grads) + 1)...  26.4 us
    ppermute x34, starting transfers between devices, over_members(): return lax.ppermute(value, 'layer', pairs)  21.7 us
    ppermute x9, starting transfers between devices, over_feat(): return lax.ppermute(value, 'feat', pairs)  15.4 us
    ppermute x4, starting transfers between devices, to_layer(): return lax.ppermute(value, 'layer', pairs)  15.2 us
    ppermute x9, waiting for transfers between devices, over_feat(): return lax.ppermute(value, 'feat', pairs)  14.6 us
    pallas_call x4, Pallas kernels, decode(): pl.pallas_call(kernel, in_specs=[in_vmem] * 2 + ([in_smem, in_hbm] if ahe...  10.6 us
    ppermute x34, waiting for transfers between devices, over_members(): return lax.ppermute(value, 'layer', pairs)  6.04 us
    ppermute x4, starting transfers between devices, from_layer(): return lax.ppermute(value, 'layer', pairs)  4.98 us
  transfers between devices with their start and end apart: 51, of which 12 were waited for; matrix products, arithmetic and copies ran while one was open for 2% of the time, Pallas kernels for 27%

profile of v1, /device:TPU:0, one launch (start us, length us, event | category | flops | bytes accessed | tf_op | source)
XLA Modules:
  0.0 135.0 jit_solution(1678064407382081043)
XLA Ops:
  0.6 3.1 %collective-permute-start.1 = (bf16[128,512]{1,0:T(8,128)(2,1)}, bf16[128,512]{1,0:T(8,128)(2,1)S(1)}, u32[]{:S(2)}, u32[]{:S(2)}) collective-permute-start(bf16[128,512]{1,0:T(8,128)(2,1)} %param.5), channel_id=1, source_target_pairs={{0,1},{1,0},{2,3},{3,2},{4,5},{5,4},{6,7},{7,6},{8,9},{9,8},{10,11... | collective-permute-start | bytes 393224 | tf_op jit(solution)/shard_map/ppermute | solution.py:17
  3.7 2.6 %collective-permute-start.2 = (bf16[128,512]{1,0:T(8,128)(2,1)}, bf16[128,512]{1,0:T(8,128)(2,1)S(1)}, u32[]{:S(2)}, u32[]{:S(2)}) collective-permute-start(bf16[128,512]{1,0:T(8,128)(2,1)} %param.5), channel_id=1, source_target_pairs={{0,2},{1,3},{2,0},{3,1},{4,6},{5,7},{6,4},{7,5},{8,10},{9,11},{10,... | collective-permute-start | bytes 393224 | tf_op jit(solution)/shard_map/ppermute | solution.py:17
  6.3 1.7 %collective-permute-start = (bf16[128,512]{1,0:T(8,128)(2,1)}, bf16[128,512]{1,0:T(8,128)(2,1)S(1)}, u32[]{:S(2)}, u32[]{:S(2)}) collective-permute-start(bf16[128,512]{1,0:T(8,128)(2,1)} %param.5), channel_id=1, source_target_pairs={{0,8},{4,12},{8,0},{12,4},{16,24},{20,28},{24,16},{28,20},{1,9},{5... | collective-permute-start | bytes 393224 | tf_op jit(solution)/shard_map/ppermute | solution.py:23
  8.0 0.9 collective-permute-done.1
  9.0 1.7 %collective-permute-start.4 = (bf16[128,512]{1,0:T(8,128)(2,1)S(1)}, bf16[128,512]{1,0:T(8,128)(2,1)S(1)}, u32[]{:S(2)}, u32[]{:S(2)}) collective-permute-start(bf16[128,512]{1,0:T(8,128)(2,1)S(1)} %collective-permute-done.1), channel_id=1, source_target_pairs={{0,8},{4,12},{8,0},{12,4},{16,24},{20,28},{24,16},{28,20},{1,9},{5... | collective-permute-start | bytes 393224 | tf_op jit(solution)/shard_map/ppermute | solution.py:23
  10.7 6.2 %collective-permute-done.2 = bf16[128,512]{1,0:T(8,128)(2,1)S(1)} collective-permute-done((bf16[128,512]{1,0:T(8,128)(2,1)}, bf16[128,512]{1,0:T(8,128)(2,1)S(1)}, u32[]{:S(2)}, u32[]{:S(2)}) %collective-permute-start.2) | collective-permute-done | bytes 131104 | tf_op jit(solution)/shard_map/ppermute | solution.py:17
  16.9 1.0 pad_maximum_fusion.refs_0_
  18.0 1.6 %collective-permute-start.6 = (bf16[128,512]{1,0:T(8,128)(2,1)S(1)}, bf16[128,512]{1,0:T(8,128)(2,1)S(1)}, u32[]{:S(2)}, u32[]{:S(2)}) collective-permute-start(bf16[128,512]{1,0:T(8,128)(2,1)S(1)} %collective-permute-done.2), channel_id=1, source_target_pairs={{0,8},{4,12},{8,0},{12,4},{16,24},{20,28},{24,16},{28,20},{1,9},{5... | collective-permute-start | bytes 393224 | tf_op jit(solution)/shard_map/ppermute | solution.py:23
  19.5 0.5 collective-permute-start.7
  20.2 3.9 %encode_first.1 = (f32[512,1024]{1,0:T(8,128)S(1)}, bf16[2,512,1024]{2,1,0:T(8,128)(2,1)S(1)}, bf16[2,1024,512]{2,1,0:T(8,128)(2,1)S(1)}) custom-call(s32[6]{0:T(128)S(1)} %concatenate.3.index_ref, bf16[4,128,512]{2,1,0:T(8,128)(2,1)S(1)} %pad_maximum_fusion.refs_0_, bf16[4,128,512]{2,1,0:T(8,128)(2,1)S(1)} %collective-permute-done.5.refs_1_, ...), custom_call_target="tpu_custom_call" | custom-call | flops 1073741824 | bytes 8388608 | tf_op jit(solution)/shard_map/encode_first/pallas_call | solution.py:110
  24.3 2.3 %collective-permute-done.7 = bf16[128,512]{1,0:T(8,128)(2,1)S(1)} collective-permute-done((bf16[128,512]{1,0:T(8,128)(2,1)S(1)}, bf16[128,512]{1,0:T(8,128)(2,1)S(1)}, u32[]{:S(2)}, u32[]{:S(2)}) %collective-permute-start.7) | collective-permute-done | bytes 131104 | tf_op jit(solution)/shard_map/ppermute | solution.py:23
  26.8 0.7 encode_next.2.partial_ref
  27.6 1.1 collective-permute-done.8.piece_ref
  28.7 0.9 encode_next.3.feat_ref.refs_4_
  29.6 3.1 %decode.4 = (bf16[2,2,128,512]{3,2,1,0:T(8,128)(2,1)S(1)}, bf16[2,1,128,512]{3,2,1,0:T(8,128)(2,1)S(1)}, bf16[2,1,128,512]{3,2,1,0:T(8,128)(2,1)S(1)}, bf16[2,1024,512]{2,1,0:T(8,128)(2,1)S(1)}) custom-call(bf16[2,512,1024]{2,1,0:T(8,128)(2,1)S(1)} %encode_next.3.feat_ref.refs_4_, bf16[2,1024,512]{2,1,0:T(8,128)(2,1)S(1)} %get-tuple-element.91.weight_ref, ...), custom_call_target="tpu_custom_call" | custom-call | flops 1073741824 | bytes 2097152 | tf_op jit(solution)/shard_map/decode/pallas_call | solution.py:194
  33.5 3.1 %decode.5 = (bf16[2,2,128,512]{3,2,1,0:T(8,128)(2,1)S(1)}, bf16[2,1,128,512]{3,2,1,0:T(8,128)(2,1)S(1)}, bf16[2,1,128,512]{3,2,1,0:T(8,128)(2,1)S(1)}, bf16[2,1024,512]{2,1,0:T(8,128)(2,1)S(1)}) custom-call(bf16[2,512,1024]{2,1,0:T(8,128)(2,1)S(1)} %encode_next.3.feat_ref.refs_4_, bf16[2,1024,512]{2,1,0:T(8,128)(2,1)S(1)} %get-tuple-element.92.weight_ref, ...), custom_call_target="tpu_custom_call" | custom-call | flops 1073741824 | bytes 2097152 | tf_op jit(solution)/shard_map/decode/pallas_call | solution.py:194
  36.7 3.1 %decode.6 = (bf16[2,2,128,512]{3,2,1,0:T(8,128)(2,1)S(1)}, bf16[2,1,128,512]{3,2,1,0:T(8,128)(2,1)S(1)}, bf16[2,1,128,512]{3,2,1,0:T(8,128)(2,1)S(1)}, bf16[2,1024,512]{2,1,0:T(8,128)(2,1)S(1)}) custom-call(bf16[2,512,1024]{2,1,0:T(8,128)(2,1)S(1)} %encode_next.3.feat_ref.refs_4_, bf16[2,1024,512]{2,1,0:T(8,128)(2,1)S(1)} %get-tuple-element.96.weight_ref, ...), custom_call_target="tpu_custom_call" | custom-call | flops 1073741824 | bytes 2097152 | tf_op jit(solution)/shard_map/decode/pallas_call | solution.py:194
  39.8 0.4 collective-permute-start.10
  40.3 0.4 collective-permute-start.17
  40.7 1.2 decode.7
  42.0 1.6 %collective-permute-start.15 = (bf16[1,1,128,512]{3,2,1,0:T(8,128)(2,1)S(1)}, bf16[1,1,128,512]{3,2,1,0:T(8,128)(2,1)S(1)}, u32[]{:S(2)}, u32[]{:S(2)}) collective-permute-start(bf16[1,1,128,512]{3,2,1,0:T(8,128)(2,1)S(1)} %slice_bitcast_fusion.10), channel_id=1, source_target_pairs={{0,8},{4,12},{8,0},{12,4},{16,24},{20,28},{24,16},{28,20},{1,9},{5... | collective-permute-start | bytes 393224 | tf_op jit(solution)/shard_map/ppermute | solution.py:23
  43.9 0.6 collective-permute-start.18
  44.5 3.4 %collective-permute-start.13 = (bf16[1,2,128,512]{3,2,1,0:T(8,128)(2,1)S(1)}, bf16[1,2,128,512]{3,2,1,0:T(8,128)(2,1)S(1)}, u32[]{:S(2)}, u32[]{:S(2)}) collective-permute-start(bf16[1,2,128,512]{3,2,1,0:T(8,128)(2,1)S(1)} %get-tuple-element.104), channel_id=1, source_target_pairs={{0,16},{4,20},{8,24},{12,28},{1,17},{5,21},{9,25},{13,29},{2,18},{... | collective-permute-start | bytes 786440 | tf_op jit(solution)/shard_map/ppermute | solution.py:30
  48.0 0.4 collective-permute-done.15
  48.4 1.5 %collective-permute-start.16 = (bf16[1,1,128,512]{3,2,1,0:T(8,128)(2,1)S(1)}, bf16[1,1,128,512]{3,2,1,0:T(8,128)(2,1)S(1)}, u32[]{:S(2)}, u32[]{:S(2)}) collective-permute-start(bf16[1,1,128,512]{3,2,1,0:T(8,128)(2,1)S(1)} %slice_bitcast_fusion.11), channel_id=1, source_target_pairs={{0,8},{4,12},{8,0},{12,4},{16,24},{20,28},{24,16},{28,20},{1,9},{5... | collective-permute-start | bytes 393224 | tf_op jit(solution)/shard_map/ppermute | solution.py:23
  50.0 3.4 %collective-permute-start.20 = (bf16[1,1,128,512]{3,2,1,0:T(8,128)(2,1)S(1)}, bf16[1,1,128,512]{3,2,1,0:T(8,128)(2,1)S(1)}, u32[]{:S(2)}, u32[]{:S(2)}) collective-permute-start(bf16[1,1,128,512]{3,2,1,0:T(8,128)(2,1)S(1)} %fusion.13), channel_id=1, source_target_pairs={{0,16},{4,20},{8,24},{12,28},{1,17},{5,21},{9,25},{13,29},{2,18},{... | collective-permute-start | bytes 393224 | tf_op jit(solution)/shard_map/ppermute | solution.py:30
  53.5 0.6 collective-permute-start.21
  54.1 3.9 %collective-permute-start.22 = (bf16[1,1,128,512]{3,2,1,0:T(8,128)(2,1)S(1)}, bf16[1,1,128,512]{3,2,1,0:T(8,128)(2,1)S(1)}, u32[]{:S(2)}, u32[]{:S(2)}) collective-permute-start(bf16[1,1,128,512]{3,2,1,0:T(8,128)(2,1)S(1)} %fusion.10), channel_id=1, source_target_pairs={{0,16},{4,20},{8,24},{12,28},{1,17},{5,21},{9,25},{13,29},{2,18},{... | collective-permute-start | bytes 393224 | tf_op jit(solution)/shard_map/ppermute | solution.py:30
  58.3 1.5 %collective-permute-start.19 = (bf16[1,2,128,512]{3,2,1,0:T(8,128)(2,1)S(1)}, bf16[1,2,128,512]{3,2,1,0:T(8,128)(2,1)S(1)}, u32[]{:S(2)}, u32[]{:S(2)}) collective-permute-start(bf16[1,2,128,512]{3,2,1,0:T(8,128)(2,1)S(1)} %fusion.2), channel_id=1, source_target_pairs={{0,8},{4,12},{8,0},{12,4},{16,24},{20,28},{24,16},{28,20},{1,9},{5... | collective-permute-start | bytes 786440 | tf_op jit(solution)/shard_map/ppermute | solution.py:23
  59.8 0.6 collective-permute-done.22
  60.5 4.5 %collective-permute-start.23 = (bf16[1,2,128,512]{3,2,1,0:T(8,128)(2,1)S(1)}, bf16[1,2,128,512]{3,2,1,0:T(8,128)(2,1)S(1)}, u32[]{:S(2)}, u32[]{:S(2)}) collective-permute-start(bf16[1,2,128,512]{3,2,1,0:T(8,128)(2,1)S(1)} %get-tuple-element.116), channel_id=1, source_target_pairs={{0,16},{4,20},{8,24},{12,28},{1,17},{5,21},{9,25},{13,29},{2,18},{... | collective-permute-start | bytes 786440 | tf_op jit(solution)/shard_map/ppermute | solution.py:30
  65.1 2.3 %collective-permute-start.24 = (bf16[128,512]{1,0:T(8,128)(2,1)S(1)}, bf16[128,512]{1,0:T(8,128)(2,1)S(1)}, u32[]{:S(2)}, u32[]{:S(2)}) collective-permute-start(bf16[128,512]{1,0:T(8,128)(2,1)S(1)} %fusion.16), channel_id=1, source_target_pairs={{0,3},{1,2},{2,1},{3,0},{4,7},{5,6},{6,5},{7,4},{8,11},{9,10},{10,... | collective-permute-start | bytes 393224 | tf_op jit(solution)/shard_map/ppermute | solution.py:17
  67.4 1.1 collective-permute-start.25
  68.9 1.9 %collective-permute-start.26 = (bf16[128,512]{1,0:T(8,128)(2,1)S(1)}, bf16[128,512]{1,0:T(8,128)(2,1)S(1)}, u32[]{:S(2)}, u32[]{:S(2)}) collective-permute-start(bf16[128,512]{1,0:T(8,128)(2,1)S(1)} %fusion.18), channel_id=1, source_target_pairs={{0,1},{1,0},{2,3},{3,2},{4,5},{5,4},{6,7},{7,6},{8,9},{9,8},{10,11... | collective-permute-start | bytes 393224 | tf_op jit(solution)/shard_map/ppermute | solution.py:17
  72.4 0.8 copy-done.10
  73.1 3.8 %collective-permute-done.25 = bf16[128,512]{1,0:T(8,128)(2,1)S(1)} collective-permute-done((bf16[128,512]{1,0:T(8,128)(2,1)S(1)}, bf16[128,512]{1,0:T(8,128)(2,1)S(1)}, u32[]{:S(2)}, u32[]{:S(2)}) %collective-permute-start.25) | collective-permute-done | bytes 131104 | tf_op jit(solution)/shard_map/ppermute | solution.py:17
  76.9 0.8 multiply_convert_fusion
  77.7 1.0 collective-permute-start.27
  79.1 2.6 %collective-permute-start.33 = (bf16[128,512]{1,0:T(8,128)(2,1)S(1)}, bf16[128,512]{1,0:T(8,128)(2,1)S(1)}, u32[]{:S(2)}, u32[]{:S(2)}) collective-permute-start(bf16[128,512]{1,0:T(8,128)(2,1)S(1)} %get-tuple-element.163), channel_id=1, source_target_pairs={{0,2},{1,3},{2,0},{3,1},{4,6},{5,7},{6,4},{7,5},{8,10},{9,11},{10,... | collective-permute-start | bytes 393224 | tf_op jit(solution)/shard_map/ppermute | solution.py:17
  81.7 1.5 %collective-permute-start.34 = (bf16[128,512]{1,0:T(8,128)(2,1)S(1)}, bf16[128,512]{1,0:T(8,128)(2,1)S(1)}, u32[]{:S(2)}, u32[]{:S(2)}) collective-permute-start(bf16[128,512]{1,0:T(8,128)(2,1)S(1)} %get-tuple-element.163), channel_id=1, source_target_pairs={{0,3},{1,2},{2,1},{3,0},{4,7},{5,6},{6,5},{7,4},{8,11},{9,10},{10,... | collective-permute-start | bytes 393224 | tf_op jit(solution)/shard_map/ppermute | solution.py:17
  83.1 1.5 %collective-permute-start.29 = (bf16[1,128,512]{2,1,0:T(8,128)(2,1)S(1)}, bf16[1,128,512]{2,1,0:T(8,128)(2,1)S(1)}, u32[]{:S(2)}, u32[]{:S(2)}) collective-permute-start(bf16[1,128,512]{2,1,0:T(8,128)(2,1)S(1)} %bitcast.120), channel_id=1, source_target_pairs={{0,8},{4,12},{8,0},{12,4},{16,24},{20,28},{24,16},{28,20},{1,9},{5... | collective-permute-start | bytes 393224 | tf_op jit(solution)/shard_map/ppermute | solution.py:23
  84.6 0.5 collective-permute-start.28
  85.2 0.7 collective-permute-done.31
  85.8 0.5 collective-permute-start.36
  86.3 3.1 %collective-permute-done.33 = bf16[128,512]{1,0:T(8,128)(2,1)S(1)} collective-permute-done((bf16[128,512]{1,0:T(8,128)(2,1)S(1)}, bf16[128,512]{1,0:T(8,128)(2,1)S(1)}, u32[]{:S(2)}, u32[]{:S(2)}) %collective-permute-start.33) | collective-permute-done | bytes 131104 | tf_op jit(solution)/shard_map/ppermute | solution.py:17
  89.4 1.5 %collective-permute-start.37 = (bf16[1,128,512]{2,1,0:T(8,128)(2,1)}, bf16[1,128,512]{2,1,0:T(8,128)(2,1)S(1)}, u32[]{:S(2)}, u32[]{:S(2)}) collective-permute-start(bf16[1,128,512]{2,1,0:T(8,128)(2,1)} %bitcast.51.refs_1_), channel_id=1, source_target_pairs={{0,8},{4,12},{8,0},{12,4},{16,24},{20,28},{24,16},{28,20},{1,9},{5... | collective-permute-start | bytes 393224 | tf_op jit(solution)/shard_map/ppermute | solution.py:23
  91.0 0.6 collective-permute-start.38
  91.6 1.7 %collective-permute-start.41 = (bf16[2,128,512]{2,1,0:T(8,128)(2,1)S(1)}, bf16[2,128,512]{2,1,0:T(8,128)(2,1)}, u32[]{:S(2)}, u32[]{:S(2)}) collective-permute-start(bf16[2,128,512]{2,1,0:T(8,128)(2,1)S(1)} %pad_maximum_fusion.2.refs_2_), channel_id=1, source_target_pairs={{0,16},{4,20},{8,24},{12,28},{16,0},{20,4},{24,8},{28,12},{1,17},{... | collective-permute-start | bytes 786440 | tf_op jit(solution)/shard_map/ppermute | solution.py:36
  93.3 1.8 %collective-permute-done.37.refs_1_ = bf16[1,128,512]{2,1,0:T(8,128)(2,1)S(1)} collective-permute-done((bf16[1,128,512]{2,1,0:T(8,128)(2,1)}, bf16[1,128,512]{2,1,0:T(8,128)(2,1)S(1)}, u32[]{:S(2)}, u32[]{:S(2)}) %collective-permute-start.37) | collective-permute-done | bytes 131104 | tf_op jit(solution)/shard_map/ppermute | solution.py:23
  95.2 0.6 copy-done.16
  95.8 3.6 %backward_piece.8 = (f32[512,1024]{1,0:T(8,128)S(1)}, bf16[2,1024,2048]{2,1,0:T(8,128)(2,1)}, f32[8,128]{1,0:T(8,128)S(1)}) custom-call(s32[2]{0:T(128)S(1)} %pad_add_fusion.6.info_ref, bf16[1,128,512]{2,1,0:T(8,128)(2,1)S(1)} %bitcast.122, bf16[1,128,512]{2,1,0:T(8,128)(2,1)} %bitcast.51.refs_1_, bf16[2,128,512]{2,1,0:T(8,128)(2,1)S(1)} %pad_maximum_fusion.2.refs_2_, ...), custom_call_target="tpu_custom_call" | custom-call | flops 262144 | bytes 262144 | tf_op jit(solution)/shard_map/backward_piece/pallas_call | solution.py:298
  99.4 3.5 %backward_piece.9 = (f32[512,1024]{1,0:T(8,128)S(1)}, bf16[2,1024,2048]{2,1,0:T(8,128)(2,1)}, f32[8,128]{1,0:T(8,128)S(1)}) custom-call(s32[2]{0:T(128)S(1)} %pad_add_fusion.3.info_ref, bf16[1,128,512]{2,1,0:T(8,128)(2,1)S(1)} %collective-permute-done.30.refs_0_, ...), custom_call_target="tpu_custom_call", output_to_operand_aliasing={{0}: (6, {}), {1}: (7, {})} | custom-call | flops 262144 | bytes 262144 | tf_op jit(solution)/shard_map/backward_piece/pallas_call | solution.py:298
  103.1 0.5 collective-permute-start.40
  103.8 1.8 %collective-permute-start.46 = (bf16[2,128,512]{2,1,0:T(8,128)(2,1)}, bf16[2,128,512]{2,1,0:T(8,128)(2,1)S(1)}, u32[]{:S(2)}, u32[]{:S(2)}) collective-permute-start(bf16[2,128,512]{2,1,0:T(8,128)(2,1)} %collective-permute-done.38.refs_2_), channel_id=1, source_target_pairs={{0,16},{4,20},{8,24},{12,28},{16,0},{20,4},{24,8},{28,12},{1,17},{... | collective-permute-start | bytes 786440 | tf_op jit(solution)/shard_map/ppermute | solution.py:36
  105.6 0.9 copy-done.19
  106.5 3.2 %backward_piece.10 = (f32[512,1024]{1,0:T(8,128)S(1)}, bf16[2,1024,2048]{2,1,0:T(8,128)(2,1)}, f32[8,128]{1,0:T(8,128)S(1)}) custom-call(s32[2]{0:T(128)S(1)} %pad_add_fusion.5.info_ref, bf16[1,128,512]{2,1,0:T(8,128)(2,1)S(1)} %copy-done.19, bf16[1,128,512]{2,1,0:T(8,128)(2,1)S(1)} %copy-done.13, ...), custom_call_target="tpu_custom_call", output_to_operand_aliasing={{0}: (6, {}), {1}: (7, {})} | custom-call | flops 262144 | bytes 262144 | tf_op jit(solution)/shard_map/backward_piece/pallas_call | solution.py:298
  109.7 2.8 %backward_piece.11 = (f32[512,1024]{1,0:T(8,128)S(1)}, bf16[2,1024,2048]{2,1,0:T(8,128)(2,1)}, f32[8,128]{1,0:T(8,128)S(1)}) custom-call(s32[2]{0:T(128)S(1)} %pad_add_fusion.4.info_ref, bf16[1,128,512]{2,1,0:T(8,128)(2,1)S(1)} %collective-permute-done.39.refs_0_, ...), custom_call_target="tpu_custom_call", output_to_operand_aliasing={{0}: (6, {}), {1}: (7, {})} | custom-call | flops 262144 | bytes 262144 | tf_op jit(solution)/shard_map/backward_piece/pallas_call | solution.py:298
  113.3 2.4 %collective-permute-start.48 = (bf16[1,128,512]{2,1,0:T(8,128)(2,1)S(1)}, bf16[1,128,512]{2,1,0:T(8,128)(2,1)S(1)}, u32[]{:S(2)}, u32[]{:S(2)}) collective-permute-start(bf16[1,128,512]{2,1,0:T(8,128)(2,1)S(1)} %copy-done.13), channel_id=1, source_target_pairs={{0,8},{4,12},{8,0},{12,4},{16,24},{20,28},{24,16},{28,20},{1,9},{5... | collective-permute-start | bytes 393224 | tf_op jit(solution)/shard_map/ppermute | solution.py:23
  115.7 3.5 %backward_piece.12 = (f32[512,1024]{1,0:T(8,128)S(1)}, bf16[2,1024,2048]{2,1,0:T(8,128)(2,1)}, f32[8,128]{1,0:T(8,128)S(1)}) custom-call(s32[2]{0:T(128)S(1)} %pad_add_fusion.8.info_ref, bf16[1,128,512]{2,1,0:T(8,128)(2,1)S(1)} %copy-done.15, bf16[1,128,512]{2,1,0:T(8,128)(2,1)S(1)} %copy-done.17, ...), custom_call_target="tpu_custom_call", output_to_operand_aliasing={{0}: (6, {}), {1}: (7, {})} | custom-call | flops 262144 | bytes 262144 | tf_op jit(solution)/shard_map/backward_piece/pallas_call | solution.py:298
  119.3 3.3 %backward_piece.13 = (f32[512,1024]{1,0:T(8,128)S(1)}, bf16[2,1024,2048]{2,1,0:T(8,128)(2,1)}, f32[8,128]{1,0:T(8,128)S(1)}) custom-call(s32[2]{0:T(128)S(1)} %pad_add_fusion.1.info_ref, bf16[1,128,512]{2,1,0:T(8,128)(2,1)S(1)} %collective-permute-done.43.refs_0_, ...), custom_call_target="tpu_custom_call", output_to_operand_aliasing={{0}: (6, {}), {1}: (7, {})} | custom-call | flops 262144 | bytes 262144 | tf_op jit(solution)/shard_map/backward_piece/pallas_call | solution.py:298
  122.8 0.5 collective-permute-start.49
  123.5 3.1 %backward_piece.14 = (f32[512,1024]{1,0:T(8,128)S(1)}, bf16[2,1024,2048]{2,1,0:T(8,128)(2,1)}, f32[8,128]{1,0:T(8,128)S(1)}) custom-call(s32[2]{0:T(128)S(1)} %pad_add_fusion.7.info_ref, bf16[1,128,512]{2,1,0:T(8,128)(2,1)} %collective-permute-done.28.refs_0_, ...), custom_call_target="tpu_custom_call", output_to_operand_aliasing={{0}: (6, {}), {1}: (7, {})} | custom-call | flops 262144 | bytes 262144 | tf_op jit(solution)/shard_map/backward_piece/pallas_call | solution.py:298
  126.7 3.4 %backward_piece.15 = (f32[512,1024]{1,0:T(8,128)S(1)}, bf16[2,1024,2048]{2,1,0:T(8,128)(2,1)}, f32[8,128]{1,0:T(8,128)S(1)}) custom-call(s32[2]{0:T(128)S(1)} %pad_add_fusion.2.info_ref, bf16[1,128,512]{2,1,0:T(8,128)(2,1)S(1)} %collective-permute-done.47.refs_0_, ...), custom_call_target="tpu_custom_call", output_to_operand_aliasing={{0}: (6, {}), {1}: (7, {})} | custom-call | flops 262144 | bytes 262144 | tf_op jit(solution)/shard_map/backward_piece/pallas_call | solution.py:298
  130.2 4.7 %encoder_grad.1 = (bf16[2048,1024]{1,0:T(8,128)(2,1)}, f32[1,1024]{1,0:T(1,128)}, f32[1,1]{1,0:T(1,128)}) custom-call(s32[4]{0:T(128)S(1)} %pad_add_fusion.index_ref, bf16[1,512,512]{2,1,0:T(8,128)(2,1)S(1)} %copy-done.11, bf16[1,512,512]{2,1,0:T(8,128)(2,1)S(1)} %copy-done.9, bf16[1,512,512]{2,1,0:T(8,128)(2,1)S(1)} %copy-done.7, ...), custom_call_target="tpu_custom_call" | custom-call | flops 2147483648 | bytes 9437184 | tf_op jit(solution)/shard_map/encoder_grad/pallas_call | solution.py:352
  (138 shorter events, 6.5 us)
Async XLA Ops:
  0.6 8.3 %collective-permute-start.1 = (bf16[128,512]{1,0:T(8,128)(2,1)}, bf16[128,512]{1,0:T(8,128)(2,1)S(1)}, u32[]{:S(2)}, u32[]{:S(2)}) collective-permute-start(bf16[128,512]{1,0:T(8,128)(2,1)} %param.5), channel_id=1, source_target_pairs={{0,1},{1,0},{2,3},{3,2},{4,5},{5,4},{6,7},{7,6},{8,9},{9,8},{10,11... | collective-permute-start | bytes 393224 | tf_op jit(solution)/shard_map/ppermute | solution.py:17
  3.7 13.2 %collective-permute-start.2 = (bf16[128,512]{1,0:T(8,128)(2,1)}, bf16[128,512]{1,0:T(8,128)(2,1)S(1)}, u32[]{:S(2)}, u32[]{:S(2)}) collective-permute-start(bf16[128,512]{1,0:T(8,128)(2,1)} %param.5), channel_id=1, source_target_pairs={{0,2},{1,3},{2,0},{3,1},{4,6},{5,7},{6,4},{7,5},{8,10},{9,11},{10,... | collective-permute-start | bytes 393224 | tf_op jit(solution)/shard_map/ppermute | solution.py:17
  6.3 10.6 %collective-permute-start.3 = (bf16[128,512]{1,0:T(8,128)(2,1)}, bf16[128,512]{1,0:T(8,128)(2,1)S(1)}, u32[]{:S(2)}, u32[]{:S(2)}) collective-permute-start(bf16[128,512]{1,0:T(8,128)(2,1)} %param.5), channel_id=1, source_target_pairs={{0,3},{1,2},{2,1},{3,0},{4,7},{5,6},{6,5},{7,4},{8,11},{9,10},{10,... | collective-permute-start | bytes 393224 | tf_op jit(solution)/shard_map/ppermute | solution.py:17
  6.3 11.5 %collective-permute-start = (bf16[128,512]{1,0:T(8,128)(2,1)}, bf16[128,512]{1,0:T(8,128)(2,1)S(1)}, u32[]{:S(2)}, u32[]{:S(2)}) collective-permute-start(bf16[128,512]{1,0:T(8,128)(2,1)} %param.5), channel_id=1, source_target_pairs={{0,8},{4,12},{8,0},{12,4},{16,24},{20,28},{24,16},{28,20},{1,9},{5... | collective-permute-start | bytes 393224 | tf_op jit(solution)/shard_map/ppermute | solution.py:23
  9.0 8.9 %collective-permute-start.4 = (bf16[128,512]{1,0:T(8,128)(2,1)S(1)}, bf16[128,512]{1,0:T(8,128)(2,1)S(1)}, u32[]{:S(2)}, u32[]{:S(2)}) collective-permute-start(bf16[128,512]{1,0:T(8,128)(2,1)S(1)} %collective-permute-done.1), channel_id=1, source_target_pairs={{0,8},{4,12},{8,0},{12,4},{16,24},{20,28},{24,16},{28,20},{1,9},{5... | collective-permute-start | bytes 393224 | tf_op jit(solution)/shard_map/ppermute | solution.py:23
  17.9 2.3 %collective-permute-start.5 = (bf16[4,128,512]{2,1,0:T(8,128)(2,1)S(1)}, bf16[4,128,512]{2,1,0:T(8,128)(2,1)S(1)}, u32[]{:S(2)}, u32[]{:S(2)}) collective-permute-start(bf16[4,128,512]{2,1,0:T(8,128)(2,1)S(1)} %pad_maximum_fusion.refs_0_), channel_id=1, source_target_pairs={{0,4},{4,0},{8,12},{12,8},{16,20},{20,16},{24,28},{28,24},{1,5},{5... | collective-permute-start | bytes 1572872 | tf_op jit(solution)/shard_map/ppermute | solution.py:23
  18.0 6.4 %collective-permute-start.6 = (bf16[128,512]{1,0:T(8,128)(2,1)S(1)}, bf16[128,512]{1,0:T(8,128)(2,1)S(1)}, u32[]{:S(2)}, u32[]{:S(2)}) collective-permute-start(bf16[128,512]{1,0:T(8,128)(2,1)S(1)} %collective-permute-done.2), channel_id=1, source_target_pairs={{0,8},{4,12},{8,0},{12,4},{16,24},{20,28},{24,16},{28,20},{1,9},{5... | collective-permute-start | bytes 393224 | tf_op jit(solution)/shard_map/ppermute | solution.py:23
  19.5 7.2 %collective-permute-start.7 = (bf16[128,512]{1,0:T(8,128)(2,1)S(1)}, bf16[128,512]{1,0:T(8,128)(2,1)S(1)}, u32[]{:S(2)}, u32[]{:S(2)}) collective-permute-start(bf16[128,512]{1,0:T(8,128)(2,1)S(1)} %collective-permute-done.3), channel_id=1, source_target_pairs={{0,8},{4,12},{8,0},{12,4},{16,24},{20,28},{24,16},{28,20},{1,9},{5... | collective-permute-start | bytes 393224 | tf_op jit(solution)/shard_map/ppermute | solution.py:23
  20.2 3.9 %copy-start.2 = (bf16[4,128,512]{2,1,0:T(8,128)(2,1)}, bf16[4,128,512]{2,1,0:T(8,128)(2,1)S(1)}, u32[]{:S(2)}) copy-start(bf16[4,128,512]{2,1,0:T(8,128)(2,1)S(1)} %collective-permute-done.5.refs_1_) | copy-start | bytes 1572868
  26.7 2.0 %collective-permute-start.8 = (bf16[4,128,512]{2,1,0:T(8,128)(2,1)S(1)}, bf16[4,128,512]{2,1,0:T(8,128)(2,1)S(1)}, u32[]{:S(2)}, u32[]{:S(2)}) collective-permute-start(bf16[4,128,512]{2,1,0:T(8,128)(2,1)S(1)} %pad_maximum_fusion.1.piece_ref), channel_id=1, source_target_pairs={{0,4},{4,0},{8,12},{12,8},{16,20},{20,16},{24,28},{28,24},{1,5},{5... | collective-permute-start | bytes 1572872 | tf_op jit(solution)/shard_map/ppermute | solution.py:23
  29.6 41.2 %copy-start = (bf16[2,512,1024]{2,1,0:T(8,128)(2,1)}, bf16[2,512,1024]{2,1,0:T(8,128)(2,1)S(1)}, u32[]{:S(2)}) copy-start(bf16[2,512,1024]{2,1,0:T(8,128)(2,1)S(1)} %encode_next.3.feat_ref.refs_4_) | copy-start | bytes 6291460
  32.8 3.8 %collective-permute-start.9 = (bf16[2,1,128,512]{3,2,0,1:T(8,128)(2,1)S(1)}, bf16[2,1,128,512]{3,2,0,1:T(8,128)(2,1)S(1)}, u32[]{:S(2)}, u32[]{:S(2)}) collective-permute-start(bf16[2,1,128,512]{3,2,0,1:T(8,128)(2,1)S(1)} %bitcast.127), channel_id=1, source_target_pairs={{0,4},{4,0},{8,12},{12,8},{16,20},{20,16},{24,28},{28,24},{1,5},{5... | collective-permute-start | bytes 786440 | tf_op jit(solution)/shard_map/ppermute | solution.py:23
  33.0 10.7 %collective-permute-start.11 = (bf16[2,2,128,512]{3,2,1,0:T(8,128)(2,1)S(1)}, bf16[2,2,128,512]{3,2,1,0:T(8,128)(2,1)S(1)}, u32[]{:S(2)}, u32[]{:S(2)}) collective-permute-start(bf16[2,2,128,512]{3,2,1,0:T(8,128)(2,1)S(1)} %get-tuple-element.101), channel_id=1, source_target_pairs={{0,4},{4,0},{8,12},{12,8},{16,20},{20,16},{24,28},{28,24},{1,5},{5... | collective-permute-start | bytes 1572872 | tf_op jit(solution)/shard_map/ppermute | solution.py:23
  33.3 8.6 %collective-permute-start.14 = (bf16[2,1,128,512]{3,2,0,1:T(8,128)(2,1)S(1)}, bf16[2,1,128,512]{3,2,0,1:T(8,128)(2,1)S(1)}, u32[]{:S(2)}, u32[]{:S(2)}) collective-permute-start(bf16[2,1,128,512]{3,2,0,1:T(8,128)(2,1)S(1)} %bitcast.125), channel_id=1, source_target_pairs={{0,4},{4,0},{8,12},{12,8},{16,20},{20,16},{24,28},{28,24},{1,5},{5... | collective-permute-start | bytes 786440 | tf_op jit(solution)/shard_map/ppermute | solution.py:23
  39.8 18.3 %collective-permute-start.10 = (bf16[2,2,128,512]{3,2,1,0:T(8,128)(2,1)S(1)}, bf16[2,2,128,512]{3,2,1,0:T(8,128)(2,1)S(1)}, u32[]{:S(2)}, u32[]{:S(2)}) collective-permute-start(bf16[2,2,128,512]{3,2,1,0:T(8,128)(2,1)S(1)} %get-tuple-element.99), channel_id=1, source_target_pairs={{0,4},{4,0},{8,12},{12,8},{16,20},{20,16},{24,28},{28,24},{1,5},{5... | collective-permute-start | bytes 1572872 | tf_op jit(solution)/shard_map/ppermute | solution.py:23
  40.2 3.6 %collective-permute-start.12 = (bf16[2,1,128,512]{3,2,0,1:T(8,128)(2,1)S(1)}, bf16[2,1,128,512]{3,2,0,1:T(8,128)(2,1)S(1)}, u32[]{:S(2)}, u32[]{:S(2)}) collective-permute-start(bf16[2,1,128,512]{3,2,0,1:T(8,128)(2,1)S(1)} %bitcast.126), channel_id=1, source_target_pairs={{0,4},{4,0},{8,12},{12,8},{16,20},{20,16},{24,28},{28,24},{1,5},{5... | collective-permute-start | bytes 786440 | tf_op jit(solution)/shard_map/ppermute | solution.py:23
  40.3 9.6 %collective-permute-start.17 = (bf16[2,1,128,512]{3,2,0,1:T(8,128)(2,1)S(1)}, bf16[2,1,128,512]{3,2,0,1:T(8,128)(2,1)S(1)}, u32[]{:S(2)}, u32[]{:S(2)}) collective-permute-start(bf16[2,1,128,512]{3,2,0,1:T(8,128)(2,1)S(1)} %bitcast.124), channel_id=1, source_target_pairs={{0,4},{4,0},{8,12},{12,8},{16,20},{20,16},{24,28},{28,24},{1,5},{5... | collective-permute-start | bytes 786440 | tf_op jit(solution)/shard_map/ppermute | solution.py:23
  42.0 6.4 %collective-permute-start.15 = (bf16[1,1,128,512]{3,2,1,0:T(8,128)(2,1)S(1)}, bf16[1,1,128,512]{3,2,1,0:T(8,128)(2,1)S(1)}, u32[]{:S(2)}, u32[]{:S(2)}) collective-permute-start(bf16[1,1,128,512]{3,2,1,0:T(8,128)(2,1)S(1)} %slice_bitcast_fusion.10), channel_id=1, source_target_pairs={{0,8},{4,12},{8,0},{12,4},{16,24},{20,28},{24,16},{28,20},{1,9},{5... | collective-permute-start | bytes 393224 | tf_op jit(solution)/shard_map/ppermute | solution.py:23
  43.9 9.5 %collective-permute-start.18 = (bf16[1,1,128,512]{3,2,1,0:T(8,128)(2,1)S(1)}, bf16[1,1,128,512]{3,2,1,0:T(8,128)(2,1)S(1)}, u32[]{:S(2)}, u32[]{:S(2)}) collective-permute-start(bf16[1,1,128,512]{3,2,1,0:T(8,128)(2,1)S(1)} %slice_bitcast_fusion.12), channel_id=1, source_target_pairs={{0,8},{4,12},{8,0},{12,4},{16,24},{20,28},{24,16},{28,20},{1,9},{5... | collective-permute-start | bytes 393224 | tf_op jit(solution)/shard_map/ppermute | solution.py:23
  44.5 13.7 %collective-permute-start.13 = (bf16[1,2,128,512]{3,2,1,0:T(8,128)(2,1)S(1)}, bf16[1,2,128,512]{3,2,1,0:T(8,128)(2,1)S(1)}, u32[]{:S(2)}, u32[]{:S(2)}) collective-permute-start(bf16[1,2,128,512]{3,2,1,0:T(8,128)(2,1)S(1)} %get-tuple-element.104), channel_id=1, source_target_pairs={{0,16},{4,20},{8,24},{12,28},{1,17},{5,21},{9,25},{13,29},{2,18},{... | collective-permute-start | bytes 786440 | tf_op jit(solution)/shard_map/ppermute | solution.py:30
  48.4 5.7 %collective-permute-start.16 = (bf16[1,1,128,512]{3,2,1,0:T(8,128)(2,1)S(1)}, bf16[1,1,128,512]{3,2,1,0:T(8,128)(2,1)S(1)}, u32[]{:S(2)}, u32[]{:S(2)}) collective-permute-start(bf16[1,1,128,512]{3,2,1,0:T(8,128)(2,1)S(1)} %slice_bitcast_fusion.11), channel_id=1, source_target_pairs={{0,8},{4,12},{8,0},{12,4},{16,24},{20,28},{24,16},{28,20},{1,9},{5... | collective-permute-start | bytes 393224 | tf_op jit(solution)/shard_map/ppermute | solution.py:23
  50.0 8.0 %collective-permute-start.20 = (bf16[1,1,128,512]{3,2,1,0:T(8,128)(2,1)S(1)}, bf16[1,1,128,512]{3,2,1,0:T(8,128)(2,1)S(1)}, u32[]{:S(2)}, u32[]{:S(2)}) collective-permute-start(bf16[1,1,128,512]{3,2,1,0:T(8,128)(2,1)S(1)} %fusion.13), channel_id=1, source_target_pairs={{0,16},{4,20},{8,24},{12,28},{1,17},{5,21},{9,25},{13,29},{2,18},{... | collective-permute-start | bytes 393224 | tf_op jit(solution)/shard_map/ppermute | solution.py:30
  53.5 6.4 %collective-permute-start.21 = (bf16[1,1,128,512]{3,2,1,0:T(8,128)(2,1)S(1)}, bf16[1,1,128,512]{3,2,1,0:T(8,128)(2,1)S(1)}, u32[]{:S(2)}, u32[]{:S(2)}) collective-permute-start(bf16[1,1,128,512]{3,2,1,0:T(8,128)(2,1)S(1)} %slice_bitcast_fusion.9), channel_id=1, source_target_pairs={{0,8},{4,12},{8,0},{12,4},{16,24},{20,28},{24,16},{28,20},{1,9},{5... | collective-permute-start | bytes 393224 | tf_op jit(solution)/shard_map/ppermute | solution.py:23
  54.1 6.4 %collective-permute-start.22 = (bf16[1,1,128,512]{3,2,1,0:T(8,128)(2,1)S(1)}, bf16[1,1,128,512]{3,2,1,0:T(8,128)(2,1)S(1)}, u32[]{:S(2)}, u32[]{:S(2)}) collective-permute-start(bf16[1,1,128,512]{3,2,1,0:T(8,128)(2,1)S(1)} %fusion.10), channel_id=1, source_target_pairs={{0,16},{4,20},{8,24},{12,28},{1,17},{5,21},{9,25},{13,29},{2,18},{... | collective-permute-start | bytes 393224 | tf_op jit(solution)/shard_map/ppermute | solution.py:30
  58.3 10.2 %collective-permute-start.19 = (bf16[1,2,128,512]{3,2,1,0:T(8,128)(2,1)S(1)}, bf16[1,2,128,512]{3,2,1,0:T(8,128)(2,1)S(1)}, u32[]{:S(2)}, u32[]{:S(2)}) collective-permute-start(bf16[1,2,128,512]{3,2,1,0:T(8,128)(2,1)S(1)} %fusion.2), channel_id=1, source_target_pairs={{0,8},{4,12},{8,0},{12,4},{16,24},{20,28},{24,16},{28,20},{1,9},{5... | collective-permute-start | bytes 786440 | tf_op jit(solution)/shard_map/ppermute | solution.py:23
  60.5 8.2 %collective-permute-start.23 = (bf16[1,2,128,512]{3,2,1,0:T(8,128)(2,1)S(1)}, bf16[1,2,128,512]{3,2,1,0:T(8,128)(2,1)S(1)}, u32[]{:S(2)}, u32[]{:S(2)}) collective-permute-start(bf16[1,2,128,512]{3,2,1,0:T(8,128)(2,1)S(1)} %get-tuple-element.116), channel_id=1, source_target_pairs={{0,16},{4,20},{8,24},{12,28},{1,17},{5,21},{9,25},{13,29},{2,18},{... | collective-permute-start | bytes 786440 | tf_op jit(solution)/shard_map/ppermute | solution.py:30
  65.1 8.1 %collective-permute-start.24 = (bf16[128,512]{1,0:T(8,128)(2,1)S(1)}, bf16[128,512]{1,0:T(8,128)(2,1)S(1)}, u32[]{:S(2)}, u32[]{:S(2)}) collective-permute-start(bf16[128,512]{1,0:T(8,128)(2,1)S(1)} %fusion.16), channel_id=1, source_target_pairs={{0,3},{1,2},{2,1},{3,0},{4,7},{5,6},{6,5},{7,4},{8,11},{9,10},{10,... | collective-permute-start | bytes 393224 | tf_op jit(solution)/shard_map/ppermute | solution.py:17
  67.4 9.5 %collective-permute-start.25 = (bf16[128,512]{1,0:T(8,128)(2,1)S(1)}, bf16[128,512]{1,0:T(8,128)(2,1)S(1)}, u32[]{:S(2)}, u32[]{:S(2)}) collective-permute-start(bf16[128,512]{1,0:T(8,128)(2,1)S(1)} %fusion.17), channel_id=1, source_target_pairs={{0,2},{1,3},{2,0},{3,1},{4,6},{5,7},{6,4},{7,5},{8,10},{9,11},{10,... | collective-permute-start | bytes 393224 | tf_op jit(solution)/shard_map/ppermute | solution.py:17
  68.9 8.0 %collective-permute-start.26 = (bf16[128,512]{1,0:T(8,128)(2,1)S(1)}, bf16[128,512]{1,0:T(8,128)(2,1)S(1)}, u32[]{:S(2)}, u32[]{:S(2)}) collective-permute-start(bf16[128,512]{1,0:T(8,128)(2,1)S(1)} %fusion.18), channel_id=1, source_target_pairs={{0,1},{1,0},{2,3},{3,2},{4,5},{5,4},{6,7},{7,6},{8,9},{9,8},{10,11... | collective-permute-start | bytes 393224 | tf_op jit(solution)/shard_map/ppermute | solution.py:17
  71.3 5.7 %copy-start.21 = (bf16[128,512]{1,0:T(8,128)(2,1)S(1)}, bf16[128,512]{1,0:T(8,128)(2,1)}, u32[]{:S(2)}) copy-start(bf16[128,512]{1,0:T(8,128)(2,1)} %param.6) | copy-start | bytes 393220
  71.5 6.3 %copy-start.4 = (bf16[1,512,512]{2,1,0:T(8,128)(2,1)}, bf16[1,512,512]{2,1,0:T(8,128)(2,1)S(1)}, u32[]{:S(2)}) copy-start(bf16[1,512,512]{2,1,0:T(8,128)(2,1)S(1)} %turned.9.refs_3_) | copy-start | bytes 1572868
  71.7 23.5 %copy-start.6 = (bf16[1,512,512]{2,1,0:T(8,128)(2,1)}, bf16[1,512,512]{2,1,0:T(8,128)(2,1)S(1)}, u32[]{:S(2)}) copy-start(bf16[1,512,512]{2,1,0:T(8,128)(2,1)S(1)} %turned.8.refs_2_) | copy-start | bytes 1572868
  72.1 23.0 %copy-start.8 = (bf16[1,512,512]{2,1,0:T(8,128)(2,1)}, bf16[1,512,512]{2,1,0:T(8,128)(2,1)S(1)}, u32[]{:S(2)}) copy-start(bf16[1,512,512]{2,1,0:T(8,128)(2,1)S(1)} %turned.7.refs_1_) | copy-start | bytes 1572868
  77.7 6.9 %collective-permute-start.27 = (bf16[1,128,512]{2,1,0:T(8,128)(2,1)S(1)}, bf16[1,128,512]{2,1,0:T(8,128)(2,1)S(1)}, u32[]{:S(2)}, u32[]{:S(2)}) collective-permute-start(bf16[1,128,512]{2,1,0:T(8,128)(2,1)S(1)} %bitcast.119), channel_id=1, source_target_pairs={{0,16},{4,20},{8,24},{12,28},{16,0},{20,4},{24,8},{28,12},{1,17},{... | collective-permute-start | bytes 393224 | tf_op jit(solution)/shard_map/ppermute | solution.py:36
  78.8 7.1 %collective-permute-start.31 = (bf16[128,512]{1,0:T(8,128)(2,1)S(1)}, bf16[128,512]{1,0:T(8,128)(2,1)}, u32[]{:S(2)}, u32[]{:S(2)}) collective-permute-start(bf16[128,512]{1,0:T(8,128)(2,1)S(1)} %get-tuple-element.163), channel_id=1, source_target_pairs={{0,1},{1,0},{2,3},{3,2},{4,5},{5,4},{6,7},{7,6},{8,9},{9,8},{10,11... | collective-permute-start | bytes 393224 | tf_op jit(solution)/shard_map/ppermute | solution.py:17
  79.1 10.3 %collective-permute-start.33 = (bf16[128,512]{1,0:T(8,128)(2,1)S(1)}, bf16[128,512]{1,0:T(8,128)(2,1)S(1)}, u32[]{:S(2)}, u32[]{:S(2)}) collective-permute-start(bf16[128,512]{1,0:T(8,128)(2,1)S(1)} %get-tuple-element.163), channel_id=1, source_target_pairs={{0,2},{1,3},{2,0},{3,1},{4,6},{5,7},{6,4},{7,5},{8,10},{9,11},{10,... | collective-permute-start | bytes 393224 | tf_op jit(solution)/shard_map/ppermute | solution.py:17
  81.7 9.2 %collective-permute-start.34 = (bf16[128,512]{1,0:T(8,128)(2,1)S(1)}, bf16[128,512]{1,0:T(8,128)(2,1)S(1)}, u32[]{:S(2)}, u32[]{:S(2)}) collective-permute-start(bf16[128,512]{1,0:T(8,128)(2,1)S(1)} %get-tuple-element.163), channel_id=1, source_target_pairs={{0,3},{1,2},{2,1},{3,0},{4,7},{5,6},{6,5},{7,4},{8,11},{9,10},{10,... | collective-permute-start | bytes 393224 | tf_op jit(solution)/shard_map/ppermute | solution.py:17
  83.1 7.9 %collective-permute-start.29 = (bf16[1,128,512]{2,1,0:T(8,128)(2,1)S(1)}, bf16[1,128,512]{2,1,0:T(8,128)(2,1)S(1)}, u32[]{:S(2)}, u32[]{:S(2)}) collective-permute-start(bf16[1,128,512]{2,1,0:T(8,128)(2,1)S(1)} %bitcast.120), channel_id=1, source_target_pairs={{0,8},{4,12},{8,0},{12,4},{16,24},{20,28},{24,16},{28,20},{1,9},{5... | collective-permute-start | bytes 393224 | tf_op jit(solution)/shard_map/ppermute | solution.py:23
  84.6 10.5 %copy-start.18 = (bf16[1,128,512]{2,1,0:T(8,128)(2,1)}, bf16[1,128,512]{2,1,0:T(8,128)(2,1)S(1)}, u32[]{:S(2)}) copy-start(bf16[1,128,512]{2,1,0:T(8,128)(2,1)S(1)} %collective-permute-done.27.refs_0_) | copy-start | bytes 393220
  84.6 7.0 %collective-permute-start.28 = (bf16[1,128,512]{2,1,0:T(8,128)(2,1)S(1)}, bf16[1,128,512]{2,1,0:T(8,128)(2,1)}, u32[]{:S(2)}, u32[]{:S(2)}) collective-permute-start(bf16[1,128,512]{2,1,0:T(8,128)(2,1)S(1)} %collective-permute-done.27.refs_0_), channel_id=1, source_target_pairs={{0,8},{4,12},{8,0},{12,4},{16,24},{20,28},{24,16},{28,20},{1,9},{5... | collective-permute-start | bytes 393224 | tf_op jit(solution)/shard_map/ppermute | solution.py:23
  85.8 7.5 %collective-permute-start.36 = (bf16[1,128,512]{2,1,0:T(8,128)(2,1)}, bf16[1,128,512]{2,1,0:T(8,128)(2,1)S(1)}, u32[]{:S(2)}, u32[]{:S(2)}) collective-permute-start(bf16[1,128,512]{2,1,0:T(8,128)(2,1)} %bitcast.51.refs_1_), channel_id=1, source_target_pairs={{0,16},{4,20},{8,24},{12,28},{16,0},{20,4},{24,8},{28,12},{1,17},{... | collective-permute-start | bytes 393224 | tf_op jit(solution)/shard_map/ppermute | solution.py:36
  89.4 5.7 %collective-permute-start.37 = (bf16[1,128,512]{2,1,0:T(8,128)(2,1)}, bf16[1,128,512]{2,1,0:T(8,128)(2,1)S(1)}, u32[]{:S(2)}, u32[]{:S(2)}) collective-permute-start(bf16[1,128,512]{2,1,0:T(8,128)(2,1)} %bitcast.51.refs_1_), channel_id=1, source_target_pairs={{0,8},{4,12},{8,0},{12,4},{16,24},{20,28},{24,16},{28,20},{1,9},{5... | collective-permute-start | bytes 393224 | tf_op jit(solution)/shard_map/ppermute | solution.py:23
  90.9 8.5 %collective-permute-start.35 = (bf16[2,128,512]{2,1,0:T(8,128)(2,1)S(1)}, bf16[2,128,512]{2,1,0:T(8,128)(2,1)}, u32[]{:S(2)}, u32[]{:S(2)}) collective-permute-start(bf16[2,128,512]{2,1,0:T(8,128)(2,1)S(1)} %pad_maximum_fusion.2.refs_2_), channel_id=1, source_target_pairs={{0,4},{4,0},{8,12},{12,8},{16,20},{20,16},{24,28},{28,24},{1,5},{5... | collective-permute-start | bytes 786440 | tf_op jit(solution)/shard_map/ppermute | solution.py:23
  91.0 4.2 %copy-start.14 = (bf16[1,128,512]{2,1,0:T(8,128)(2,1)}, bf16[1,128,512]{2,1,0:T(8,128)(2,1)S(1)}, u32[]{:S(2)}) copy-start(bf16[1,128,512]{2,1,0:T(8,128)(2,1)S(1)} %collective-permute-done.29.refs_0_) | copy-start | bytes 393220
  91.0 12.0 %collective-permute-start.38 = (bf16[2,128,512]{2,1,0:T(8,128)(2,1)S(1)}, bf16[2,128,512]{2,1,0:T(8,128)(2,1)}, u32[]{:S(2)}, u32[]{:S(2)}) collective-permute-start(bf16[2,128,512]{2,1,0:T(8,128)(2,1)S(1)} %pad_maximum_fusion.2.refs_2_), channel_id=1, source_target_pairs={{0,8},{4,12},{8,0},{12,4},{16,24},{20,28},{24,16},{28,20},{1,9},{5... | collective-permute-start | bytes 786440 | tf_op jit(solution)/shard_map/ppermute | solution.py:23
  91.6 11.4 %collective-permute-start.41 = (bf16[2,128,512]{2,1,0:T(8,128)(2,1)S(1)}, bf16[2,128,512]{2,1,0:T(8,128)(2,1)}, u32[]{:S(2)}, u32[]{:S(2)}) collective-permute-start(bf16[2,128,512]{2,1,0:T(8,128)(2,1)S(1)} %pad_maximum_fusion.2.refs_2_), channel_id=1, source_target_pairs={{0,16},{4,20},{8,24},{12,28},{16,0},{20,4},{24,8},{28,12},{1,17},{... | collective-permute-start | bytes 786440 | tf_op jit(solution)/shard_map/ppermute | solution.py:36
  93.3 6.1 %collective-permute-start.30 = (bf16[1,128,512]{2,1,0:T(8,128)(2,1)S(1)}, bf16[1,128,512]{2,1,0:T(8,128)(2,1)S(1)}, u32[]{:S(2)}, u32[]{:S(2)}) collective-permute-start(bf16[1,128,512]{2,1,0:T(8,128)(2,1)S(1)} %bitcast.121), channel_id=1, source_target_pairs={{0,4},{4,0},{8,12},{12,8},{16,20},{20,16},{24,28},{28,24},{1,5},{5... | collective-permute-start | bytes 393224 | tf_op jit(solution)/shard_map/ppermute | solution.py:23
  95.1 4.3 %collective-permute-start.32 = (bf16[1,128,512]{2,1,0:T(8,128)(2,1)}, bf16[1,128,512]{2,1,0:T(8,128)(2,1)S(1)}, u32[]{:S(2)}, u32[]{:S(2)}) collective-permute-start(bf16[1,128,512]{2,1,0:T(8,128)(2,1)} %bitcast.51.refs_1_), channel_id=1, source_target_pairs={{0,4},{4,0},{8,12},{12,8},{16,20},{20,16},{24,28},{28,24},{1,5},{5... | collective-permute-start | bytes 393224 | tf_op jit(solution)/shard_map/ppermute | solution.py:23
  99.4 3.7 %copy-start.13 = (bf16[1,128,512]{2,1,0:T(8,128)(2,1)S(1)}, bf16[1,128,512]{2,1,0:T(8,128)(2,1)}, u32[]{:S(2)}) copy-start(bf16[1,128,512]{2,1,0:T(8,128)(2,1)} %copy-done.12) | copy-start | bytes 393220
  103.0 6.7 %collective-permute-start.42 = (bf16[2,128,512]{2,1,0:T(8,128)(2,1)}, bf16[2,128,512]{2,1,0:T(8,128)(2,1)S(1)}, u32[]{:S(2)}, u32[]{:S(2)}) collective-permute-start(bf16[2,128,512]{2,1,0:T(8,128)(2,1)} %collective-permute-done.41.refs_2_), channel_id=1, source_target_pairs={{0,4},{4,0},{8,12},{12,8},{16,20},{20,16},{24,28},{28,24},{1,5},{5... | collective-permute-start | bytes 786440 | tf_op jit(solution)/shard_map/ppermute | solution.py:23
  103.1 6.6 %collective-permute-start.40 = (bf16[1,128,512]{2,1,0:T(8,128)(2,1)S(1)}, bf16[1,128,512]{2,1,0:T(8,128)(2,1)S(1)}, u32[]{:S(2)}, u32[]{:S(2)}) collective-permute-start(bf16[1,128,512]{2,1,0:T(8,128)(2,1)S(1)} %copy-done.13), channel_id=1, source_target_pairs={{0,4},{4,0},{8,12},{12,8},{16,20},{20,16},{24,28},{28,24},{1,5},{5... | collective-permute-start | bytes 393224 | tf_op jit(solution)/shard_map/ppermute | solution.py:23
  103.6 6.1 %collective-permute-start.39 = (bf16[1,128,512]{2,1,0:T(8,128)(2,1)}, bf16[1,128,512]{2,1,0:T(8,128)(2,1)S(1)}, u32[]{:S(2)}, u32[]{:S(2)}) collective-permute-start(bf16[1,128,512]{2,1,0:T(8,128)(2,1)} %copy-done.18), channel_id=1, source_target_pairs={{0,4},{4,0},{8,12},{12,8},{16,20},{20,16},{24,28},{28,24},{1,5},{5... | collective-permute-start | bytes 393224 | tf_op jit(solution)/shard_map/ppermute | solution.py:23
  103.8 15.4 %collective-permute-start.46 = (bf16[2,128,512]{2,1,0:T(8,128)(2,1)}, bf16[2,128,512]{2,1,0:T(8,128)(2,1)S(1)}, u32[]{:S(2)}, u32[]{:S(2)}) collective-permute-start(bf16[2,128,512]{2,1,0:T(8,128)(2,1)} %collective-permute-done.38.refs_2_), channel_id=1, source_target_pairs={{0,16},{4,20},{8,24},{12,28},{16,0},{20,4},{24,8},{28,12},{1,17},{... | collective-permute-start | bytes 786440 | tf_op jit(solution)/shard_map/ppermute | solution.py:36
  112.5 6.8 %collective-permute-start.45 = (bf16[2,128,512]{2,1,0:T(8,128)(2,1)}, bf16[2,128,512]{2,1,0:T(8,128)(2,1)S(1)}, u32[]{:S(2)}, u32[]{:S(2)}) collective-permute-start(bf16[2,128,512]{2,1,0:T(8,128)(2,1)} %collective-permute-done.38.refs_2_), channel_id=1, source_target_pairs={{0,4},{4,0},{8,12},{12,8},{16,20},{20,16},{24,28},{28,24},{1,5},{5... | collective-permute-start | bytes 786440 | tf_op jit(solution)/shard_map/ppermute | solution.py:23
  112.7 6.6 %collective-permute-start.44 = (bf16[1,128,512]{2,1,0:T(8,128)(2,1)S(1)}, bf16[1,128,512]{2,1,0:T(8,128)(2,1)S(1)}, u32[]{:S(2)}, u32[]{:S(2)}) collective-permute-start(bf16[1,128,512]{2,1,0:T(8,128)(2,1)S(1)} %copy-done.17), channel_id=1, source_target_pairs={{0,4},{4,0},{8,12},{12,8},{16,20},{20,16},{24,28},{28,24},{1,5},{5... | collective-permute-start | bytes 393224 | tf_op jit(solution)/shard_map/ppermute | solution.py:23
  113.1 6.2 %collective-permute-start.43 = (bf16[1,128,512]{2,1,0:T(8,128)(2,1)S(1)}, bf16[1,128,512]{2,1,0:T(8,128)(2,1)S(1)}, u32[]{:S(2)}, u32[]{:S(2)}) collective-permute-start(bf16[1,128,512]{2,1,0:T(8,128)(2,1)S(1)} %copy-done.15), channel_id=1, source_target_pairs={{0,4},{4,0},{8,12},{12,8},{16,20},{20,16},{24,28},{28,24},{1,5},{5... | collective-permute-start | bytes 393224 | tf_op jit(solution)/shard_map/ppermute | solution.py:23
  113.3 9.5 %collective-permute-start.48 = (bf16[1,128,512]{2,1,0:T(8,128)(2,1)S(1)}, bf16[1,128,512]{2,1,0:T(8,128)(2,1)S(1)}, u32[]{:S(2)}, u32[]{:S(2)}) collective-permute-start(bf16[1,128,512]{2,1,0:T(8,128)(2,1)S(1)} %copy-done.13), channel_id=1, source_target_pairs={{0,8},{4,12},{8,0},{12,4},{16,24},{20,28},{24,16},{28,20},{1,9},{5... | collective-permute-start | bytes 393224 | tf_op jit(solution)/shard_map/ppermute | solution.py:23
  122.6 4.0 %collective-permute-start.50 = (bf16[2,128,512]{2,1,0:T(8,128)(2,1)S(1)}, bf16[2,128,512]{2,1,0:T(8,128)(2,1)S(1)}, u32[]{:S(2)}, u32[]{:S(2)}) collective-permute-start(bf16[2,128,512]{2,1,0:T(8,128)(2,1)S(1)} %collective-permute-done.46.refs_2_), channel_id=1, source_target_pairs={{0,4},{4,0},{8,12},{12,8},{16,20},{20,16},{24,28},{28,24},{1,5},{5... | collective-permute-start | bytes 786440 | tf_op jit(solution)/shard_map/ppermute | solution.py:23
  122.8 3.8 %collective-permute-start.49 = (bf16[1,128,512]{2,1,0:T(8,128)(2,1)S(1)}, bf16[1,128,512]{2,1,0:T(8,128)(2,1)S(1)}, u32[]{:S(2)}, u32[]{:S(2)}) collective-permute-start(bf16[1,128,512]{2,1,0:T(8,128)(2,1)S(1)} %collective-permute-done.48.refs_1_), channel_id=1, source_target_pairs={{0,4},{4,0},{8,12},{12,8},{16,20},{20,16},{24,28},{28,24},{1,5},{5... | collective-permute-start | bytes 393224 | tf_op jit(solution)/shard_map/ppermute | solution.py:23
  123.3 3.4 %collective-permute-start.47 = (bf16[1,128,512]{2,1,0:T(8,128)(2,1)}, bf16[1,128,512]{2,1,0:T(8,128)(2,1)S(1)}, u32[]{:S(2)}, u32[]{:S(2)}) collective-permute-start(bf16[1,128,512]{2,1,0:T(8,128)(2,1)} %collective-permute-done.28.refs_0_), channel_id=1, source_target_pairs={{0,4},{4,0},{8,12},{12,8},{16,20},{20,16},{24,28},{28,24},{1,5},{5... | collective-permute-start | bytes 393224 | tf_op jit(solution)/shard_map/ppermute | solution.py:23
  126.7 3.5 %copy-start.1 = (bf16[2,512,1024]{2,1,0:T(8,128)(2,1)S(1)}, bf16[2,512,1024]{2,1,0:T(8,128)(2,1)}, u32[]{:S(2)}) copy-start(bf16[2,512,1024]{2,1,0:T(8,128)(2,1)} %copy-done) | copy-start | bytes 6291460
  126.7 3.5 %copy-start.5 = (bf16[1,512,512]{2,1,0:T(8,128)(2,1)S(1)}, bf16[1,512,512]{2,1,0:T(8,128)(2,1)}, u32[]{:S(2)}) copy-start(bf16[1,512,512]{2,1,0:T(8,128)(2,1)} %copy-done.4) | copy-start | bytes 1572868
  126.7 3.5 %copy-start.7 = (bf16[1,512,512]{2,1,0:T(8,128)(2,1)S(1)}, bf16[1,512,512]{2,1,0:T(8,128)(2,1)}, u32[]{:S(2)}) copy-start(bf16[1,512,512]{2,1,0:T(8,128)(2,1)} %copy-done.6) | copy-start | bytes 1572868
  126.7 3.5 %copy-start.9 = (bf16[1,512,512]{2,1,0:T(8,128)(2,1)S(1)}, bf16[1,512,512]{2,1,0:T(8,128)(2,1)}, u32[]{:S(2)}) copy-start(bf16[1,512,512]{2,1,0:T(8,128)(2,1)} %copy-done.8) | copy-start | bytes 1572868
  (9 other events, 17.0 us)

commit v2 on v1

--- a/solution.py
+++ b/solution.py
@@ -25,9 +25,10 @@
 
 def to_layer(value, offset, sub_count):
     count = lax.axis_size("layer")
-    shift = offset * sub_count
-    pairs = [(p, p + shift) for p in range(count - shift)]
-    return lax.ppermute(value, "layer", pairs)
+    pairs = [(p, (p + offset * sub_count) % count) for p in range(count)]
+    moved = lax.ppermute(value, "layer", pairs)
+    real = lax.axis_index("layer") >= offset * sub_count
+    return jnp.where(real, moved, jnp.zeros_like(moved))
 
 
 def from_layer(value, offset, sub_count):
@@ -66,7 +67,7 @@
     return pl.ds(pl.multiple_of(index * size, size), size)
 
 
-def in_parts(source, target, sems, first, count=8):
+def in_parts(source, target, sems, first, count=4):
     size = target.shape[0] // count
     return [
         pltpu.make_async_copy(
@@ -78,7 +79,7 @@
     ]
 
 
-def encode_first(indices, pieces, enc_weight, dec_weight, offset, late, ahead):
+def encode_first(indices, pieces, enc_weight, dec_weight, offset, late):
     feat_count, rows, cols = pieces[0].shape
     tok = feat_count * rows
     width = enc_weight.shape[1]
@@ -91,20 +92,18 @@
         for i in range(now + late):
             target = held.at[i] if i < now else late_ref.at[i - now]
             source = weight_ref.at[span(index_ref[i], cols)]
-            copies += in_parts(source, target, sems, 8 * i)
-        for i in range(ahead):
-            source = next_ref.at[offset, :, span(index_ref[now + late + i], cols)]
-            copies += in_parts(source, ahead_ref.at[i], sems, 8 * (now + late + i))
+            copies += in_parts(source, target, sems, 4 * i)
+        copies += in_parts(next_ref.at[offset], ahead_ref, sems, 4 * (now + late))
         for copy in copies:
             copy.start()
-        for copy in copies[: 8 * now]:
+        for copy in copies[: 4 * now]:
             copy.wait()
         left = jnp.concatenate([ref[...].reshape(tok, cols) for ref in piece_refs], 1)
         for start in range(0, width, tile):
             here = slice(start, start + tile)
             right = jnp.concatenate([held[i, :, here] for i in range(now)], 0)
             out_ref[:, here] = dot(left, right, (1, 0))
-        for copy in copies[8 * now :]:
+        for copy in copies[4 * now :]:
             copy.wait()
 
     return pl.pallas_call(
@@ -114,14 +113,14 @@
         out_shape=[
             jax.ShapeDtypeStruct((tok, width), jnp.float32),
             jax.ShapeDtypeStruct((late, cols, width), jnp.bfloat16),
-            jax.ShapeDtypeStruct((ahead, width, cols), jnp.bfloat16),
+            jax.ShapeDtypeStruct(dec_weight.shape[1:], jnp.bfloat16),
         ],
         scratch_shapes=[
             pltpu.VMEM((now, cols, width), jnp.bfloat16),
-            pltpu.SemaphoreType.DMA((8 * (now + late + ahead),)),
+            pltpu.SemaphoreType.DMA((4 * (now + late + 1),)),
         ],
         name="encode_first",
-        **params(2 * now * tok * cols * width, 2 * (now + late + 2 * ahead) * cols * width, 12),
+        **params(2 * now * tok * cols * width, 4 * (now + late) * cols * width, 6),
     )(indices, *pieces, enc_weight, dec_weight)
 
 
@@ -157,50 +156,56 @@
     )(piece, weights, *extra)
 
 
-def decode(features, weights, groups, rows, indices=None, dec_weight=None, offset=None):
+def decode(member, features, weights, groups, rows, cols, dec_weight=None, offset=None):
     _, tok, width = features.shape
-    count, _, cols = weights.shape
-    ahead = indices is not None
-
-    def kernel(feat_ref, weight_ref, *refs):
+    count = weights.shape[1] // cols // 2
+    ahead = dec_weight is not None
+
+    def kernel(member_ref, feat_ref, weight_ref, *refs):
         if ahead:
-            index_ref, next_ref = refs[:2]
-            out_refs, next_out, sems = refs[2:-2], refs[-2], refs[-1]
-            copies = []
-            for i in range(count):
-                source = next_ref.at[offset, :, span(index_ref[i], cols)]
-                copies += in_parts(source, next_out.at[i], sems, 8 * i)
+            copies = in_parts(refs[0].at[offset], refs[-2], refs[-1], 0)
             for copy in copies:
                 copy.start()
+            out_refs = refs[1:-2]
         else:
             out_refs = refs
         left = feat_ref[0]
-        for piece in range(count):
+        even = member_ref[0] % 2 == 0
+        for pair in range(count):
+            piece = pair ^ (member_ref[0] // 2)
             for start in range(0, cols, tile):
-                here = slice(start, start + tile)
-                product = dot(left, weight_ref[piece, :, here], (1, 0)).astype(jnp.bfloat16)
-                for group, out_ref in zip(groups, out_refs):
-                    for place, block in enumerate(group):
-                        out_ref[piece, place, :, here] = product[block * rows : (block + 1) * rows]
+                low, high = (
+                    dot(left, weight_ref[:, base + start : base + start + tile], (1, 0)).astype(
+                        jnp.bfloat16
+                    )
+                    for base in (2 * pair * cols, (2 * pair + 1) * cols)
+                )
+                sides = (jnp.where(even, high, low), jnp.where(even, low, high))
+                for side, product in enumerate(sides):
+                    for number, group in enumerate(groups):
+                        for place, block in enumerate(group):
+                            out_refs[side * len(groups) + number][
+                                piece, place, :, start : start + tile
+                            ] = product[block * rows : (block + 1) * rows]
         if ahead:
             for copy in copies:
                 copy.wait()
 
     out_shape = [
         jax.ShapeDtypeStruct((count, len(group), rows, cols), jnp.bfloat16) for group in groups
-    ]
+    ] * 2
     if ahead:
-        out_shape.append(jax.ShapeDtypeStruct((count, width, cols), jnp.bfloat16))
+        out_shape.append(jax.ShapeDtypeStruct(weights.shape, jnp.bfloat16))
     result = pl.pallas_call(
         kernel,
-        in_specs=[in_vmem] * 2 + ([in_smem, in_hbm] if ahead else []),
+        in_specs=[in_smem] + [in_vmem] * 2 + ([in_hbm] if ahead else []),
         out_specs=[in_vmem] * len(out_shape),
         out_shape=out_shape,
-        scratch_shapes=[pltpu.SemaphoreType.DMA((8 * count,))] if ahead else [],
+        scratch_shapes=[pltpu.SemaphoreType.DMA((4,))] if ahead else [],
         name="decode",
-        **params(2 * count * tok * cols * width, 2 * count * cols * width, 8),
-    )(features, weights, *([indices, dec_weight] if ahead else []))
-    return result[: len(groups)], (result[-1] if ahead else None)
+        **params(4 * count * tok * cols * width, 4 * count * cols * width, 4),
+    )(member, features, weights, *([dec_weight] if ahead else []))
+    return result[: len(groups)], result[len(groups) : 2 * len(groups)], result[-1]
 
 
 def turned(value):
@@ -229,18 +234,19 @@
     return values[0]
 
 
-def backward_piece(info, offset, grads, turned_features, dec_weight, feature_grad, dec_grad):
+def backward_pair(info, offset, own, other, turned_features, dec_weight, feature_grad, dec_grad):
     layers, width, depth = dec_weight.shape
     tok = turned_features.shape[1]
-    cols = grads[0].shape[2]
+    cols = own[0].shape[2]
     first = feature_grad is None
     extra = [] if first else [feature_grad, dec_grad]
+    inputs = [*own, *other]
 
     def kernel(info_ref, *refs):
-        grad_refs = refs[: len(grads)]
-        feat_ref, weight_ref = refs[len(grads) : len(grads) + 2]
+        grad_refs = refs[: len(inputs)]
+        feat_ref, weight_ref = refs[len(inputs) : len(inputs) + 2]
         out_ref, dec_ref, square_ref, held, weights, sems = refs[-6:]
-        columns = span(info_ref[0], cols)
+        columns = span(info_ref[1], 2 * cols)
         starts = range(0, width, tile)
         fetches = in_parts(weight_ref.at[offset, :, columns], weights, sems, len(starts))
         for fetch in fetches:
@@ -253,19 +259,26 @@
             )
             for place, start in enumerate(starts)
         ]
-        blocks = [ref[i] for ref in grad_refs for i in range(ref.shape[0])]
-        sums = []
-        for block in blocks:
-            total = jnp.zeros((8, 128), jnp.float32)
-            for row in range(0, block.shape[0], 8):
-                for col in range(0, cols, 128):
-                    part = block[row : row + 8, col : col + 128].astype(jnp.float32)
-                    total += part * part
-            sums.append(total)
+        sides, sums = [], []
+        for side in (grad_refs[: len(own)], grad_refs[len(own) :]):
+            blocks = [ref[i] for ref in side for i in range(ref.shape[0])]
+            totals = []
+            for block in blocks:
+                total = jnp.zeros((8, 128), jnp.float32)
+                for row in range(0, block.shape[0], 8):
+                    for col in range(0, cols, 128):
+                        part = block[row : row + 8, col : col + 128].astype(jnp.float32)
+                        total += part * part
+                totals.append(total)
+            sums.append(tree_sum(totals))
+            sides.append(jnp.concatenate(blocks, 0))
         square_ref[...] = tree_sum(sums)
 
         def products():
-            grad = jnp.concatenate(blocks, 0)
+            second = info_ref[0] > 0
+            grad = jnp.concatenate(
+                [jnp.where(second, sides[1], sides[0]), jnp.where(second, sides[0], sides[1])], 1
+            )
             for copy, start in zip(copies, starts):
                 here = slice(start, start + tile)
                 held[here] = dot(feat_ref[here], grad, (1, 0)).astype(jnp.bfloat16)
@@ -276,29 +289,29 @@
                 here = slice(start, start + tile)
                 product = dot(grad, weights[here], (1, 1))
                 if not first:
-                    product += refs[len(grads) + 2][:, here]
+                    product += refs[len(inputs) + 2][:, here]
                 out_ref[:, here] = product
 
         def nothing():
             held[...] = jnp.zeros_like(held)
             for copy in copies:
                 copy.start()
-            out_ref[...] = refs[len(grads) + 2][...]
+            out_ref[...] = refs[len(inputs) + 2][...]
             for fetch in fetches:
                 fetch.wait()
 
         if offset == 0:
             products()
         else:
-            pl.when(info_ref[1] > 0)(products)
-            pl.when(info_ref[1] == 0)(nothing)
+            pl.when(info_ref[2] > 0)(products)
+            pl.when(info_ref[2] == 0)(nothing)
         for copy in copies:
             copy.wait()
 
     return pl.pallas_call(
         kernel,
         in_specs=[in_smem]
-        + [in_vmem] * (len(grads) + 1)
+        + [in_vmem] * (len(inputs) + 1)
         + [in_hbm]
         + ([] if first else [in_vmem, in_hbm]),
         out_specs=[in_vmem, in_hbm, in_vmem],
@@ -308,14 +321,14 @@
             jax.ShapeDtypeStruct((8, 128), jnp.float32),
         ],
         scratch_shapes=[
-            pltpu.VMEM((width, cols), jnp.bfloat16),
-            pltpu.VMEM((width, cols), jnp.bfloat16),
-            pltpu.SemaphoreType.DMA((width // tile + 8,)),
+            pltpu.VMEM((width, 2 * cols), jnp.bfloat16),
+            pltpu.VMEM((width, 2 * cols), jnp.bfloat16),
+            pltpu.SemaphoreType.DMA((width // tile + 4,)),
         ],
-        input_output_aliases={} if first else {len(grads) + 3: 0, len(grads) + 4: 1},
-        name="backward_piece",
-        **params(tok * cols, tok * cols, 6),
-    )(info, *grads, turned_features, dec_weight, *extra)
+        input_output_aliases={} if first else {len(inputs) + 3: 0, len(inputs) + 4: 1},
+        name="backward_pair",
+        **params(tok * cols, tok * cols, 10),
+    )(info, *inputs, turned_features, dec_weight, *extra)
 
 
 def encoder_grad(indices, turned_tokens, features, feature_grad, squares, scale):
@@ -382,8 +395,6 @@
     rows, cols = tokens_in.shape
     tok = feat_count * rows
     bit_count = sub_count.bit_length() - 1
-    near = member ^ (2 * jnp.arange(sub_count // 2, dtype=jnp.int32))
-    far = near ^ 1
     groups = [list(range(feat_count // 2))]
     groups += [[s] for s in range(feat_count // 2, feat_count)]
 
@@ -405,13 +416,12 @@
     tokens = {0: after(jnp.stack(held[0], 0), *early)}
     tokens[1] = over_members(tokens[0], 0)
     partial, late_weights, weights = encode_first(
-        jnp.concatenate([jnp.stack([member ^ rel for rel in order]), far]),
+        jnp.stack([member ^ rel for rel in order]),
         [tokens[0], tokens[1]],
         enc_weight,
         dec_weight,
         layers - 1,
         len(order) - 2,
-        len(order) // 2,
     )
     for rel in order[2::2]:
         tokens[rel] = jnp.stack([after(block, partial) for block in held[rel]], 0)
@@ -424,11 +434,10 @@
 
     current, source = {}, features
     for k in reversed(range(layers)):
-        sent, weights = decode(source, weights, groups, rows, near, dec_weight, k)
-        if k > 0:
-            kept, weights = decode(source, weights, groups, rows, far, dec_weight, k - 1)
-        else:
-            kept, weights = decode(source, weights, groups, rows)
+        ahead = (dec_weight, k - 1) if k > 0 else ()
+        sent, kept, weights = decode(
+            member.reshape(1), source, weights, groups, rows, cols, *ahead
+        )
         for place in reversed(range(len(groups))):
             current[place, k] = add_pair(kept[place], over_members(sent[place], 0))
         source = after(features, current[len(groups) - 1, k])
@@ -516,29 +525,27 @@
     feature_grad, dec_grad, squares = None, None, {}
     for number, stage in enumerate(stages):
         for k in range(layers):
-            if k > 0 and number + 1 < len(stages):
-                guard = [part for rel in stages[number + 1] for part in groups_of[rel, k - 1]]
-                feature_grad = after(feature_grad, *guard)
             for rel in stage:
                 parts = groups_of[rel, k]
-                if feature_grad is not None:
+                if feature_grad is None:
+                    parts = [after(parts[0], *early)] + parts[1:]
+                else:
                     parts = [after(part, feature_grad) for part in parts]
-                groups_of[rel ^ 1, k] = [over_members(part, 0) for part in parts]
-                if feature_grad is None:
-                    groups_of[rel, k][0] = after(parts[0], *early)
-                for half in (rel, rel ^ 1):
-                    if k == 0 and number > 0:
-                        coming = groups_of[rel, layers - 1][-(half % 2)]
-                        feature_grad = after(feature_grad, coming)
-                    feature_grad, dec_grad, squares[k, half] = backward_piece(
-                        jnp.stack([member ^ half, there[k]]),
-                        k,
-                        groups_of[half, k],
-                        turned_features,
-                        dec_weight,
-                        feature_grad,
-                        dec_grad,
-                    )
+                if k == 0 and number > 0:
+                    feature_grad = after(feature_grad, groups_of[rel, layers - 1][-1])
+                elif k > 0 and number + 1 < len(stages):
+                    coming = [groups_of[other, k - 1][-1] for other in stages[number + 1]]
+                    feature_grad = after(feature_grad, *coming)
+                feature_grad, dec_grad, squares[k, rel] = backward_pair(
+                    jnp.stack([member % 2, (member ^ rel) // 2, there[k]]),
+                    k,
+                    parts,
+                    [over_members(part, 0) for part in parts],
+                    turned_features,
+                    dec_weight,
+                    feature_grad,
+                    dec_grad,
+                )
     scale = (tok / loss_scale) ** 2 / (layers * tok * depth)
     enc_grad, bias_grad, mean_square = encoder_grad(
         jnp.stack([member ^ rel for rel in order]),

time: 136 us -> 134 us (0.985)
  starting transfers between devices: 57.4 us -> 44.4 us
  local copies, waits for them, and re-layouts: 2.87 us -> 14.9 us
  Pallas kernels: 48.1 us -> 36.1 us
  waiting for transfers between devices: 21.6 us -> 32.3 us
    pallas_call x12 -> x6, Pallas kernels: 36.9 us -> 24.7 us  [the longest x4 17.9 us: backward_pair(): pl.pallas_call(kernel, in_specs=[in_smem] + [in_vmem] * (len(inputs) + 1)...]
    unnamed x44 -> x74, local copies, waits for them, and re-layouts: 2.62 us -> 14.7 us
    ppermute x4, starting transfers between devices: 15.2 us -> 6.27 us  [to_layer(): moved = lax.ppermute(value, 'layer', pairs)]
    ppermute x34, waiting for transfers between devices: 6.04 us -> 10.9 us  [over_members(): return lax.ppermute(value, 'layer', pairs)]
    ppermute x9, starting transfers between devices: 15.4 us -> 11.9 us  [over_feat(): return lax.ppermute(value, 'feat', pairs)]
    ppermute x9, waiting for transfers between devices: 14.6 us -> 18 us  [over_feat(): return lax.ppermute(value, 'feat', pairs)]
    ppermute x4, waiting for transfers between devices: 0.91 us -> 3.33 us  [to_layer(): moved = lax.ppermute(value, 'layer', pairs)]
  transfers between devices with their start and end apart: 51 -> 51, of which waited for: 12 -> 20; matrix products, arithmetic and copies ran while one was open for 2% -> 3% of each run, Pallas kernels for 27% -> 16%
where the time goes in v2:
time: 134 us; the launch traced here: 133 us
  starting transfers between devices  44.4 us (33%)
  Pallas kernels  36.1 us (27%)
  waiting for transfers between devices  32.3 us (24%)
  local copies, waits for them, and re-layouts  14.9 us (11%)
  other arithmetic  4.17 us (3%)
  between operations  1.46 us (1%)
    ppermute x34, starting transfers between devices, over_members(): return lax.ppermute(value, 'layer', pairs)  21.6 us
    ppermute x9, waiting for transfers between devices, over_feat(): return lax.ppermute(value, 'feat', pairs)  18 us
    pallas_call x4, Pallas kernels, backward_pair(): pl.pallas_call(kernel, in_specs=[in_smem] + [in_vmem] * (len(inputs) + 1)...  17.9 us
    unnamed x74, local copies, waits for them, and re-layouts  14.7 us
    ppermute x9, starting transfers between devices, over_feat(): return lax.ppermute(value, 'feat', pairs)  11.9 us
    ppermute x34, waiting for transfers between devices, over_members(): return lax.ppermute(value, 'layer', pairs)  10.9 us
    pallas_call x2, Pallas kernels, decode(): pl.pallas_call(kernel, in_specs=[in_smem] + [in_vmem] * 2 + ([in_hbm] if...  6.8 us
    ppermute x4, starting transfers between devices, to_layer(): moved = lax.ppermute(value, 'layer', pairs)  6.27 us
  transfers between devices with their start and end apart: 51, of which 20 were waited for; matrix products, arithmetic and copies ran while one was open for 3% of the time, Pallas kernels for 16%

profile of v2, /device:TPU:0, one launch (start us, length us, event | category | flops | bytes accessed | tf_op | source)
XLA Modules:
  0.0 133.3 jit_solution(9646292781138474950)
XLA Ops:
  0.6 3.1 %collective-permute-start.1 = (bf16[128,512]{1,0:T(8,128)(2,1)}, bf16[128,512]{1,0:T(8,128)(2,1)S(1)}, u32[]{:S(2)}, u32[]{:S(2)}) collective-permute-start(bf16[128,512]{1,0:T(8,128)(2,1)} %param.5), channel_id=1, source_target_pairs={{0,1},{1,0},{2,3},{3,2},{4,5},{5,4},{6,7},{7,6},{8,9},{9,8},{10,11... | collective-permute-start | bytes 393224 | tf_op jit(solution)/shard_map/ppermute | solution.py:17
  3.7 2.5 %collective-permute-start.3 = (bf16[128,512]{1,0:T(8,128)(2,1)}, bf16[128,512]{1,0:T(8,128)(2,1)S(1)}, u32[]{:S(2)}, u32[]{:S(2)}) collective-permute-start(bf16[128,512]{1,0:T(8,128)(2,1)} %param.5), channel_id=1, source_target_pairs={{0,3},{1,2},{2,1},{3,0},{4,7},{5,6},{6,5},{7,4},{8,11},{9,10},{10,... | collective-permute-start | bytes 393224 | tf_op jit(solution)/shard_map/ppermute | solution.py:17
  6.3 1.5 %collective-permute-start = (bf16[128,512]{1,0:T(8,128)(2,1)}, bf16[128,512]{1,0:T(8,128)(2,1)S(1)}, u32[]{:S(2)}, u32[]{:S(2)}) collective-permute-start(bf16[128,512]{1,0:T(8,128)(2,1)} %param.5), channel_id=1, source_target_pairs={{0,8},{4,12},{8,0},{12,4},{16,24},{20,28},{24,16},{28,20},{1,9},{5... | collective-permute-start | bytes 393224 | tf_op jit(solution)/shard_map/ppermute | solution.py:23
  7.8 1.3 collective-permute-start.4
  9.1 4.6 %collective-permute-done.3 = bf16[128,512]{1,0:T(8,128)(2,1)S(1)} collective-permute-done((bf16[128,512]{1,0:T(8,128)(2,1)}, bf16[128,512]{1,0:T(8,128)(2,1)S(1)}, u32[]{:S(2)}, u32[]{:S(2)}) %collective-permute-start.3) | collective-permute-done | bytes 131104 | tf_op jit(solution)/shard_map/ppermute | solution.py:17
  13.7 4.5 %collective-permute-done.2 = bf16[128,512]{1,0:T(8,128)(2,1)S(1)} collective-permute-done((bf16[128,512]{1,0:T(8,128)(2,1)}, bf16[128,512]{1,0:T(8,128)(2,1)S(1)}, u32[]{:S(2)}, u32[]{:S(2)}) %collective-permute-start.2) | collective-permute-done | bytes 131104 | tf_op jit(solution)/shard_map/ppermute | solution.py:17
  18.2 1.0 pad_maximum_fusion.refs_0_
  19.3 1.6 %collective-permute-start.7 = (bf16[128,512]{1,0:T(8,128)(2,1)S(1)}, bf16[128,512]{1,0:T(8,128)(2,1)S(1)}, u32[]{:S(2)}, u32[]{:S(2)}) collective-permute-start(bf16[128,512]{1,0:T(8,128)(2,1)S(1)} %collective-permute-done.3), channel_id=1, source_target_pairs={{0,8},{4,12},{8,0},{12,4},{16,24},{20,28},{24,16},{28,20},{1,9},{5... | collective-permute-start | bytes 393224 | tf_op jit(solution)/shard_map/ppermute | solution.py:23
  21.5 4.1 %encode_first.1 = (f32[512,1024]{1,0:T(8,128)S(1)}, bf16[2,512,1024]{2,1,0:T(8,128)(2,1)S(1)}, bf16[1024,2048]{1,0:T(8,128)(2,1)S(1)}) custom-call(s32[4]{0:T(128)S(1)} %pad_add_fusion.index_ref, bf16[4,128,512]{2,1,0:T(8,128)(2,1)S(1)} %pad_maximum_fusion.refs_0_, bf16[4,128,512]{2,1,0:T(8,128)(2,1)S(1)} %collective-permute-done.5.refs_1_, ...), custom_call_target="tpu_custom_call" | custom-call | flops 1073741824 | bytes 8388608 | tf_op jit(solution)/shard_map/encode_first/pallas_call | solution.py:109
  25.7 2.3 %collective-permute-done.6 = bf16[128,512]{1,0:T(8,128)(2,1)S(1)} collective-permute-done((bf16[128,512]{1,0:T(8,128)(2,1)S(1)}, bf16[128,512]{1,0:T(8,128)(2,1)S(1)}, u32[]{:S(2)}, u32[]{:S(2)}) %collective-permute-start.6) | collective-permute-done | bytes 131104 | tf_op jit(solution)/shard_map/ppermute | solution.py:23
  28.1 0.7 encode_next.2.partial_ref
  28.9 1.2 collective-permute-done.8.piece_ref
  30.0 0.9 encode_next.3.feat_ref.refs_4_
  30.9 4.5 %decode.2 = (bf16[2,2,128,512]{3,2,1,0:T(8,128)(2,1)S(1)}, bf16[2,1,128,512]{3,2,1,0:T(8,128)(2,1)S(1)}, bf16[2,1,128,512]{3,2,1,0:T(8,128)(2,1)}, bf16[2,2,128,...) custom-call(s32[1]{0:T(128)} %bitcast.member_ref, ...), custom_call_target="tpu_custom_call" | custom-call | flops 2147483648 | bytes 4194304 | tf_op jit(solution)/shard_map/decode/pallas_call | solution.py:199
  35.4 0.8 copy-done.6
  36.2 0.7 copy-done.16
  36.9 2.0 %copy-done.32 = bf16[1024,2048]{1,0:T(8,128)(2,1)} copy-done((bf16[1024,2048]{1,0:T(8,128)(2,1)}, bf16[1024,2048]{1,0:T(8,128)(2,1)S(1)}, u32[]{:S(2)}) %copy-start.32) | copy-done | bytes 4194328
  38.9 0.8 copy-done.34
  40.5 1.2 collective-permute-done.9
  41.7 1.1 add_convert_fusion.5
  42.8 2.2 %copy-done.33 = bf16[1024,2048]{1,0:T(8,128)(2,1)S(1)} copy-done((bf16[1024,2048]{1,0:T(8,128)(2,1)S(1)}, bf16[1024,2048]{1,0:T(8,128)(2,1)}, u32[]{:S(2)}) %copy-start.33) | copy-done | bytes 4194328
  45.0 2.4 %decode.3 = (bf16[2,2,128,512]{3,2,1,0:T(8,128)(2,1)S(1)}, bf16[2,1,128,512]{3,2,1,0:T(8,128)(2,1)S(1)}, bf16[2,1,128,512]{3,2,1,0:T(8,128)(2,1)S(1)}, bf16[2,2,...) custom-call(s32[1]{0:T(128)} %bitcast.member_ref, ...), custom_call_target="tpu_custom_call" | custom-call | flops 2147483648 | bytes 4194304 | tf_op jit(solution)/shard_map/decode/pallas_call | solution.py:199
  47.9 1.6 %collective-permute-start.15 = (bf16[1,1,128,512]{3,2,1,0:T(8,128)(2,1)S(1)}, bf16[1,1,128,512]{3,2,1,0:T(8,128)(2,1)S(1)}, u32[]{:S(2)}, u32[]{:S(2)}) collective-permute-start(bf16[1,1,128,512]{3,2,1,0:T(8,128)(2,1)S(1)} %slice_bitcast_fusion.10), channel_id=1, source_target_pairs={{0,8},{4,12},{8,0},{12,4},{16,24},{20,28},{24,16},{28,20},{1,9},{5... | collective-permute-start | bytes 393224 | tf_op jit(solution)/shard_map/ppermute | solution.py:23
  49.9 0.7 collective-permute-start.18
  50.6 1.5 %collective-permute-start.13 = (bf16[1,2,128,512]{3,2,1,0:T(8,128)(2,1)S(1)}, bf16[1,2,128,512]{3,2,1,0:T(8,128)(2,1)S(1)}, u32[]{:S(2)}, u32[]{:S(2)}) collective-permute-start(bf16[1,2,128,512]{3,2,1,0:T(8,128)(2,1)S(1)} %get-tuple-element.87), channel_id=1, source_target_pairs={{0,16},{4,20},{8,24},{12,28},{16,0},{20,4},{24,8},{28,12},{1,17},{... | collective-permute-start | bytes 786440 | tf_op jit(solution)/shard_map/ppermute | solution.py:29
  52.1 1.8 %collective-permute-done.15 = bf16[1,1,128,512]{3,2,1,0:T(8,128)(2,1)S(1)} collective-permute-done((bf16[1,1,128,512]{3,2,1,0:T(8,128)(2,1)S(1)}, bf16[1,1,128,512]{3,2,1,0:T(8,128)(2,1)S(1)}, u32[]{:S(2)}, u32[]{:S(2)}) %collective-permute-start.15) | collective-permute-done | bytes 131104 | tf_op jit(solution)/shard_map/ppermute | solution.py:23
  54.0 1.9 %collective-permute-start.16 = (bf16[1,1,128,512]{3,2,1,0:T(8,128)(2,1)S(1)}, bf16[1,1,128,512]{3,2,1,0:T(8,128)(2,1)S(1)}, u32[]{:S(2)}, u32[]{:S(2)}) collective-permute-start(bf16[1,1,128,512]{3,2,1,0:T(8,128)(2,1)S(1)} %slice_bitcast_fusion.11), channel_id=1, source_target_pairs={{0,8},{4,12},{8,0},{12,4},{16,24},{20,28},{24,16},{28,20},{1,9},{5... | collective-permute-start | bytes 393224 | tf_op jit(solution)/shard_map/ppermute | solution.py:23
  56.0 1.6 %collective-permute-start.20 = (bf16[1,1,128,512]{3,2,1,0:T(8,128)(2,1)S(1)}, bf16[1,1,128,512]{3,2,1,0:T(8,128)(2,1)S(1)}, u32[]{:S(2)}, u32[]{:S(2)}) collective-permute-start(bf16[1,1,128,512]{3,2,1,0:T(8,128)(2,1)S(1)} %fusion.13), channel_id=1, source_target_pairs={{0,16},{4,20},{8,24},{12,28},{16,0},{20,4},{24,8},{28,12},{1,17},{... | collective-permute-start | bytes 393224 | tf_op jit(solution)/shard_map/ppermute | solution.py:29
  57.6 1.1 collective-permute-start.21
  58.6 1.0 collective-permute-done.16
  59.7 1.6 %collective-permute-start.22 = (bf16[1,1,128,512]{3,2,1,0:T(8,128)(2,1)S(1)}, bf16[1,1,128,512]{3,2,1,0:T(8,128)(2,1)S(1)}, u32[]{:S(2)}, u32[]{:S(2)}) collective-permute-start(bf16[1,1,128,512]{3,2,1,0:T(8,128)(2,1)S(1)} %fusion.10), channel_id=1, source_target_pairs={{0,16},{4,20},{8,24},{12,28},{16,0},{20,4},{24,8},{28,12},{1,17},{... | collective-permute-start | bytes 393224 | tf_op jit(solution)/shard_map/ppermute | solution.py:29
  61.3 1.3 collective-permute-done.20
  62.9 1.5 %collective-permute-start.19 = (bf16[1,2,128,512]{3,2,1,0:T(8,128)(2,1)S(1)}, bf16[1,2,128,512]{3,2,1,0:T(8,128)(2,1)S(1)}, u32[]{:S(2)}, u32[]{:S(2)}) collective-permute-start(bf16[1,2,128,512]{3,2,1,0:T(8,128)(2,1)S(1)} %fusion.2), channel_id=1, source_target_pairs={{0,8},{4,12},{8,0},{12,4},{16,24},{20,28},{24,16},{28,20},{1,9},{5... | collective-permute-start | bytes 786440 | tf_op jit(solution)/shard_map/ppermute | solution.py:23
  64.8 1.6 %collective-permute-start.23 = (bf16[1,2,128,512]{3,2,1,0:T(8,128)(2,1)S(1)}, bf16[1,2,128,512]{3,2,1,0:T(8,128)(2,1)S(1)}, u32[]{:S(2)}, u32[]{:S(2)}) collective-permute-start(bf16[1,2,128,512]{3,2,1,0:T(8,128)(2,1)S(1)} %get-tuple-element.99), channel_id=1, source_target_pairs={{0,16},{4,20},{8,24},{12,28},{16,0},{20,4},{24,8},{28,12},{1,17},{... | collective-permute-start | bytes 786440 | tf_op jit(solution)/shard_map/ppermute | solution.py:29
  66.4 2.6 %collective-permute-start.24 = (bf16[128,512]{1,0:T(8,128)(2,1)S(1)}, bf16[128,512]{1,0:T(8,128)(2,1)S(1)}, u32[]{:S(2)}, u32[]{:S(2)}) collective-permute-start(bf16[128,512]{1,0:T(8,128)(2,1)S(1)} %fusion.16), channel_id=1, source_target_pairs={{0,3},{1,2},{2,1},{3,0},{4,7},{5,6},{6,5},{7,4},{8,11},{9,10},{10,... | collective-permute-start | bytes 393224 | tf_op jit(solution)/shard_map/ppermute | solution.py:17
  69.0 0.7 collective-permute-done.19
  69.7 1.6 %collective-permute-done.23 = bf16[1,2,128,512]{3,2,1,0:T(8,128)(2,1)S(1)} collective-permute-done((bf16[1,2,128,512]{3,2,1,0:T(8,128)(2,1)S(1)}, bf16[1,2,128,512]{3,2,1,0:T(8,128)(2,1)S(1)}, u32[]{:S(2)}, u32[]{:S(2)}) %collective-permute-start.23) | collective-permute-done | bytes 262176 | tf_op jit(solution)/shard_map/ppermute | solution.py:29
  72.8 0.8 copy-done.14
  74.0 4.6 %collective-permute-done.25 = bf16[128,512]{1,0:T(8,128)(2,1)S(1)} collective-permute-done((bf16[128,512]{1,0:T(8,128)(2,1)S(1)}, bf16[128,512]{1,0:T(8,128)(2,1)S(1)}, u32[]{:S(2)}, u32[]{:S(2)}) %collective-permute-start.25) | collective-permute-done | bytes 131104 | tf_op jit(solution)/shard_map/ppermute | solution.py:17
  78.6 0.8 multiply_convert_fusion
  79.4 1.4 %collective-permute-start.27 = (bf16[1,128,512]{2,1,0:T(8,128)(2,1)S(1)}, bf16[1,128,512]{2,1,0:T(8,128)(2,1)}, u32[]{:S(2)}, u32[]{:S(2)}) collective-permute-start(bf16[1,128,512]{2,1,0:T(8,128)(2,1)S(1)} %bitcast.118), channel_id=1, source_target_pairs={{0,16},{4,20},{8,24},{12,28},{16,0},{20,4},{24,8},{28,12},{1,17},{... | collective-permute-start | bytes 393224 | tf_op jit(solution)/shard_map/ppermute | solution.py:37
  80.8 2.5 %collective-permute-start.34 = (bf16[128,512]{1,0:T(8,128)(2,1)S(1)}, bf16[128,512]{1,0:T(8,128)(2,1)S(1)}, u32[]{:S(2)}, u32[]{:S(2)}) collective-permute-start(bf16[128,512]{1,0:T(8,128)(2,1)S(1)} %get-tuple-element.133), channel_id=1, source_target_pairs={{0,3},{1,2},{2,1},{3,0},{4,7},{5,6},{6,5},{7,4},{8,11},{9,10},{10,... | collective-permute-start | bytes 393224 | tf_op jit(solution)/shard_map/ppermute | solution.py:17
  83.4 0.9 collective-permute-start.33
  84.3 1.8 %collective-permute-start.29 = (bf16[1,128,512]{2,1,0:T(8,128)(2,1)S(1)}, bf16[1,128,512]{2,1,0:T(8,128)(2,1)S(1)}, u32[]{:S(2)}, u32[]{:S(2)}) collective-permute-start(bf16[1,128,512]{2,1,0:T(8,128)(2,1)S(1)} %bitcast.119), channel_id=1, source_target_pairs={{0,8},{4,12},{8,0},{12,4},{16,24},{20,28},{24,16},{28,20},{1,9},{5... | collective-permute-start | bytes 393224 | tf_op jit(solution)/shard_map/ppermute | solution.py:23
  86.4 1.1 collective-permute-start.31
  87.5 1.0 collective-permute-start.32
  88.5 1.3 collective-permute-start.28
  89.8 3.6 %collective-permute-done.33 = bf16[128,512]{1,0:T(8,128)(2,1)S(1)} collective-permute-done((bf16[128,512]{1,0:T(8,128)(2,1)S(1)}, bf16[128,512]{1,0:T(8,128)(2,1)S(1)}, u32[]{:S(2)}, u32[]{:S(2)}) %collective-permute-start.33) | collective-permute-done | bytes 131104 | tf_op jit(solution)/shard_map/ppermute | solution.py:17
  93.6 1.6 %collective-permute-start.38 = (bf16[2,128,512]{2,1,0:T(8,128)(2,1)S(1)}, bf16[2,128,512]{2,1,0:T(8,128)(2,1)}, u32[]{:S(2)}, u32[]{:S(2)}) collective-permute-start(bf16[2,128,512]{2,1,0:T(8,128)(2,1)S(1)} %pad_maximum_fusion.2.refs_2_), channel_id=1, source_target_pairs={{0,16},{4,20},{8,24},{12,28},{16,0},{20,4},{24,8},{28,12},{1,17},{... | collective-permute-start | bytes 786440 | tf_op jit(solution)/shard_map/ppermute | solution.py:37
  95.7 1.1 collective-permute-start.42
  97.6 0.7 copy-done.17
  98.9 0.9 copy-done.18
  99.9 0.9 copy-done.24
  100.8 0.9 copy-done.26
  101.7 0.9 copy-done.28
  102.6 4.1 %backward_pair.4 = (f32[512,1024]{1,0:T(8,128)S(1)}, bf16[2,1024,2048]{2,1,0:T(8,128)(2,1)}, f32[8,128]{1,0:T(8,128)S(1)}) custom-call(s32[3]{0:T(128)S(1)} %pad_add_fusion.5.info_ref, bf16[1,128,512]{2,1,0:T(8,128)(2,1)S(1)} %bitcast.121, bf16[1,128,512]{2,1,0:T(8,128)(2,1)S(1)} %bitcast.125, bf16[2,128,512]{2,1,0:T(8,128)(2,1)S(1)} %pad_maximum_fusion.2.refs_2_, ...), custom_call_target="tpu_custom_call" | custom-call | flops 262144 | bytes 262144 | tf_op jit(solution)/shard_map/backward_pair/pallas_call | solution.py:311
  107.9 0.7 collective-permute-done.39.refs_3_
  109.3 0.9 copy-done.30
  110.2 4.3 %backward_pair.5 = (f32[512,1024]{1,0:T(8,128)S(1)}, bf16[2,1024,2048]{2,1,0:T(8,128)(2,1)}, f32[8,128]{1,0:T(8,128)S(1)}) custom-call(s32[3]{0:T(128)S(1)} %pad_add_fusion.3.info_ref, bf16[1,128,512]{2,1,0:T(8,128)(2,1)} %collective-permute-done.27.refs_0_, ...), custom_call_target="tpu_custom_call", output_to_operand_aliasing={{0}: (9, {}), {1}: (10, {})} | custom-call | flops 262144 | bytes 262144 | tf_op jit(solution)/shard_map/backward_pair/pallas_call | solution.py:311
  115.3 1.0 collective-permute-start.47
  116.9 5.2 %backward_pair.6 = (f32[512,1024]{1,0:T(8,128)S(1)}, bf16[2,1024,2048]{2,1,0:T(8,128)(2,1)}, f32[8,128]{1,0:T(8,128)S(1)}) custom-call(s32[3]{0:T(128)S(1)} %pad_add_fusion.6.info_ref, bf16[1,128,512]{2,1,0:T(8,128)(2,1)S(1)} %copy-done.22, bf16[1,128,512]{2,1,0:T(8,128)(2,1)} %collective-permute-done.32.refs_1_, ...), custom_call_target="tpu_custom_call", output_to_operand_aliasing={{0}: (9, {}), {1}: (10, {})} | custom-call | flops 262144 | bytes 262144 | tf_op jit(solution)/shard_map/backward_pair/pallas_call | solution.py:311
  122.9 1.0 collective-permute-done.48.refs_3_
  124.1 4.2 %backward_pair.7 = (f32[512,1024]{1,0:T(8,128)S(1)}, bf16[2,1024,2048]{2,1,0:T(8,128)(2,1)}, f32[8,128]{1,0:T(8,128)S(1)}) custom-call(s32[3]{0:T(128)S(1)} %pad_add_fusion.4.info_ref, bf16[1,128,512]{2,1,0:T(8,128)(2,1)S(1)} %copy-done.20, bf16[1,128,512]{2,1,0:T(8,128)(2,1)S(1)} %collective-permute-done.47.refs_1_, ...), custom_call_target="tpu_custom_call", output_to_operand_aliasing={{0}: (9, {}), {1}: (10, {})} | custom-call | flops 262144 | bytes 262144 | tf_op jit(solution)/shard_map/backward_pair/pallas_call | solution.py:311
  128.4 4.7 %encoder_grad.1 = (bf16[2048,1024]{1,0:T(8,128)(2,1)}, f32[1,1024]{1,0:T(1,128)}, f32[1,1]{1,0:T(1,128)}) custom-call(s32[4]{0:T(128)S(1)} %pad_add_fusion.index_ref, bf16[1,512,512]{2,1,0:T(8,128)(2,1)S(1)} %copy-done.9, bf16[1,512,512]{2,1,0:T(8,128)(2,1)S(1)} %copy-done.11, bf16[1,512,512]{2,1,0:T(8,128)(2,1)S(1)} %copy-done.13, ...), custom_call_target="tpu_custom_call" | custom-call | flops 2147483648 | bytes 9437184 | tf_op jit(solution)/shard_map/encoder_grad/pallas_call | solution.py:365
  (155 shorter events, 11.9 us)
Async XLA Ops:
  0.6 7.2 %collective-permute-start.1 = (bf16[128,512]{1,0:T(8,128)(2,1)}, bf16[128,512]{1,0:T(8,128)(2,1)S(1)}, u32[]{:S(2)}, u32[]{:S(2)}) collective-permute-start(bf16[128,512]{1,0:T(8,128)(2,1)} %param.5), channel_id=1, source_target_pairs={{0,1},{1,0},{2,3},{3,2},{4,5},{5,4},{6,7},{7,6},{8,9},{9,8},{10,11... | collective-permute-start | bytes 393224 | tf_op jit(solution)/shard_map/ppermute | solution.py:17
  3.7 10.0 %collective-permute-start.3 = (bf16[128,512]{1,0:T(8,128)(2,1)}, bf16[128,512]{1,0:T(8,128)(2,1)S(1)}, u32[]{:S(2)}, u32[]{:S(2)}) collective-permute-start(bf16[128,512]{1,0:T(8,128)(2,1)} %param.5), channel_id=1, source_target_pairs={{0,3},{1,2},{2,1},{3,0},{4,7},{5,6},{6,5},{7,4},{8,11},{9,10},{10,... | collective-permute-start | bytes 393224 | tf_op jit(solution)/shard_map/ppermute | solution.py:17
  6.2 12.0 %collective-permute-start.2 = (bf16[128,512]{1,0:T(8,128)(2,1)}, bf16[128,512]{1,0:T(8,128)(2,1)S(1)}, u32[]{:S(2)}, u32[]{:S(2)}) collective-permute-start(bf16[128,512]{1,0:T(8,128)(2,1)} %param.5), channel_id=1, source_target_pairs={{0,2},{1,3},{2,0},{3,1},{4,6},{5,7},{6,4},{7,5},{8,10},{9,11},{10,... | collective-permute-start | bytes 393224 | tf_op jit(solution)/shard_map/ppermute | solution.py:17
  6.3 12.9 %collective-permute-start = (bf16[128,512]{1,0:T(8,128)(2,1)}, bf16[128,512]{1,0:T(8,128)(2,1)S(1)}, u32[]{:S(2)}, u32[]{:S(2)}) collective-permute-start(bf16[128,512]{1,0:T(8,128)(2,1)} %param.5), channel_id=1, source_target_pairs={{0,8},{4,12},{8,0},{12,4},{16,24},{20,28},{24,16},{28,20},{1,9},{5... | collective-permute-start | bytes 393224 | tf_op jit(solution)/shard_map/ppermute | solution.py:23
  7.8 11.4 %collective-permute-start.4 = (bf16[128,512]{1,0:T(8,128)(2,1)S(1)}, bf16[128,512]{1,0:T(8,128)(2,1)S(1)}, u32[]{:S(2)}, u32[]{:S(2)}) collective-permute-start(bf16[128,512]{1,0:T(8,128)(2,1)S(1)} %collective-permute-done.1), channel_id=1, source_target_pairs={{0,8},{4,12},{8,0},{12,4},{16,24},{20,28},{24,16},{28,20},{1,9},{5... | collective-permute-start | bytes 393224 | tf_op jit(solution)/shard_map/ppermute | solution.py:23
  19.2 2.3 %collective-permute-start.5 = (bf16[4,128,512]{2,1,0:T(8,128)(2,1)S(1)}, bf16[4,128,512]{2,1,0:T(8,128)(2,1)S(1)}, u32[]{:S(2)}, u32[]{:S(2)}) collective-permute-start(bf16[4,128,512]{2,1,0:T(8,128)(2,1)S(1)} %pad_maximum_fusion.refs_0_), channel_id=1, source_target_pairs={{0,4},{4,0},{8,12},{12,8},{16,20},{20,16},{24,28},{28,24},{1,5},{5... | collective-permute-start | bytes 1572872 | tf_op jit(solution)/shard_map/ppermute | solution.py:23
  19.3 6.4 %collective-permute-start.7 = (bf16[128,512]{1,0:T(8,128)(2,1)S(1)}, bf16[128,512]{1,0:T(8,128)(2,1)S(1)}, u32[]{:S(2)}, u32[]{:S(2)}) collective-permute-start(bf16[128,512]{1,0:T(8,128)(2,1)S(1)} %collective-permute-done.3), channel_id=1, source_target_pairs={{0,8},{4,12},{8,0},{12,4},{16,24},{20,28},{24,16},{28,20},{1,9},{5... | collective-permute-start | bytes 393224 | tf_op jit(solution)/shard_map/ppermute | solution.py:23
  20.8 7.1 %collective-permute-start.6 = (bf16[128,512]{1,0:T(8,128)(2,1)S(1)}, bf16[128,512]{1,0:T(8,128)(2,1)S(1)}, u32[]{:S(2)}, u32[]{:S(2)}) collective-permute-start(bf16[128,512]{1,0:T(8,128)(2,1)S(1)} %collective-permute-done.2), channel_id=1, source_target_pairs={{0,8},{4,12},{8,0},{12,4},{16,24},{20,28},{24,16},{28,20},{1,9},{5... | collective-permute-start | bytes 393224 | tf_op jit(solution)/shard_map/ppermute | solution.py:23
  25.6 4.4 %copy-start.31 = (f32[1024]{0:T(1024)S(1)}, f32[1024]{0:T(1024)}, u32[]{:S(2)}) copy-start(f32[1024]{0:T(1024)} %param.8) | copy-start | bytes 12292
  28.1 2.0 %collective-permute-start.8 = (bf16[4,128,512]{2,1,0:T(8,128)(2,1)S(1)}, bf16[4,128,512]{2,1,0:T(8,128)(2,1)S(1)}, u32[]{:S(2)}, u32[]{:S(2)}) collective-permute-start(bf16[4,128,512]{2,1,0:T(8,128)(2,1)S(1)} %pad_maximum_fusion.1.piece_ref), channel_id=1, source_target_pairs={{0,4},{4,0},{8,12},{12,8},{16,20},{20,16},{24,28},{28,24},{1,5},{5... | collective-permute-start | bytes 1572872 | tf_op jit(solution)/shard_map/ppermute | solution.py:23
  30.9 40.6 %copy-start = (bf16[2,512,1024]{2,1,0:T(8,128)(2,1)}, bf16[2,512,1024]{2,1,0:T(8,128)(2,1)S(1)}, u32[]{:S(2)}) copy-start(bf16[2,512,1024]{2,1,0:T(8,128)(2,1)S(1)} %encode_next.3.feat_ref.refs_4_) | copy-start | bytes 6291460
  39.8 1.9 %collective-permute-start.9 = (bf16[2,1,128,512]{3,2,0,1:T(8,128)(2,1)}, bf16[2,1,128,512]{3,2,0,1:T(8,128)(2,1)}, u32[]{:S(2)}, u32[]{:S(2)}) collective-permute-start(bf16[2,1,128,512]{3,2,0,1:T(8,128)(2,1)} %bitcast.14), channel_id=1, source_target_pairs={{0,4},{4,0},{8,12},{12,8},{16,20},{20,16},{24,28},{28,24},{1,5},{5... | collective-permute-start | bytes 786440 | tf_op jit(solution)/shard_map/ppermute | solution.py:23
  40.0 9.6 %collective-permute-start.11 = (bf16[2,2,128,512]{3,2,1,0:T(8,128)(2,1)}, bf16[2,2,128,512]{3,2,1,0:T(8,128)(2,1)S(1)}, u32[]{:S(2)}, u32[]{:S(2)}) collective-permute-start(bf16[2,2,128,512]{3,2,1,0:T(8,128)(2,1)} %copy-done.34), channel_id=1, source_target_pairs={{0,4},{4,0},{8,12},{12,8},{16,20},{20,16},{24,28},{28,24},{1,5},{5... | collective-permute-start | bytes 1572872 | tf_op jit(solution)/shard_map/ppermute | solution.py:23
  40.3 9.2 %collective-permute-start.14 = (bf16[2,1,128,512]{3,2,0,1:T(8,128)(2,1)}, bf16[2,1,128,512]{3,2,0,1:T(8,128)(2,1)S(1)}, u32[]{:S(2)}, u32[]{:S(2)}) collective-permute-start(bf16[2,1,128,512]{3,2,0,1:T(8,128)(2,1)} %bitcast.128), channel_id=1, source_target_pairs={{0,4},{4,0},{8,12},{12,8},{16,20},{20,16},{24,28},{28,24},{1,5},{5... | collective-permute-start | bytes 786440 | tf_op jit(solution)/shard_map/ppermute | solution.py:23
  45.0 4.6 %copy-start.7 = (bf16[2,2,128,512]{3,2,1,0:T(8,128)(2,1)S(1)}, bf16[2,2,128,512]{3,2,1,0:T(8,128)(2,1)}, u32[]{:S(2)}) copy-start(bf16[2,2,128,512]{3,2,1,0:T(8,128)(2,1)} %copy-done.6) | copy-start | bytes 1572868
  47.3 2.5 %collective-permute-start.12 = (bf16[2,1,128,512]{3,2,0,1:T(8,128)(2,1)S(1)}, bf16[2,1,128,512]{3,2,0,1:T(8,128)(2,1)S(1)}, u32[]{:S(2)}, u32[]{:S(2)}) collective-permute-start(bf16[2,1,128,512]{3,2,0,1:T(8,128)(2,1)S(1)} %bitcast.129), channel_id=1, source_target_pairs={{0,4},{4,0},{8,12},{12,8},{16,20},{20,16},{24,28},{28,24},{1,5},{5... | collective-permute-start | bytes 786440 | tf_op jit(solution)/shard_map/ppermute | solution.py:23
  47.6 15.1 %collective-permute-start.10 = (bf16[2,2,128,512]{3,2,1,0:T(8,128)(2,1)S(1)}, bf16[2,2,128,512]{3,2,1,0:T(8,128)(2,1)S(1)}, u32[]{:S(2)}, u32[]{:S(2)}) collective-permute-start(bf16[2,2,128,512]{3,2,1,0:T(8,128)(2,1)S(1)} %get-tuple-element.82), channel_id=1, source_target_pairs={{0,4},{4,0},{8,12},{12,8},{16,20},{20,16},{24,28},{28,24},{1,5},{5... | collective-permute-start | bytes 1572872 | tf_op jit(solution)/shard_map/ppermute | solution.py:23
  47.9 6.0 %collective-permute-start.15 = (bf16[1,1,128,512]{3,2,1,0:T(8,128)(2,1)S(1)}, bf16[1,1,128,512]{3,2,1,0:T(8,128)(2,1)S(1)}, u32[]{:S(2)}, u32[]{:S(2)}) collective-permute-start(bf16[1,1,128,512]{3,2,1,0:T(8,128)(2,1)S(1)} %slice_bitcast_fusion.10), channel_id=1, source_target_pairs={{0,8},{4,12},{8,0},{12,4},{16,24},{20,28},{24,16},{28,20},{1,9},{5... | collective-permute-start | bytes 393224 | tf_op jit(solution)/shard_map/ppermute | solution.py:23
  49.5 6.4 %collective-permute-start.17 = (bf16[2,1,128,512]{3,2,0,1:T(8,128)(2,1)S(1)}, bf16[2,1,128,512]{3,2,0,1:T(8,128)(2,1)S(1)}, u32[]{:S(2)}, u32[]{:S(2)}) collective-permute-start(bf16[2,1,128,512]{3,2,0,1:T(8,128)(2,1)S(1)} %bitcast.127), channel_id=1, source_target_pairs={{0,4},{4,0},{8,12},{12,8},{16,20},{20,16},{24,28},{28,24},{1,5},{5... | collective-permute-start | bytes 786440 | tf_op jit(solution)/shard_map/ppermute | solution.py:23
  49.9 7.7 %collective-permute-start.18 = (bf16[1,1,128,512]{3,2,1,0:T(8,128)(2,1)S(1)}, bf16[1,1,128,512]{3,2,1,0:T(8,128)(2,1)S(1)}, u32[]{:S(2)}, u32[]{:S(2)}) collective-permute-start(bf16[1,1,128,512]{3,2,1,0:T(8,128)(2,1)S(1)} %slice_bitcast_fusion.12), channel_id=1, source_target_pairs={{0,8},{4,12},{8,0},{12,4},{16,24},{20,28},{24,16},{28,20},{1,9},{5... | collective-permute-start | bytes 393224 | tf_op jit(solution)/shard_map/ppermute | solution.py:23
  50.6 12.2 %collective-permute-start.13 = (bf16[1,2,128,512]{3,2,1,0:T(8,128)(2,1)S(1)}, bf16[1,2,128,512]{3,2,1,0:T(8,128)(2,1)S(1)}, u32[]{:S(2)}, u32[]{:S(2)}) collective-permute-start(bf16[1,2,128,512]{3,2,1,0:T(8,128)(2,1)S(1)} %get-tuple-element.87), channel_id=1, source_target_pairs={{0,16},{4,20},{8,24},{12,28},{16,0},{20,4},{24,8},{28,12},{1,17},{... | collective-permute-start | bytes 786440 | tf_op jit(solution)/shard_map/ppermute | solution.py:29
  54.0 5.7 %collective-permute-start.16 = (bf16[1,1,128,512]{3,2,1,0:T(8,128)(2,1)S(1)}, bf16[1,1,128,512]{3,2,1,0:T(8,128)(2,1)S(1)}, u32[]{:S(2)}, u32[]{:S(2)}) collective-permute-start(bf16[1,1,128,512]{3,2,1,0:T(8,128)(2,1)S(1)} %slice_bitcast_fusion.11), channel_id=1, source_target_pairs={{0,8},{4,12},{8,0},{12,4},{16,24},{20,28},{24,16},{28,20},{1,9},{5... | collective-permute-start | bytes 393224 | tf_op jit(solution)/shard_map/ppermute | solution.py:23
  56.0 6.6 %collective-permute-start.20 = (bf16[1,1,128,512]{3,2,1,0:T(8,128)(2,1)S(1)}, bf16[1,1,128,512]{3,2,1,0:T(8,128)(2,1)S(1)}, u32[]{:S(2)}, u32[]{:S(2)}) collective-permute-start(bf16[1,1,128,512]{3,2,1,0:T(8,128)(2,1)S(1)} %fusion.13), channel_id=1, source_target_pairs={{0,16},{4,20},{8,24},{12,28},{16,0},{20,4},{24,8},{28,12},{1,17},{... | collective-permute-start | bytes 393224 | tf_op jit(solution)/shard_map/ppermute | solution.py:29
  57.6 6.8 %collective-permute-start.21 = (bf16[1,1,128,512]{3,2,1,0:T(8,128)(2,1)S(1)}, bf16[1,1,128,512]{3,2,1,0:T(8,128)(2,1)S(1)}, u32[]{:S(2)}, u32[]{:S(2)}) collective-permute-start(bf16[1,1,128,512]{3,2,1,0:T(8,128)(2,1)S(1)} %slice_bitcast_fusion.9), channel_id=1, source_target_pairs={{0,8},{4,12},{8,0},{12,4},{16,24},{20,28},{24,16},{28,20},{1,9},{5... | collective-permute-start | bytes 393224 | tf_op jit(solution)/shard_map/ppermute | solution.py:23
  59.7 5.0 %collective-permute-start.22 = (bf16[1,1,128,512]{3,2,1,0:T(8,128)(2,1)S(1)}, bf16[1,1,128,512]{3,2,1,0:T(8,128)(2,1)S(1)}, u32[]{:S(2)}, u32[]{:S(2)}) collective-permute-start(bf16[1,1,128,512]{3,2,1,0:T(8,128)(2,1)S(1)} %fusion.10), channel_id=1, source_target_pairs={{0,16},{4,20},{8,24},{12,28},{16,0},{20,4},{24,8},{28,12},{1,17},{... | collective-permute-start | bytes 393224 | tf_op jit(solution)/shard_map/ppermute | solution.py:29
  62.8 9.4 %copy-start.5 = (bf16[4,128,512]{2,1,0:T(8,128)(2,1)S(1)}, bf16[4,128,512]{2,1,0:T(8,128)(2,1)}, u32[]{:S(2)}) copy-start(bf16[4,128,512]{2,1,0:T(8,128)(2,1)} %copy-done.4) | copy-start | bytes 1572868
  62.9 6.8 %collective-permute-start.19 = (bf16[1,2,128,512]{3,2,1,0:T(8,128)(2,1)S(1)}, bf16[1,2,128,512]{3,2,1,0:T(8,128)(2,1)S(1)}, u32[]{:S(2)}, u32[]{:S(2)}) collective-permute-start(bf16[1,2,128,512]{3,2,1,0:T(8,128)(2,1)S(1)} %fusion.2), channel_id=1, source_target_pairs={{0,8},{4,12},{8,0},{12,4},{16,24},{20,28},{24,16},{28,20},{1,9},{5... | collective-permute-start | bytes 786440 | tf_op jit(solution)/shard_map/ppermute | solution.py:23
  64.8 7.8 %copy-start.3 = (bf16[4,128,512]{2,1,0:T(8,128)(2,1)S(1)}, bf16[4,128,512]{2,1,0:T(8,128)(2,1)}, u32[]{:S(2)}) copy-start(bf16[4,128,512]{2,1,0:T(8,128)(2,1)} %copy-done.2) | copy-start | bytes 1572868
  64.8 6.5 %collective-permute-start.23 = (bf16[1,2,128,512]{3,2,1,0:T(8,128)(2,1)S(1)}, bf16[1,2,128,512]{3,2,1,0:T(8,128)(2,1)S(1)}, u32[]{:S(2)}, u32[]{:S(2)}) collective-permute-start(bf16[1,2,128,512]{3,2,1,0:T(8,128)(2,1)S(1)} %get-tuple-element.99), channel_id=1, source_target_pairs={{0,16},{4,20},{8,24},{12,28},{16,0},{20,4},{24,8},{28,12},{1,17},{... | collective-permute-start | bytes 786440 | tf_op jit(solution)/shard_map/ppermute | solution.py:29
  66.4 7.6 %collective-permute-start.24 = (bf16[128,512]{1,0:T(8,128)(2,1)S(1)}, bf16[128,512]{1,0:T(8,128)(2,1)S(1)}, u32[]{:S(2)}, u32[]{:S(2)}) collective-permute-start(bf16[128,512]{1,0:T(8,128)(2,1)S(1)} %fusion.16), channel_id=1, source_target_pairs={{0,3},{1,2},{2,1},{3,0},{4,7},{5,6},{6,5},{7,4},{8,11},{9,10},{10,... | collective-permute-start | bytes 393224 | tf_op jit(solution)/shard_map/ppermute | solution.py:17
  69.0 9.6 %collective-permute-start.25 = (bf16[128,512]{1,0:T(8,128)(2,1)S(1)}, bf16[128,512]{1,0:T(8,128)(2,1)S(1)}, u32[]{:S(2)}, u32[]{:S(2)}) collective-permute-start(bf16[128,512]{1,0:T(8,128)(2,1)S(1)} %fusion.17), channel_id=1, source_target_pairs={{0,2},{1,3},{2,0},{3,1},{4,6},{5,7},{6,4},{7,5},{8,10},{9,11},{10,... | collective-permute-start | bytes 393224 | tf_op jit(solution)/shard_map/ppermute | solution.py:17
  71.5 7.1 %copy-start.36 = (bf16[128,512]{1,0:T(8,128)(2,1)S(1)}, bf16[128,512]{1,0:T(8,128)(2,1)}, u32[]{:S(2)}) copy-start(bf16[128,512]{1,0:T(8,128)(2,1)} %param.6) | copy-start | bytes 393220
  71.5 7.1 %collective-permute-start.26 = (bf16[128,512]{1,0:T(8,128)(2,1)S(1)}, bf16[128,512]{1,0:T(8,128)(2,1)S(1)}, u32[]{:S(2)}, u32[]{:S(2)}) collective-permute-start(bf16[128,512]{1,0:T(8,128)(2,1)S(1)} %fusion.18), channel_id=1, source_target_pairs={{0,1},{1,0},{2,3},{3,2},{4,5},{5,4},{6,7},{7,6},{8,9},{9,8},{10,11... | collective-permute-start | bytes 393224 | tf_op jit(solution)/shard_map/ppermute | solution.py:17
  72.2 25.3 %copy-start.8 = (bf16[1,512,512]{2,1,0:T(8,128)(2,1)}, bf16[1,512,512]{2,1,0:T(8,128)(2,1)S(1)}, u32[]{:S(2)}) copy-start(bf16[1,512,512]{2,1,0:T(8,128)(2,1)S(1)} %turned.6.refs_0_) | copy-start | bytes 1572868
  72.4 25.1 %copy-start.10 = (bf16[1,512,512]{2,1,0:T(8,128)(2,1)}, bf16[1,512,512]{2,1,0:T(8,128)(2,1)S(1)}, u32[]{:S(2)}) copy-start(bf16[1,512,512]{2,1,0:T(8,128)(2,1)S(1)} %turned.7.refs_1_) | copy-start | bytes 1572868
  72.6 6.0 %copy-start.12 = (bf16[1,512,512]{2,1,0:T(8,128)(2,1)}, bf16[1,512,512]{2,1,0:T(8,128)(2,1)S(1)}, u32[]{:S(2)}) copy-start(bf16[1,512,512]{2,1,0:T(8,128)(2,1)S(1)} %turned.8.refs_2_) | copy-start | bytes 1572868
  79.4 7.0 %collective-permute-start.30 = (bf16[128,512]{1,0:T(8,128)(2,1)S(1)}, bf16[128,512]{1,0:T(8,128)(2,1)S(1)}, u32[]{:S(2)}, u32[]{:S(2)}) collective-permute-start(bf16[128,512]{1,0:T(8,128)(2,1)S(1)} %get-tuple-element.133), channel_id=1, source_target_pairs={{0,1},{1,0},{2,3},{3,2},{4,5},{5,4},{6,7},{7,6},{8,9},{9,8},{10,11... | collective-permute-start | bytes 393224 | tf_op jit(solution)/shard_map/ppermute | solution.py:17
  79.4 8.1 %collective-permute-start.27 = (bf16[1,128,512]{2,1,0:T(8,128)(2,1)S(1)}, bf16[1,128,512]{2,1,0:T(8,128)(2,1)}, u32[]{:S(2)}, u32[]{:S(2)}) collective-permute-start(bf16[1,128,512]{2,1,0:T(8,128)(2,1)S(1)} %bitcast.118), channel_id=1, source_target_pairs={{0,16},{4,20},{8,24},{12,28},{16,0},{20,4},{24,8},{28,12},{1,17},{... | collective-permute-start | bytes 393224 | tf_op jit(solution)/shard_map/ppermute | solution.py:37
  80.8 7.7 %collective-permute-start.34 = (bf16[128,512]{1,0:T(8,128)(2,1)S(1)}, bf16[128,512]{1,0:T(8,128)(2,1)S(1)}, u32[]{:S(2)}, u32[]{:S(2)}) collective-permute-start(bf16[128,512]{1,0:T(8,128)(2,1)S(1)} %get-tuple-element.133), channel_id=1, source_target_pairs={{0,3},{1,2},{2,1},{3,0},{4,7},{5,6},{6,5},{7,4},{8,11},{9,10},{10,... | collective-permute-start | bytes 393224 | tf_op jit(solution)/shard_map/ppermute | solution.py:17
  83.4 10.1 %collective-permute-start.33 = (bf16[128,512]{1,0:T(8,128)(2,1)S(1)}, bf16[128,512]{1,0:T(8,128)(2,1)S(1)}, u32[]{:S(2)}, u32[]{:S(2)}) collective-permute-start(bf16[128,512]{1,0:T(8,128)(2,1)S(1)} %get-tuple-element.133), channel_id=1, source_target_pairs={{0,2},{1,3},{2,0},{3,1},{4,6},{5,7},{6,4},{7,5},{8,10},{9,11},{10,... | collective-permute-start | bytes 393224 | tf_op jit(solution)/shard_map/ppermute | solution.py:17
  84.3 9.2 %collective-permute-start.29 = (bf16[1,128,512]{2,1,0:T(8,128)(2,1)S(1)}, bf16[1,128,512]{2,1,0:T(8,128)(2,1)S(1)}, u32[]{:S(2)}, u32[]{:S(2)}) collective-permute-start(bf16[1,128,512]{2,1,0:T(8,128)(2,1)S(1)} %bitcast.119), channel_id=1, source_target_pairs={{0,8},{4,12},{8,0},{12,4},{16,24},{20,28},{24,16},{28,20},{1,9},{5... | collective-permute-start | bytes 393224 | tf_op jit(solution)/shard_map/ppermute | solution.py:23
  86.4 11.1 %copy-start.23 = (bf16[128,512]{1,0:T(8,128)(2,1)}, bf16[128,512]{1,0:T(8,128)(2,1)S(1)}, u32[]{:S(2)}) copy-start(bf16[128,512]{1,0:T(8,128)(2,1)S(1)} %collective-permute-done.30) | copy-start | bytes 393220
  86.4 8.9 %collective-permute-start.31 = (bf16[1,128,512]{2,1,0:T(8,128)(2,1)S(1)}, bf16[1,128,512]{2,1,0:T(8,128)(2,1)}, u32[]{:S(2)}, u32[]{:S(2)}) collective-permute-start(bf16[1,128,512]{2,1,0:T(8,128)(2,1)S(1)} %bitcast.122), channel_id=1, source_target_pairs={{0,16},{4,20},{8,24},{12,28},{16,0},{20,4},{24,8},{28,12},{1,17},{... | collective-permute-start | bytes 393224 | tf_op jit(solution)/shard_map/ppermute | solution.py:37
  87.5 7.8 %collective-permute-start.32 = (bf16[1,128,512]{2,1,0:T(8,128)(2,1)S(1)}, bf16[1,128,512]{2,1,0:T(8,128)(2,1)}, u32[]{:S(2)}, u32[]{:S(2)}) collective-permute-start(bf16[1,128,512]{2,1,0:T(8,128)(2,1)S(1)} %bitcast.123), channel_id=1, source_target_pairs={{0,8},{4,12},{8,0},{12,4},{16,24},{20,28},{24,16},{28,20},{1,9},{5... | collective-permute-start | bytes 393224 | tf_op jit(solution)/shard_map/ppermute | solution.py:23
  88.5 6.6 %collective-permute-start.28 = (bf16[1,128,512]{2,1,0:T(8,128)(2,1)}, bf16[1,128,512]{2,1,0:T(8,128)(2,1)S(1)}, u32[]{:S(2)}, u32[]{:S(2)}) collective-permute-start(bf16[1,128,512]{2,1,0:T(8,128)(2,1)} %collective-permute-done.27.refs_0_), channel_id=1, source_target_pairs={{0,8},{4,12},{8,0},{12,4},{16,24},{20,28},{24,16},{28,20},{1,9},{5... | collective-permute-start | bytes 393224 | tf_op jit(solution)/shard_map/ppermute | solution.py:23
  93.5 4.0 %collective-permute-start.37 = (bf16[2,128,512]{2,1,0:T(8,128)(2,1)S(1)}, bf16[2,128,512]{2,1,0:T(8,128)(2,1)S(1)}, u32[]{:S(2)}, u32[]{:S(2)}) collective-permute-start(bf16[2,128,512]{2,1,0:T(8,128)(2,1)S(1)} %pad_maximum_fusion.2.refs_2_), channel_id=1, source_target_pairs={{0,4},{4,0},{8,12},{12,8},{16,20},{20,16},{24,28},{28,24},{1,5},{5... | collective-permute-start | bytes 786440 | tf_op jit(solution)/shard_map/ppermute | solution.py:23
  93.6 13.1 %collective-permute-start.38 = (bf16[2,128,512]{2,1,0:T(8,128)(2,1)S(1)}, bf16[2,128,512]{2,1,0:T(8,128)(2,1)}, u32[]{:S(2)}, u32[]{:S(2)}) collective-permute-start(bf16[2,128,512]{2,1,0:T(8,128)(2,1)S(1)} %pad_maximum_fusion.2.refs_2_), channel_id=1, source_target_pairs={{0,16},{4,20},{8,24},{12,28},{16,0},{20,4},{24,8},{28,12},{1,17},{... | collective-permute-start | bytes 786440 | tf_op jit(solution)/shard_map/ppermute | solution.py:37
  95.2 1.7 %collective-permute-start.36 = (bf16[1,128,512]{2,1,0:T(8,128)(2,1)S(1)}, bf16[1,128,512]{2,1,0:T(8,128)(2,1)S(1)}, u32[]{:S(2)}, u32[]{:S(2)}) collective-permute-start(bf16[1,128,512]{2,1,0:T(8,128)(2,1)S(1)} %bitcast.124), channel_id=1, source_target_pairs={{0,4},{4,0},{8,12},{12,8},{16,20},{20,16},{24,28},{28,24},{1,5},{5... | collective-permute-start | bytes 393224 | tf_op jit(solution)/shard_map/ppermute | solution.py:23
  95.3 2.9 %collective-permute-start.35 = (bf16[1,128,512]{2,1,0:T(8,128)(2,1)S(1)}, bf16[1,128,512]{2,1,0:T(8,128)(2,1)S(1)}, u32[]{:S(2)}, u32[]{:S(2)}) collective-permute-start(bf16[1,128,512]{2,1,0:T(8,128)(2,1)S(1)} %bitcast.120), channel_id=1, source_target_pairs={{0,4},{4,0},{8,12},{12,8},{16,20},{20,16},{24,28},{28,24},{1,5},{5... | collective-permute-start | bytes 393224 | tf_op jit(solution)/shard_map/ppermute | solution.py:23
  95.7 11.7 %collective-permute-start.42 = (bf16[2,128,512]{2,1,0:T(8,128)(2,1)S(1)}, bf16[2,128,512]{2,1,0:T(8,128)(2,1)}, u32[]{:S(2)}, u32[]{:S(2)}) collective-permute-start(bf16[2,128,512]{2,1,0:T(8,128)(2,1)S(1)} %pad_maximum_fusion.2.refs_2_), channel_id=1, source_target_pairs={{0,8},{4,12},{8,0},{12,4},{16,24},{20,28},{24,16},{28,20},{1,9},{5... | collective-permute-start | bytes 786440 | tf_op jit(solution)/shard_map/ppermute | solution.py:23
  106.7 2.7 %collective-permute-start.41 = (bf16[2,128,512]{2,1,0:T(8,128)(2,1)}, bf16[2,128,512]{2,1,0:T(8,128)(2,1)}, u32[]{:S(2)}, u32[]{:S(2)}) collective-permute-start(bf16[2,128,512]{2,1,0:T(8,128)(2,1)} %collective-permute-done.38.refs_2_), channel_id=1, source_target_pairs={{0,4},{4,0},{8,12},{12,8},{16,20},{20,16},{24,28},{28,24},{1,5},{5... | collective-permute-start | bytes 786440 | tf_op jit(solution)/shard_map/ppermute | solution.py:23
  106.8 1.9 %collective-permute-start.39 = (bf16[1,128,512]{2,1,0:T(8,128)(2,1)}, bf16[1,128,512]{2,1,0:T(8,128)(2,1)S(1)}, u32[]{:S(2)}, u32[]{:S(2)}) collective-permute-start(bf16[1,128,512]{2,1,0:T(8,128)(2,1)} %collective-permute-done.27.refs_0_), channel_id=1, source_target_pairs={{0,4},{4,0},{8,12},{12,8},{16,20},{20,16},{24,28},{28,24},{1,5},{5... | collective-permute-start | bytes 393224 | tf_op jit(solution)/shard_map/ppermute | solution.py:23
  107.3 2.1 %collective-permute-start.40 = (bf16[1,128,512]{2,1,0:T(8,128)(2,1)}, bf16[1,128,512]{2,1,0:T(8,128)(2,1)}, u32[]{:S(2)}, u32[]{:S(2)}) collective-permute-start(bf16[1,128,512]{2,1,0:T(8,128)(2,1)} %collective-permute-done.31.refs_1_), channel_id=1, source_target_pairs={{0,4},{4,0},{8,12},{12,8},{16,20},{20,16},{24,28},{28,24},{1,5},{5... | collective-permute-start | bytes 393224 | tf_op jit(solution)/shard_map/ppermute | solution.py:23
  107.4 8.9 %collective-permute-start.46 = (bf16[2,128,512]{2,1,0:T(8,128)(2,1)}, bf16[2,128,512]{2,1,0:T(8,128)(2,1)S(1)}, u32[]{:S(2)}, u32[]{:S(2)}) collective-permute-start(bf16[2,128,512]{2,1,0:T(8,128)(2,1)} %collective-permute-done.42.refs_2_), channel_id=1, source_target_pairs={{0,16},{4,20},{8,24},{12,28},{16,0},{20,4},{24,8},{28,12},{1,17},{... | collective-permute-start | bytes 786440 | tf_op jit(solution)/shard_map/ppermute | solution.py:37
  110.2 4.5 %copy-start.22 = (bf16[1,128,512]{2,1,0:T(8,128)(2,1)S(1)}, bf16[1,128,512]{2,1,0:T(8,128)(2,1)}, u32[]{:S(2)}) copy-start(bf16[1,128,512]{2,1,0:T(8,128)(2,1)} %copy-done.21) | copy-start | bytes 393220
  114.6 2.3 %collective-permute-start.45 = (bf16[2,128,512]{2,1,0:T(8,128)(2,1)}, bf16[2,128,512]{2,1,0:T(8,128)(2,1)}, u32[]{:S(2)}, u32[]{:S(2)}) collective-permute-start(bf16[2,128,512]{2,1,0:T(8,128)(2,1)} %collective-permute-done.42.refs_2_), channel_id=1, source_target_pairs={{0,4},{4,0},{8,12},{12,8},{16,20},{20,16},{24,28},{28,24},{1,5},{5... | collective-permute-start | bytes 786440 | tf_op jit(solution)/shard_map/ppermute | solution.py:23
  114.7 1.7 %collective-permute-start.43 = (bf16[1,128,512]{2,1,0:T(8,128)(2,1)S(1)}, bf16[1,128,512]{2,1,0:T(8,128)(2,1)}, u32[]{:S(2)}, u32[]{:S(2)}) collective-permute-start(bf16[1,128,512]{2,1,0:T(8,128)(2,1)S(1)} %copy-done.22), channel_id=1, source_target_pairs={{0,4},{4,0},{8,12},{12,8},{16,20},{20,16},{24,28},{28,24},{1,5},{5... | collective-permute-start | bytes 393224 | tf_op jit(solution)/shard_map/ppermute | solution.py:23
  115.1 1.7 %collective-permute-start.44 = (bf16[1,128,512]{2,1,0:T(8,128)(2,1)}, bf16[1,128,512]{2,1,0:T(8,128)(2,1)}, u32[]{:S(2)}, u32[]{:S(2)}) collective-permute-start(bf16[1,128,512]{2,1,0:T(8,128)(2,1)} %collective-permute-done.32.refs_1_), channel_id=1, source_target_pairs={{0,4},{4,0},{8,12},{12,8},{16,20},{20,16},{24,28},{28,24},{1,5},{5... | collective-permute-start | bytes 393224 | tf_op jit(solution)/shard_map/ppermute | solution.py:23
  115.3 7.0 %collective-permute-start.47 = (bf16[1,128,512]{2,1,0:T(8,128)(2,1)}, bf16[1,128,512]{2,1,0:T(8,128)(2,1)S(1)}, u32[]{:S(2)}, u32[]{:S(2)}) collective-permute-start(bf16[1,128,512]{2,1,0:T(8,128)(2,1)} %collective-permute-done.31.refs_1_), channel_id=1, source_target_pairs={{0,8},{4,12},{8,0},{12,4},{16,24},{20,28},{24,16},{28,20},{1,9},{5... | collective-permute-start | bytes 393224 | tf_op jit(solution)/shard_map/ppermute | solution.py:23
  116.9 5.4 %copy-start.20 = (bf16[1,128,512]{2,1,0:T(8,128)(2,1)S(1)}, bf16[1,128,512]{2,1,0:T(8,128)(2,1)}, u32[]{:S(2)}) copy-start(bf16[1,128,512]{2,1,0:T(8,128)(2,1)} %copy-done.19) | copy-start | bytes 393220
  122.1 2.0 %collective-permute-start.50 = (bf16[2,128,512]{2,1,0:T(8,128)(2,1)S(1)}, bf16[2,128,512]{2,1,0:T(8,128)(2,1)S(1)}, u32[]{:S(2)}, u32[]{:S(2)}) collective-permute-start(bf16[2,128,512]{2,1,0:T(8,128)(2,1)S(1)} %collective-permute-done.46.refs_2_), channel_id=1, source_target_pairs={{0,4},{4,0},{8,12},{12,8},{16,20},{20,16},{24,28},{28,24},{1,5},{5... | collective-permute-start | bytes 786440 | tf_op jit(solution)/shard_map/ppermute | solution.py:23
  122.3 1.6 %collective-permute-start.48 = (bf16[1,128,512]{2,1,0:T(8,128)(2,1)S(1)}, bf16[1,128,512]{2,1,0:T(8,128)(2,1)S(1)}, u32[]{:S(2)}, u32[]{:S(2)}) collective-permute-start(bf16[1,128,512]{2,1,0:T(8,128)(2,1)S(1)} %copy-done.20), channel_id=1, source_target_pairs={{0,4},{4,0},{8,12},{12,8},{16,20},{20,16},{24,28},{28,24},{1,5},{5... | collective-permute-start | bytes 393224 | tf_op jit(solution)/shard_map/ppermute | solution.py:23
  122.7 1.4 %collective-permute-start.49 = (bf16[1,128,512]{2,1,0:T(8,128)(2,1)S(1)}, bf16[1,128,512]{2,1,0:T(8,128)(2,1)S(1)}, u32[]{:S(2)}, u32[]{:S(2)}) collective-permute-start(bf16[1,128,512]{2,1,0:T(8,128)(2,1)S(1)} %collective-permute-done.47.refs_1_), channel_id=1, source_target_pairs={{0,4},{4,0},{8,12},{12,8},{16,20},{20,16},{24,28},{28,24},{1,5},{5... | collective-permute-start | bytes 393224 | tf_op jit(solution)/shard_map/ppermute | solution.py:23
  124.1 4.3 %copy-start.13 = (bf16[1,512,512]{2,1,0:T(8,128)(2,1)S(1)}, bf16[1,512,512]{2,1,0:T(8,128)(2,1)}, u32[]{:S(2)}) copy-start(bf16[1,512,512]{2,1,0:T(8,128)(2,1)} %copy-done.12) | copy-start | bytes 1572868
  (24 other events, 44.0 us)
